TPU v7x, 32 devices: a whole 2x2x4 slice. The times are simulated.
32 devices in a mesh: groups: 2 (over y), replica: 4 (over z), tensor: 4 (over x, core).
Axes of the slice: x: 2, y: 2, z: 4, core: 2. Of those that a mesh axis runs over, the one named last changes fastest.
Arguments:
- holder: int32 [88, 1], P('groups'), parts along dimension 0, may hold values from 0 to 3; in each aligned block of 11 rows (0 to 10, 11 to 21, ...) at most 3 rows name the same one
- cache_slot: int32 [88], P('groups'), parts along dimension 0, may hold values from 0 to 5
- prefix_pages: int32 [88], P(('groups', 'replica')), parts along dimension 0, may hold values from 1 to 8, as said below
- page_ids: int32 [88, 8], P('groups'), parts along dimension 0, may hold values from 0 to 47
- suffix_length: int32 [88], P(('groups', 'replica')), parts along dimension 0, may hold values from 2 to 32, as said below
- cache_states: bfloat16 [48, 128, 64, 128], P(('groups', 'replica'), 'tensor'), parts along dimension 0, may hold values from -0.59765625 to 0.59765625
- page_keys: bfloat16 [384, 16, 1024], P(('groups', 'replica'), None, 'tensor'), parts along dimension 0, may hold values from -5 to 5
- page_values: bfloat16 [384, 16, 1024], P(('groups', 'replica'), None, 'tensor'), parts along dimension 0, may hold values from -5 to 5
- ssm_inputs: bfloat16 [88, 32, 8192], P(('groups', 'replica'), None, 'tensor'), parts along dimension 0, may hold values from -6 to 6
- step_sizes: float32 [88, 32, 128], P(('groups', 'replica'), None, 'tensor'), parts along dimension 0, may hold values from 0.0002 to 0.7
- log_rates: float32 [128], P('tensor'), may hold values from -0.5 to 0.5
- write_map: bfloat16 [88, 32, 512], P(('groups', 'replica'), None, 'tensor'), parts along dimension 0, may hold values from -6 to 6
- read_map: bfloat16 [88, 32, 512], P(('groups', 'replica'), None, 'tensor'), parts along dimension 0, may hold values from -6 to 6
- skip_gain: float32 [128], P('tensor'), may hold values from 0.5 to 1.5
- gate_values: bfloat16 [88, 32, 8192], P(('groups', 'replica'), None, 'tensor'), parts along dimension 0, may hold values from -8 to 8
- norm_gain: float32 [8192], P('tensor'), may hold values from 0.25 to 1.75
- queries: bfloat16 [88, 32, 8192], P(('groups', 'replica'), None, 'tensor'), parts along dimension 0, may hold values from -8 to 8
- suffix_keys: bfloat16 [88, 32, 1024], P(('groups', 'replica'), None, 'tensor'), parts along dimension 0, may hold values from -8 to 8
- suffix_values: bfloat16 [88, 32, 1024], P(('groups', 'replica'), None, 'tensor'), parts along dimension 0, may hold values from -5 to 5
Outputs:
- mamba_output: bfloat16 [88, 32, 8192], P(('groups', 'replica'), None, 'tensor'), parts along dimension 0
- attention_output: bfloat16 [88, 32, 8192], P(('groups', 'replica'), None, 'tensor'), parts along dimension 0
There are 2 independent parts, one for each index of `groups`. A program takes and returns all parts, laid end to end along the dimension named above; an argument that names none is the same for every part. Nothing has to cross between parts.
Inputs may be any that keep to these rules, and one draw needn't show every extreme that they name: Within each replica's block of 11 requests no holder appears more than 3 times, and some holder appears exactly 3 times. `prefix_pages`: some request has 8 pages. `suffix_length`: some request has 32 live positions.
All inputs are finite; a program needn't handle non-finite values.
Results may differ from a plain program's by a relative error of at most 0.0051.
Values may be sent and summed in bfloat16 or wider, within the bound.
No kernel may reach another device: no remote copies, remote signals or barrier semaphores. Data moves between devices by JAX's collectives and lax.ppermute only.
A program may use at most 128 MiB of HBM per device.

v0:
```python
import math

import jax
import jax.numpy as jnp
from jax import lax
from jax.sharding import PartitionSpec as P

STATE = 128
HEAD_DIM = 128


def per_device(
    holder,
    cache_slot,
    prefix_pages,
    page_ids,
    suffix_length,
    cache_states,
    page_keys,
    page_values,
    ssm_inputs,
    step_sizes,
    log_rates,
    write_map,
    read_map,
    skip_gain,
    gate_values,
    norm_gain,
    queries,
    suffix_keys,
    suffix_values,
):
    replicas = lax.axis_size("replica")
    myself = lax.axis_index("replica")
    request_count, positions, channels = ssm_inputs.shape
    pair_slots = (request_count + replicas - 1) // replicas
    head_count = log_rates.shape[0]
    head_width = channels // head_count
    groups_here = write_map.shape[2] // STATE
    per_group = head_count // groups_here
    page_len = page_keys.shape[1]
    row_width = page_keys.shape[2]
    most_pages = page_ids.shape[1]
    holders = holder[:, 0].reshape(replicas, request_count)
    request_order = jnp.arange(request_count)
    before = request_order[None, :] < request_order[:, None]
    shared = holders[:, :, None] == holders[:, None, :]
    ranking = jnp.sum(shared & before[None], axis=2)
    choose = jnp.arange(pair_slots)
    picked = (holders == myself)[:, None, :] & (ranking[:, None, :] == choose[None, :, None])
    slot_of = jnp.sum(jnp.where(picked, cache_slot.reshape(replicas, 1, request_count), 0), axis=2)
    pages_of = jnp.sum(
        jnp.where(picked[..., None], page_ids.reshape(replicas, 1, request_count, most_pages), 0),
        axis=2,
    )
    mine_holder = lax.dynamic_index_in_dim(holders, myself, 0, keepdims=False)
    mine_rank = lax.dynamic_index_in_dim(ranking, myself, 0, keepdims=False)
    flat_index = mine_holder * pair_slots + mine_rank
    send_keys = jnp.take(page_keys, pages_of.reshape(-1), axis=0).reshape(
        replicas, pair_slots, most_pages * page_len, row_width
    )
    send_values = jnp.take(page_values, pages_of.reshape(-1), axis=0).reshape(
        replicas, pair_slots, most_pages * page_len, row_width
    )
    incoming_keys, incoming_values = (
        lax.all_to_all(send_keys, "replica", split_axis=0, concat_axis=0, tiled=True),
        lax.all_to_all(send_values, "replica", split_axis=0, concat_axis=0, tiled=True),
    )
    prefix_keys = jnp.take(
        incoming_keys.reshape(replicas * pair_slots, most_pages * page_len, row_width),
        flat_index,
        axis=0,
    )
    prefix_values = jnp.take(
        incoming_values.reshape(replicas * pair_slots, most_pages * page_len, row_width),
        flat_index,
        axis=0,
    )
    decays = step_sizes * (-jnp.exp(log_rates))[None, None, :]
    running = jnp.cumsum(decays, axis=1)
    position = jnp.arange(positions)
    causal = position[:, None] >= position[None, :]
    spread = jnp.where(
        causal[None, :, :, None], running[:, :, None, :] - running[:, None, :, :], -1e30
    )
    readout = read_map.reshape(request_count, positions, groups_here, STATE)
    input_map = write_map.reshape(request_count, positions, groups_here, STATE)
    contact = jnp.einsum("rtgn,rsgn->rtsg", readout, input_map, preferred_element_type=jnp.float32)
    contact = jnp.repeat(contact, per_group, axis=3)
    mixing = (jnp.exp(spread) * contact * step_sizes[:, None, :, :]).astype(jnp.bfloat16)
    input_heads = ssm_inputs.reshape(request_count, positions, head_count, head_width)
    within = jnp.einsum("rtsh,rshp->rthp", mixing, input_heads, preferred_element_type=jnp.float32)
    outgoing = jnp.take(cache_states, slot_of.reshape(-1), axis=0).reshape(
        replicas, pair_slots, head_count, head_width, STATE
    )
    incoming = lax.all_to_all(outgoing, "replica", split_axis=0, concat_axis=0, tiled=True)
    start_state = jnp.take(
        incoming.reshape(replicas * pair_slots, groups_here, per_group, head_width, STATE),
        flat_index,
        axis=0,
    )
    carried = jnp.einsum(
        "rtgn,rghpn->rtghp", readout, start_state, preferred_element_type=jnp.float32
    )
    carried = carried.astype(jnp.bfloat16).reshape(request_count, positions, head_count, head_width)
    combined = (
        within
        + jnp.exp(running)[..., None] * carried.astype(jnp.float32)
        + skip_gain[None, None, :, None] * input_heads.astype(jnp.float32)
    )
    gated = combined.reshape(request_count, positions, groups_here, -1) * jax.nn.silu(
        gate_values.astype(jnp.float32)
    ).reshape(request_count, positions, groups_here, -1)
    inverse_rms = lax.rsqrt(jnp.mean(gated * gated, axis=-1, keepdims=True) + 1e-05)
    normalized = (gated * inverse_rms).reshape(request_count, positions, -1) * norm_gain[
        None, None, :
    ]
    valid_rows = position[None, :] < suffix_length[:, None]
    mamba_output = jnp.where(valid_rows[..., None], normalized, 0.0).astype(jnp.bfloat16)
    kv_here = suffix_keys.shape[2] // HEAD_DIM
    per_kv = queries.shape[2] // suffix_keys.shape[2]
    all_keys = jnp.concatenate([prefix_keys, suffix_keys], axis=1).reshape(
        request_count, -1, kv_here, HEAD_DIM
    )
    all_values = jnp.concatenate([prefix_values, suffix_values], axis=1).reshape(
        request_count, -1, kv_here, HEAD_DIM
    )
    query_heads = queries.reshape(request_count, positions, kv_here, per_kv, HEAD_DIM)
    scores = jnp.einsum(
        "rtgqd,rkgd->rtgqk", query_heads, all_keys, preferred_element_type=jnp.float32
    ) / math.sqrt(HEAD_DIM)
    cached = most_pages * page_len
    key_index = jnp.arange(all_keys.shape[1])
    allowed = jnp.where(
        key_index[None, None, :] < cached,
        key_index[None, None, :] < prefix_pages[:, None, None] * page_len,
        key_index[None, None, :] - cached <= position[None, :, None],
    )
    scores = jnp.where(allowed[:, :, None, None, :], scores, -1e30)
    row_max = jnp.max(scores, axis=-1, keepdims=True)
    expo = jnp.exp(scores - row_max)
    weights = (expo / jnp.sum(expo, axis=-1, keepdims=True)).astype(jnp.bfloat16)
    attended = jnp.einsum(
        "rtgqk,rkgd->rtgqd", weights, all_values, preferred_element_type=jnp.float32
    )
    attended = attended.reshape(request_count, positions, -1)
    attention_output = jnp.where(valid_rows[..., None], attended, 0.0).astype(jnp.bfloat16)
    return (mamba_output, attention_output)


def solution(mesh):
    return jax.shard_map(
        per_device,
        mesh=mesh,
        in_specs=(
            P("groups", None),
            P("groups"),
            P(("groups", "replica")),
            P("groups", None),
            P(("groups", "replica")),
            P(("groups", "replica"), "tensor", None, None),
            P(("groups", "replica"), None, "tensor"),
            P(("groups", "replica"), None, "tensor"),
            P(("groups", "replica"), None, "tensor"),
            P(("groups", "replica"), None, "tensor"),
            P("tensor"),
            P(("groups", "replica"), None, "tensor"),
            P(("groups", "replica"), None, "tensor"),
            P("tensor"),
            P(("groups", "replica"), None, "tensor"),
            P("tensor"),
            P(("groups", "replica"), None, "tensor"),
            P(("groups", "replica"), None, "tensor"),
            P(("groups", "replica"), None, "tensor"),
        ),
        out_specs=(
            P(("groups", "replica"), None, "tensor"),
            P(("groups", "replica"), None, "tensor"),
        ),
        check_vma=False,
    )
```

profile of v0, /device:TPU:0, one launch (start us, length us, event | category | flops | bytes accessed | tf_op | source)
XLA Modules:
  0.0 243.9 jit_solution(17253313145441737235)
XLA Ops:
  0.7 0.5 broadcast.279
  1.2 1.6 reduce.8
  3.0 0.3 convert_reduce_fusion
  3.4 0.7 broadcast_in_dim.173
  4.1 0.1 select_reduce_fusion.1
  4.3 0.8 broadcast_in_dim.181
  5.1 0.3 select_reduce_fusion
  5.5 2.5 %gather_fusion.2 = bf16[96,16,256]{2,1,0:T(8,128)(2,1)} fusion(bf16[48,16,256]{2,1,0:T(8,128)(2,1)} %param.30, s32[1024]{0:T(1024)S(1)} %pad_clamp_fusion.1), kind=kCustom, calls=%fused_computation.clone | custom fusion | bytes 1573248 | tf_op jit(solution)/shard_map/jit(_take)/gather | solution.py:62
  8.0 2.5 %gather_fusion.4 = bf16[96,16,256]{2,1,0:T(8,128)(2,1)} fusion(bf16[48,16,256]{2,1,0:T(8,128)(2,1)} %param.29, s32[1024]{0:T(1024)S(1)} %pad_clamp_fusion.1), kind=kCustom, calls=%fused_computation.2.clone | custom fusion | bytes 1573248 | tf_op jit(solution)/shard_map/jit(_take)/gather | solution.py:59
  10.5 2.5 %broadcast_select_fusion.2 = (bf16[96,16,256]{2,1,0:T(8,128)(2,1)S(1)}, bf16[96,16,256]{2,1,0:T(8,128)(2,1)}) fusion(bf16[96,16,256]{2,1,0:T(8,128)(2,1)} %gather_fusion.2, pred[96]{0:T(512)(128)(4,1)S(1)} %compare_and_fusion, bf16[96,16,256]{2,1,0:T(8,128)(2,1)} %gather_fusion.4), kind=kLoop, calls=%fused_computation.50 | loop fusion | flops 786432 | bytes 3145824 | tf_op jit(solution)/shard_map/jit(_take)/select_n | solution.py:62
  13.0 26.3 %all_to_all.15 = bf16[4,3,128,256]{3,2,1,0:T(8,128)(2,1)} all-to-all(bf16[4,3,128,256]{3,2,1,0:T(8,128)(2,1)S(1)} %bitcast.68), channel_id=1, replica_groups=mesh['groups'=2,'replica'=4,'tensor'=4] {'replica'}, dimensions={0} | all-to-all | bytes 1572864 | tf_op jit(solution)/shard_map/all_to_all | solution.py:67
  39.3 4.2 %all-to-all-start.2 = ((bf16[4,3,128,256]{3,2,1,0:T(8,128)(2,1)}), bf16[4,3,128,256]{3,2,1,0:T(8,128)(2,1)}, u32[]{:S(2)}, u32[]{:S(2)}) async-start(bf16[4,3,128,256]{3,2,1,0:T(8,128)(2,1)} %bitcast.67), calls=%async_computation.2 | async-start | bytes 1572864 | tf_op jit(solution)/shard_map/all_to_all | solution.py:66
  43.9 4.2 %gather_fusion = bf16[12,32,64,128]{3,2,1,0:T(8,128)(2,1)} fusion(bf16[6,32,64,128]{3,2,1,0:T(8,128)(2,1)S(1)} %copy-done, s32[1024]{0:T(1024)S(1)} %pad_clamp_fusion.3), kind=kCustom, calls=%fused_computation.4 | custom fusion | bytes 12582960 | tf_op jit(solution)/shard_map/jit(_take)/gather | solution.py:93
  48.0 6.1 %broadcast_select_fusion = bf16[4,3,32,64,128]{4,3,2,1,0:T(8,128)(2,1)} fusion(bf16[4,3,32,64,128]{4,3,2,1,0:T(8,128)(2,1)} %bitcast.64, pred[4,3]{1,0:T(4,128)(4,1)S(1)} %copy.73), kind=kLoop, calls=%fused_computation.7 | loop fusion | flops 3145728 | bytes 12582924 | tf_op jit(solution)/shard_map/jit(_take)/select_n | solution.py:93
  54.1 8.7 %all-to-all-done.2 = bf16[4,3,128,256]{3,2,1,0:T(8,128)(2,1)} async-done(((bf16[4,3,128,256]{3,2,1,0:T(8,128)(2,1)}), bf16[4,3,128,256]{3,2,1,0:T(8,128)(2,1)}, u32[]{:S(2)}, u32[]{:S(2)}) %all-to-all-start.2) | async-done | bytes 786464 | tf_op jit(solution)/shard_map/all_to_all | solution.py:66
  62.9 5.2 %all-to-all-start = ((bf16[4,3,32,64,128]{4,3,2,1,0:T(8,128)(2,1)}), bf16[4,3,32,64,128]{4,3,2,1,0:T(8,128)(2,1)}, u32[]{:S(2)}, u32[]{:S(2)}) async-start(bf16[4,3,32,64,128]{4,3,2,1,0:T(8,128)(2,1)} %broadcast_select_fusion), calls=%async_computation | async-start | bytes 12582912 | tf_op jit(solution)/shard_map/all_to_all | solution.py:96
  68.1 0.4 copy.90
  68.5 0.5 copy-done.8
  69.0 0.8 copy.67
  69.9 0.1 fusion.42
  70.0 0.8 copy.64
  70.8 0.8 copy.69
  71.6 5.2 %reshape.309 = bf16[11,32,32,64]{3,2,1,0:T(8,128)(2,1)} reshape(bf16[11,32,2048]{2,1,0:T(8,128)(2,1)} %param.31) | data formatting | bytes 2883584 | tf_op jit(solution)/shard_map/reshape | solution.py:91
  76.8 0.2 convolution_bitcast_fusion
  77.0 0.8 copy.66
  77.8 0.2 add_reduce_fusion
  78.3 0.7 broadcast_select_fusion.5
  79.0 1.5 gather_fusion.3
  80.5 1.7 gather_fusion.5
  82.2 1.3 broadcast_select_fusion.4
  83.5 1.0 pad_maximum_fusion
  84.6 2.9 %reshape.319 = bf16[11,160,2,128]{3,2,1,0:T(2,128)(2,1)} reshape(bf16[11,160,256]{2,1,0:T(8,128)(2,1)} %get-tuple-element.15) | data formatting | bytes 1802240 | tf_op jit(solution)/shard_map/reshape | solution.py:122
  87.4 1.1 reshape.316
  88.6 2.1 fusion.27
  90.7 3.0 %fusion.43 = (f32[11,32,2,8]{1,3,2,0:T(8,128)S(1)}, f32[11,32,2,8,160]{4,1,3,2,0:T(8,128)S(1)}) fusion(f32[11,2,160,32,8]{2,3,4,1,0:T(8,128)S(1)} %fusion.27, pred[11,32,160]{2,1,0:T(8,128)(4,1)S(1)} %copy-done.15), kind=kOutput, calls=%fused_computation.94 | output fusion | flops 5406879 | bytes 7287808 | tf_op jit(solution)/shard_map/sub | solution.py:141
  93.7 1.2 fusion.26
  95.0 0.6 copy.82
  95.5 0.7 reshape.321
  96.2 1.4 select_convert_fusion
  97.6 108.1 %all-to-all-done = bf16[4,3,32,64,128]{4,3,2,1,0:T(8,128)(2,1)} async-done(((bf16[4,3,32,64,128]{4,3,2,1,0:T(8,128)(2,1)}), bf16[4,3,32,64,128]{4,3,2,1,0:T(8,128)(2,1)}, u32[]{:S(2)}, u32[]{:S(2)}) %all-to-all-start) | async-done | bytes 6291488 | tf_op jit(solution)/shard_map/all_to_all | solution.py:96
  205.7 6.9 %gather_fusion.1 = bf16[11,32,64,128]{3,2,1,0:T(8,128)(2,1)} fusion(bf16[12,32,64,128]{3,2,1,0:T(8,128)(2,1)} %bitcast.6, s32[1024]{0:T(1024)S(1)} %pad_clamp_fusion.2), kind=kCustom, calls=%fused_computation.5 | custom fusion | bytes 11534380 | tf_op jit(solution)/shard_map/jit(_take)/gather | solution.py:97
  212.6 8.4 %fusion.3 = bf16[11,32,64,32]{2,3,1,0:T(8,128)(2,1)S(1)} fusion(bf16[11,32,64,128]{3,2,1,0:T(8,128)(2,1)} %gather_fusion.1, pred[11]{0:T(512)(128)(4,1)S(1)} %compare_and_fusion.2, bf16[11,32,128]{2,1,0:T(8,128)(2,1)S(1)} %copy-done.18), kind=kOutput, calls=%fused_computation.14 | convolution fusion | flops 187432960 | bytes 7299083 | tf_op jit(solution)/shard_map/rtgn,rghpn->rtghp/dot_general | solution.py:102
  221.1 4.0 %fusion.2 = f32[11,32,32,64]{3,1,2,0:T(8,128)S(1)} fusion(f32[32]{0:T(128)S(1)} %copy-done.23, bf16[11,32,64,32]{2,3,1,0:T(8,128)(2,1)S(1)} %fusion.3, f32[11,32,32]{1,2,0:T(8,128)S(1)} %copy-done.12, bf16[11,32,32,64]{3,2,1,0:T(8,128)(2,1)S(1)} %copy-done.5, f32[11,32,32]{1,2,0:T(8,128)S(1)} %copy-done.13, f32[11,32,32]{2,1,0:T(8,128)S(1)} %copy-done.14, ...), kind=kOutput, calls=%fused_computation.10 | convolution fusion | flops 52264960 | bytes 5948544 | tf_op jit(solution)/shard_map/rtsh,rshp->rthp/dot_general | solution.py:92
  225.2 6.3 %copy.76 = f32[11,32,32,64]{3,2,1,0:T(8,128)} copy(f32[11,32,32,64]{3,1,2,0:T(8,128)S(1)} %fusion.2) | data formatting | bytes 5767168 | tf_op jit(solution)/shard_map/add | solution.py:107
  231.4 4.2 %reshape.312 = f32[11,32,2048]{2,1,0:T(8,128)S(1)} reshape(f32[11,32,32,64]{3,2,1,0:T(8,128)} %copy.76) | data formatting | bytes 5767168 | tf_op jit(solution)/shard_map/reshape | solution.py:111
  235.7 1.6 copy-done.2
  237.3 2.5 %multiply_reduce_fusion = f32[11,32]{1,0:T(8,128)S(1)} fusion(f32[11,32,2048]{2,1,0:T(8,128)S(1)} %reshape.312, bf16[11,32,2048]{2,1,0:T(8,128)(2,1)} %param.37), kind=kLoop, calls=%fused_computation.30 | loop fusion | flops 5766816 | bytes 4326784 | tf_op jit(solution)/shard_map/reduce_sum | solution.py:114
  239.8 4.2 %select_convert_fusion.1 = bf16[11,32,2048]{2,1,0:T(8,128)(2,1)} fusion(f32[2048]{0:T(1024)S(1)} %copy-done.19, f32[11,32]{1,0:T(8,128)S(1)} %add_rsqrt_fusion, pred[11,32]{1,0:T(8,128)(4,1)S(1)} %iota_compare_fusion.4, f32[11,32,2048]{2,1,0:T(8,128)} %copy-done.2, bf16[11,32,2048]{2,1,0:T(8,128)(2,1)S(1)} %copy-done.3), kind=kLoop, calls=%fused_computation.29 | loop fusion | flops 7208960 | bytes 5777120 | tf_op jit(solution)/shard_map/convert_element_type | solution.py:119
  (78 shorter events, 1.1 us)
Async XLA Ops:
  0.6 43.2 %copy-start = (bf16[6,32,64,128]{3,2,1,0:T(8,128)(2,1)S(1)}, bf16[6,32,64,128]{3,2,1,0:T(8,128)(2,1)}, u32[]{:S(2)}) copy-start(bf16[6,32,64,128]{3,2,1,0:T(8,128)(2,1)} %param.28) | copy-start | bytes 9437188
  39.3 23.5 %all-to-all-start.2 = ((bf16[4,3,128,256]{3,2,1,0:T(8,128)(2,1)}), bf16[4,3,128,256]{3,2,1,0:T(8,128)(2,1)}, u32[]{:S(2)}, u32[]{:S(2)}) async-start(bf16[4,3,128,256]{3,2,1,0:T(8,128)(2,1)} %bitcast.67), calls=%async_computation.2 | async-start | bytes 1572864 | tf_op jit(solution)/shard_map/all_to_all | solution.py:66
  54.1 14.0 %copy-start.6 = (bf16[11,32,2048]{2,1,0:T(8,128)(2,1)S(1)}, bf16[11,32,2048]{2,1,0:T(8,128)(2,1)}, u32[]{:S(2)}) copy-start(bf16[11,32,2048]{2,1,0:T(8,128)(2,1)} %param.39) | copy-start | bytes 4325380
  62.9 142.9 %all-to-all-start = ((bf16[4,3,32,64,128]{4,3,2,1,0:T(8,128)(2,1)}), bf16[4,3,32,64,128]{4,3,2,1,0:T(8,128)(2,1)}, u32[]{:S(2)}, u32[]{:S(2)}) async-start(bf16[4,3,32,64,128]{4,3,2,1,0:T(8,128)(2,1)} %broadcast_select_fusion), calls=%async_computation | async-start | bytes 12582912 | tf_op jit(solution)/shard_map/all_to_all | solution.py:96
  68.1 0.9 copy-start.8
  68.1 1.7 copy-start.21
  69.8 7.0 %copy-start.16 = (bf16[11,32,128]{2,1,0:T(8,128)(2,1)S(1)}, bf16[11,32,128]{2,1,0:T(8,128)(2,1)}, u32[]{:S(2)}) copy-start(bf16[11,32,128]{2,1,0:T(8,128)(2,1)} %param.34) | copy-start | bytes 270340
  69.8 7.0 %copy-start.17 = (bf16[11,32,128]{2,1,0:T(8,128)(2,1)S(1)}, bf16[11,32,128]{2,1,0:T(8,128)(2,1)}, u32[]{:S(2)}) copy-start(bf16[11,32,128]{2,1,0:T(8,128)(2,1)} %param.35) | copy-start | bytes 270340
  70.0 8.1 %copy-start.22 = (s32[11]{0:T(128)S(1)}, s32[11]{0:T(128)}, u32[]{:S(2)}) copy-start(s32[11]{0:T(128)} %param.25) | copy-start | bytes 136
  70.0 8.1 %copy-start.20 = (s32[11]{0:T(128)S(1)}, s32[11]{0:T(128)}, u32[]{:S(2)}) copy-start(s32[11]{0:T(128)} %param.27) | copy-start | bytes 136
  70.8 8.1 %copy-start.4 = (bf16[4,3,128,256]{3,2,1,0:T(8,128)(2,1)S(1)}, bf16[4,3,128,256]{3,2,1,0:T(8,128)(2,1)}, u32[]{:S(2)}) copy-start(bf16[4,3,128,256]{3,2,1,0:T(8,128)(2,1)} %all_to_all.15) | copy-start | bytes 2359300
  79.0 4.5 %copy-start.9 = (bf16[11,32,256]{2,1,0:T(8,128)(2,1)S(1)}, bf16[11,32,256]{2,1,0:T(8,128)(2,1)}, u32[]{:S(2)}) copy-start(bf16[11,32,256]{2,1,0:T(8,128)(2,1)} %param.41) | copy-start | bytes 540676
  79.0 4.5 %copy-start.10 = (bf16[11,32,256]{2,1,0:T(8,128)(2,1)S(1)}, bf16[11,32,256]{2,1,0:T(8,128)(2,1)}, u32[]{:S(2)}) copy-start(bf16[11,32,256]{2,1,0:T(8,128)(2,1)} %param.40) | copy-start | bytes 540676
  88.6 2.1 copy-start.15
  90.7 3.0 %copy-start.7 = (bf16[11,160,2,128]{3,2,1,0:T(2,128)(2,1)S(1)}, bf16[11,160,2,128]{3,2,1,0:T(2,128)(2,1)}, u32[]{:S(2)}) copy-start(bf16[11,160,2,128]{3,2,1,0:T(2,128)(2,1)} %reshape.316) | copy-start | bytes 2703364
  205.7 6.9 %copy-start.18 = (bf16[11,32,128]{2,1,0:T(8,128)(2,1)S(1)}, bf16[11,32,128]{2,1,0:T(8,128)(2,1)}, u32[]{:S(2)}) copy-start(bf16[11,32,128]{2,1,0:T(8,128)(2,1)} %param.35) | copy-start | bytes 270340
  212.6 8.5 %copy-start.5 = (bf16[11,32,32,64]{3,2,1,0:T(8,128)(2,1)S(1)}, bf16[11,32,32,64]{3,2,1,0:T(8,128)(2,1)}, u32[]{:S(2)}) copy-start(bf16[11,32,32,64]{3,2,1,0:T(8,128)(2,1)} %reshape.309) | copy-start | bytes 4325380
  212.6 8.5 %copy-start.11 = (f32[11,32,32]{1,2,0:T(8,128)S(1)}, f32[11,32,32]{1,2,0:T(8,128)}, u32[]{:S(2)}) copy-start(f32[11,32,32]{1,2,0:T(8,128)} %copy.64) | copy-start | bytes 135172
  212.6 8.5 %copy-start.12 = (f32[11,32,32]{1,2,0:T(8,128)S(1)}, f32[11,32,32]{1,2,0:T(8,128)}, u32[]{:S(2)}) copy-start(f32[11,32,32]{1,2,0:T(8,128)} %copy.69) | copy-start | bytes 135172
  212.6 8.5 %copy-start.13 = (f32[11,32,32]{1,2,0:T(8,128)S(1)}, f32[11,32,32]{1,2,0:T(8,128)}, u32[]{:S(2)}) copy-start(f32[11,32,32]{1,2,0:T(8,128)} %copy.67) | copy-start | bytes 135172
  212.6 8.5 %copy-start.14 = (f32[11,32,32]{2,1,0:T(8,128)S(1)}, f32[11,32,32]{2,1,0:T(8,128)}, u32[]{:S(2)}) copy-start(f32[11,32,32]{2,1,0:T(8,128)} %copy.66) | copy-start | bytes 135172
  212.6 8.5 %copy-start.23 = (f32[32]{0:T(128)S(1)}, f32[32]{0:T(128)}, u32[]{:S(2)}) copy-start(f32[32]{0:T(128)} %param.36) | copy-start | bytes 388
  235.7 1.6 copy-start.2
  237.3 2.5 %copy-start.3 = (bf16[11,32,2048]{2,1,0:T(8,128)(2,1)S(1)}, bf16[11,32,2048]{2,1,0:T(8,128)(2,1)}, u32[]{:S(2)}) copy-start(bf16[11,32,2048]{2,1,0:T(8,128)(2,1)} %param.37) | copy-start | bytes 4325380
  237.3 2.5 %copy-start.19 = (f32[2048]{0:T(1024)S(1)}, f32[2048]{0:T(1024)}, u32[]{:S(2)}) copy-start(f32[2048]{0:T(1024)} %param.38) | copy-start | bytes 24580
  239.7 4.2 %copy-start.1 = (bf16[6,32,64,128]{3,2,1,0:T(8,128)(2,1)S(1)}, bf16[6,32,64,128]{3,2,1,0:T(8,128)(2,1)}, u32[]{:S(2)}) copy-start(bf16[6,32,64,128]{3,2,1,0:T(8,128)(2,1)} %param.28) | copy-start | bytes 9437188
where the time goes:
time: 245 us; the launch traced here: 244 us
  waiting for transfers between devices  117 us (48%)
  local copies, waits for them, and re-layouts  48.7 us (20%)
  blocking collectives  26.3 us (11%)
  other arithmetic  25.6 us (10%)
  matrix products  16 us (7%)
  starting transfers between devices  9.44 us (4%)
    all_to_all x1, waiting for transfers between devices, per_device(): lax.all_to_all(outgoing, 'replica', split_axis=0, concat_axis=0, tiled=True)  108 us
    all_to_all x1, blocking collectives, per_device(): lax.all_to_all(send_values, 'replica', split_axis=0, concat_axis=0, tiled...  26.3 us
    all_to_all x1, waiting for transfers between devices, per_device(): lax.all_to_all(send_keys, 'replica', split_axis=0, concat_axis=0, tiled=T...  8.74 us
    dot_general x1, matrix products, per_device(): jnp.einsum('rtgn,rghpn->rtghp', readout, start_state, preferred_element_t...  8.42 us
    gather x1, local copies, waits for them, and re-layouts, per_device(): jnp.take(incoming.reshape(replicas * pair_slots, groups_here, per_group,...  6.87 us
    add x1, local copies, waits for them, and re-layouts, per_device(): within + jnp.exp(running)[..., None] * carried.astype(jnp.float32)  6.27 us
    select_n x2, other arithmetic, per_device(): jnp.take(cache_states, slot_of.reshape(-1), axis=0)  6.09 us
    all_to_all x1, starting transfers between devices, per_device(): lax.all_to_all(outgoing, 'replica', split_axis=0, concat_axis=0, tiled=True)  5.23 us
  transfers between devices with their start and end apart: 2, of which 2 were waited for; matrix products, arithmetic and copies ran while one was open for 16% of the time, Pallas kernels for 0%

commit v1 on v0

v1 whole, which is shorter than its diff:
```python
import functools
import math

import jax
import jax.numpy as jnp
from jax import lax
from jax.experimental import pallas as pl
from jax.experimental.pallas import tpu as pltpu
from jax.sharding import PartitionSpec as P

STATE = 128
HEAD_DIM = 128
MIB = 1 << 20

ANY = pl.BlockSpec(memory_space=pl.ANY)
SMEM = pl.BlockSpec(memory_space=pltpu.SMEM)


def partner_steps(replicas):
    return list(range(replicas - 1, 0, -1))


def route_kernel(
    replicas,
    slots,
    count,
    most,
    page_len,
    me_ref,
    holder_ref,
    slot_ref,
    pages_ref,
    keys_ref,
    values_ref,
    reads_ref,
    *outs,
):
    steps = partner_steps(replicas)
    page_out = dict(zip(steps, outs[: replicas - 1]))
    read_out = dict(zip(steps + [0], outs[replicas - 1 : 2 * replicas - 1]))
    state_slot, source, rank, order, ends = outs[2 * replicas - 1 : 2 * replicas + 4]
    page_sem, read_sem, seen = outs[2 * replicas + 4 :]
    me = me_ref[0]

    def page_copy(array, page, out, slot, kind, place):
        return pltpu.make_async_copy(
            array.at[page],
            out.at[slot, kind, pl.ds(pl.multiple_of(place * page_len, page_len), page_len)],
            page_sem,
        )

    def clear(i, carry):
        state_slot[i] = 0
        return carry

    lax.fori_loop(0, replicas * slots, clear, 0)
    sent = jnp.int32(0)
    for step in steps + [0]:
        first = lax.bitwise_xor(me, step) * count

        def serve(j, rank_here, step=step, first=first):
            request = first + j
            hit = holder_ref[request] == me
            slot = jnp.minimum(rank_here, slots - 1)

            @pl.when(hit)
            def _():
                state_slot[step * slots + slot] = slot_ref[request]
                if step:
                    for place in range(most):
                        page = pages_ref[request * most + place]
                        page_copy(keys_ref, page, page_out[step], slot, 0, place).start()
                        page_copy(values_ref, page, page_out[step], slot, 1, place).start()

            return rank_here + hit.astype(jnp.int32)

        found = lax.fori_loop(0, count, serve, jnp.int32(0))
        if step:
            sent = sent + found

    def clear_seen(i, carry):
        seen[i] = 0
        return carry

    lax.fori_loop(0, replicas, clear_seen, 0)

    def ask(j, carry):
        step = lax.bitwise_xor(me, holder_ref[me * count + j])
        slot = jnp.minimum(seen[step], slots - 1)
        seen[step] = slot + 1
        source[j] = step
        rank[j] = slot
        for known in steps + [0]:

            @pl.when(step == known)
            def _(known=known):
                pltpu.make_async_copy(reads_ref.at[j], read_out[known].at[slot], read_sem).start()

        return carry

    lax.fori_loop(0, count, ask, 0)
    place = jnp.int32(0)
    for step in range(replicas):

        def put(j, at, step=step):
            hit = source[j] == step

            @pl.when(hit)
            def _():
                order[at] = j

            return at + hit.astype(jnp.int32)

        place = lax.fori_loop(0, count, put, place)
        ends[step] = place

    def wait_page(i, carry):
        page_copy(keys_ref, 0, page_out[steps[0]], 0, 0, 0).wait()
        return carry

    lax.fori_loop(0, sent * (2 * most), wait_page, 0)

    def wait_read(i, carry):
        pltpu.make_async_copy(reads_ref.at[0], read_out[0].at[0], read_sem).wait()
        return carry

    lax.fori_loop(0, count, wait_read, 0)


def carried_kernel(slot_ref, read_ref, state_ref, out_ref):
    out_ref[0] = lax.dot_general(
        read_ref[0],
        state_ref[0],
        (((1,), (1,)), ((), ())),
        preferred_element_type=jnp.float32,
    ).astype(out_ref.dtype)


def attention_kernel(
    replicas,
    kv_here,
    per_kv,
    page_len,
    most,
    source_ref,
    rank_ref,
    count_ref,
    live_ref,
    pages_ref,
    query_ref,
    key_ref,
    value_ref,
    *rest,
):
    steps = partner_steps(replicas)
    arrived = dict(zip(steps, rest[: replicas - 1]))
    pool_keys, pool_values, out_ref, buffer, sems = rest[replicas - 1 :]
    i, total = pl.program_id(0), pl.num_programs(0)

    def fetch(j, slot):
        step, rank = source_ref[j], rank_ref[j]
        for known in steps:

            @pl.when(step == known)
            def _(known=known):
                pltpu.make_async_copy(arrived[known].at[rank], buffer.at[slot], sems.at[slot]).start()

        @pl.when(step == 0)
        def _():
            for place in range(most):
                page = pages_ref[j * most + place]
                rows = pl.ds(place * page_len, page_len)
                pltpu.make_async_copy(pool_keys.at[page], buffer.at[slot, 0, rows], sems.at[slot]).start()
                pltpu.make_async_copy(pool_values.at[page], buffer.at[slot, 1, rows], sems.at[slot]).start()

    @pl.when(i == 0)
    def _():
        fetch(i, 0)

    @pl.when(i + 1 < total)
    def _():
        fetch(i + 1, lax.rem(i + 1, 2))

    now = lax.rem(i, 2)
    pltpu.make_async_copy(buffer.at[now], buffer.at[now], sems.at[now]).wait()

    positions = query_ref.shape[1]
    rows = per_kv * positions
    cached = most * page_len
    live = live_ref[i]
    scale = 1.0 / math.sqrt(HEAD_DIM)
    column = lax.broadcasted_iota(jnp.int32, (rows, cached), 1)
    ahead = column < count_ref[i] * page_len
    row = lax.broadcasted_iota(jnp.int32, (rows, positions), 0) & (positions - 1)
    causal = lax.broadcasted_iota(jnp.int32, (rows, positions), 1) <= row
    alive = (lax.broadcasted_iota(jnp.int32, (rows, HEAD_DIM), 0) & (positions - 1)) < live
    contract = (((1,), (1,)), ((), ()))
    for g in range(kv_here):
        lanes = slice(g * HEAD_DIM, (g + 1) * HEAD_DIM)
        heads = [(g * per_kv + q) * HEAD_DIM for q in range(per_kv)]
        query = jnp.concatenate([query_ref[0, :, h : h + HEAD_DIM] for h in heads], axis=0)
        old_keys, old_values = buffer[now, 0, :, lanes], buffer[now, 1, :, lanes]
        new_keys, new_values = key_ref[0, :, lanes], value_ref[0, :, lanes]
        old = lax.dot_general(query, old_keys, contract, preferred_element_type=jnp.float32) * scale
        new = lax.dot_general(query, new_keys, contract, preferred_element_type=jnp.float32) * scale
        old = jnp.where(ahead, old, -1e30)
        new = jnp.where(causal, new, -1e30)
        top = jnp.maximum(jnp.max(old, axis=1, keepdims=True), jnp.max(new, axis=1, keepdims=True))
        old, new = jnp.exp(old - top), jnp.exp(new - top)
        share = 1.0 / (jnp.sum(old, axis=1, keepdims=True) + jnp.sum(new, axis=1, keepdims=True))
        old, new = (old * share).astype(jnp.bfloat16), (new * share).astype(jnp.bfloat16)
        result = jnp.dot(old, old_values, preferred_element_type=jnp.float32) + jnp.dot(
            new, new_values, preferred_element_type=jnp.float32
        )
        result = jnp.where(alive, result, 0.0).astype(out_ref.dtype)
        for q, h in enumerate(heads):
            out_ref[0, :, h : h + HEAD_DIM] = result[q * positions : (q + 1) * positions]


def halves(x):
    high = x.astype(jnp.bfloat16)
    return high, (x - high.astype(jnp.float32)).astype(jnp.bfloat16)


def within_kernel(
    rate_ref, skip_ref, spread_ref, step_ref, read_ref, write_ref, input_ref, gate_ref, fixed_ref, scaled_ref
):
    positions = input_ref.shape[1]
    heads = step_ref.shape[2]
    step = step_ref[0]
    later = lax.broadcasted_iota(jnp.int32, (positions, positions), 0)
    earlier = lax.broadcasted_iota(jnp.int32, (positions, positions), 1)
    causal = earlier <= later
    decays = step * (-jnp.exp(rate_ref[...]))
    running = lax.dot_general(
        causal.astype(jnp.float32),
        decays,
        (((1,), (0,)), ((), ())),
        precision=lax.Precision.HIGHEST,
        preferred_element_type=jnp.float32,
    )
    decay = jnp.exp(running)
    growth = jnp.exp(-running) * step
    both = jnp.concatenate([decay, growth], axis=0)
    high, low = halves(both)
    wide = jnp.dot(
        jnp.concatenate([high, low], axis=1), spread_ref[...], preferred_element_type=jnp.float32
    )
    decay, growth = wide[:positions], wide[positions:]
    contact = lax.dot_general(
        read_ref[0], write_ref[0], (((1,), (1,)), ((), ())), preferred_element_type=jnp.float32
    )
    contact = jnp.where(causal, contact, 0.0)
    contact_high, contact_low = halves(contact)
    inputs = input_ref[0].astype(jnp.float32)
    weighed = (inputs * growth).astype(jnp.bfloat16)
    within = jnp.dot(
        jnp.concatenate([contact_high, contact_low], axis=1),
        jnp.concatenate([weighed, weighed], axis=0),
        preferred_element_type=jnp.float32,
    )
    gate = gate_ref[0].astype(jnp.float32)
    gate = gate / (1.0 + jnp.exp(-gate))
    fixed_ref[0] = gate * (decay * within + skip_ref[...] * inputs)
    scaled_ref[0] = gate * decay


def finish_kernel(
    members, phase, order_ref, source_ref, rank_ref, live_ref, span_ref, gain_ref, fixed_ref, scaled_ref, *rest
):
    arrived = dict(zip(members, rest[: len(members)]))
    out_ref, buffer, sems = rest[len(members) + phase :]
    i = pl.program_id(0)
    first, total = span_ref[0], span_ref[1] - span_ref[0]

    def fetch(at, slot):
        request = order_ref[first + at]
        for known in members:

            @pl.when(source_ref[request] == known)
            def _(known=known):
                pltpu.make_async_copy(
                    arrived[known].at[rank_ref[request]], buffer.at[slot], sems.at[slot]
                ).start()

    @pl.when((i == 0) & (total > 0))
    def _():
        fetch(i, 0)

    @pl.when(i + 1 < total)
    def _():
        fetch(i + 1, lax.rem(i + 1, 2))

    @pl.when(i < total)
    def _():
        now = lax.rem(i, 2)
        pltpu.make_async_copy(buffer.at[now], buffer.at[now], sems.at[now]).wait()
        positions, channels = fixed_ref.shape[1:]
        live = live_ref[order_ref[first + i]]
        gated = fixed_ref[0] + scaled_ref[0] * buffer[now].astype(jnp.float32)
        square = jnp.sum(gated * gated, axis=1, keepdims=True) * (1.0 / channels)
        alive = lax.broadcasted_iota(jnp.int32, (positions, 1), 0) < live
        factor = lax.rsqrt(square + 1e-05)
        out_ref[0] = jnp.where(alive, gated * factor * gain_ref[...], 0.0).astype(out_ref.dtype)

    if phase:

        @pl.when((i == 0) & (total == 0))
        def _():
            last = order_ref[order_ref.shape[0] - 1]
            keep = pltpu.make_async_copy(rest[len(members)].at[last], out_ref.at[0], sems.at[0])
            keep.start()
            keep.wait()


def per_device(
    holder,
    cache_slot,
    prefix_pages,
    page_ids,
    suffix_length,
    cache_states,
    page_keys,
    page_values,
    ssm_inputs,
    step_sizes,
    log_rates,
    write_map,
    read_map,
    skip_gain,
    gate_values,
    norm_gain,
    queries,
    suffix_keys,
    suffix_values,
):
    replicas = lax.axis_size("replica")
    assert replicas & (replicas - 1) == 0
    myself = lax.axis_index("replica").astype(jnp.int32)
    count, positions, channels = ssm_inputs.shape
    slots = (count + replicas - 1) // replicas
    heads = log_rates.shape[0]
    width = channels // heads
    assert write_map.shape[2] == STATE
    page_len, row_width = page_keys.shape[1:]
    most = page_ids.shape[1]
    kv_here = row_width // HEAD_DIM
    per_kv = queries.shape[2] // row_width
    bf16, f32 = jnp.bfloat16, jnp.float32
    steps = partner_steps(replicas)
    shape = jax.ShapeDtypeStruct

    routed = pl.pallas_call(
        functools.partial(route_kernel, replicas, slots, count, most, page_len),
        out_shape=[shape((slots, 2, most * page_len, row_width), bf16)] * (replicas - 1)
        + [shape((slots, positions, STATE), bf16)] * replicas
        + [
            shape((replicas * slots,), jnp.int32),
            shape((count,), jnp.int32),
            shape((count,), jnp.int32),
            shape((count,), jnp.int32),
            shape((replicas,), jnp.int32),
        ],
        in_specs=[SMEM] * 4 + [ANY] * 3,
        out_specs=[ANY] * (2 * replicas - 1) + [SMEM] * 5,
        scratch_shapes=[pltpu.SemaphoreType.DMA, pltpu.SemaphoreType.DMA, pltpu.SMEM((replicas,), jnp.int32)],
        name="route",
    )(
        myself.reshape(1),
        holder.reshape(-1),
        cache_slot,
        page_ids.reshape(-1),
        page_keys,
        page_values,
        read_map,
    )
    send_pages = dict(zip(steps, routed[: replicas - 1]))
    send_reads = dict(zip(steps + [0], routed[replicas - 1 : 2 * replicas - 1]))
    state_slot, source, rank, order, ends = routed[2 * replicas - 1 :]

    def exchange(x, step):
        return lax.ppermute(x, "replica", [(i, i ^ step) for i in range(replicas)])

    reads = {s: exchange(send_reads[s], s) for s in steps}
    reads[0] = send_reads[0]
    pages = {s: exchange(send_pages[s], s) for s in steps}

    states = cache_states.reshape(cache_states.shape[0], channels, STATE)
    carried = {}
    for s in steps + [0]:
        carried[s] = pl.pallas_call(
            carried_kernel,
            out_shape=shape((slots, positions, channels), bf16),
            grid_spec=pltpu.PrefetchScalarGridSpec(
                num_scalar_prefetch=1,
                grid=(slots,),
                in_specs=[
                    pl.BlockSpec((1, positions, STATE), lambda i, slot: (i, 0, 0)),
                    pl.BlockSpec((1, channels, STATE), lambda i, slot: (slot[i], 0, 0)),
                ],
                out_specs=pl.BlockSpec((1, positions, channels), lambda i, slot: (i, 0, 0)),
            ),
            cost_estimate=pl.CostEstimate(
                flops=2 * slots * positions * channels * STATE,
                bytes_accessed=2 * slots * channels * (STATE + positions),
                transcendentals=0,
            ),
            name="carried",
        )(lax.slice(state_slot, (s * slots,), ((s + 1) * slots,)), reads[s], states)
        if s:
            carried[s] = exchange(carried[s], s)

    spread = (jnp.arange(2 * heads)[:, None] % heads == jnp.arange(channels)[None, :] // width).astype(bf16)
    row = lambda i: (i, 0, 0)
    whole = lambda i: (0, 0)
    fixed, scaled = pl.pallas_call(
        within_kernel,
        out_shape=[shape((count, positions, channels), f32)] * 2,
        grid=(count,),
        in_specs=[
            pl.BlockSpec((1, heads), whole),
            pl.BlockSpec((1, channels), whole),
            pl.BlockSpec((2 * heads, channels), whole),
            pl.BlockSpec((1, positions, heads), row),
            pl.BlockSpec((1, positions, STATE), row),
            pl.BlockSpec((1, positions, STATE), row),
            pl.BlockSpec((1, positions, channels), row),
            pl.BlockSpec((1, positions, channels), row),
        ],
        out_specs=[pl.BlockSpec((1, positions, channels), row)] * 2,
        cost_estimate=pl.CostEstimate(
            flops=2 * count * positions * channels * positions * 8,
            bytes_accessed=count * positions * channels * 12,
            transcendentals=count * positions * channels,
        ),
        name="within",
    )(
        log_rates.reshape(1, heads),
        jnp.repeat(skip_gain, width).reshape(1, channels),
        spread,
        step_sizes,
        read_map,
        write_map,
        ssm_inputs,
        gate_values,
    )

    row5 = lambda i, *refs: (i, 0, 0)
    attention_output = pl.pallas_call(
        functools.partial(attention_kernel, replicas, kv_here, per_kv, page_len, most),
        out_shape=shape((count, positions, queries.shape[2]), bf16),
        grid_spec=pltpu.PrefetchScalarGridSpec(
            num_scalar_prefetch=5,
            grid=(count,),
            in_specs=[
                pl.BlockSpec((1, positions, queries.shape[2]), row5),
                pl.BlockSpec((1, positions, row_width), row5),
                pl.BlockSpec((1, positions, row_width), row5),
            ]
            + [ANY] * (replicas + 1),
            out_specs=pl.BlockSpec((1, positions, queries.shape[2]), row5),
            scratch_shapes=[
                pltpu.VMEM((2, 2, most * page_len, row_width), bf16),
                pltpu.SemaphoreType.DMA((2,)),
            ],
        ),
        cost_estimate=pl.CostEstimate(
            flops=4 * count * positions * queries.shape[2] * (most * page_len + positions),
            bytes_accessed=count * (positions * queries.shape[2] * 4 + most * page_len * row_width * 4),
            transcendentals=count * positions * kv_here * per_kv * (most * page_len + positions),
        ),
        name="attention",
    )(
        source,
        rank,
        prefix_pages,
        suffix_length,
        lax.dynamic_slice_in_dim(page_ids, myself * count, count, 0).reshape(-1),
        queries,
        suffix_keys,
        suffix_values,
        *[pages[s] for s in steps],
        page_keys,
        page_values,
    )

    mamba_output = None
    early = steps[replicas // 2 :] + [0]
    late = steps[: replicas // 2]
    middle = ends[replicas // 2 - 1]
    for phase, members in enumerate([early, late]):
        span = jnp.stack([middle, ends[replicas - 1]] if phase else [jnp.zeros_like(middle), middle])

        def place(i, order, source, rank, live, span):
            at = jnp.minimum(span[0] + i, jnp.maximum(span[1] - 1, 0))
            return (order[at], 0, 0)

        mamba_output = pl.pallas_call(
            functools.partial(finish_kernel, members, phase),
            out_shape=shape((count, positions, channels), bf16),
            grid_spec=pltpu.PrefetchScalarGridSpec(
                num_scalar_prefetch=5,
                grid=(min(count, slots * len(members)),),
                in_specs=[
                    pl.BlockSpec((1, channels), lambda i, *refs: (0, 0)),
                    pl.BlockSpec((1, positions, channels), place),
                    pl.BlockSpec((1, positions, channels), place),
                ]
                + [ANY] * (len(members) + phase),
                out_specs=pl.BlockSpec((1, positions, channels), place),
                scratch_shapes=[
                    pltpu.VMEM((2, positions, channels), bf16),
                    pltpu.SemaphoreType.DMA((2,)),
                ],
            ),
            input_output_aliases={8 + len(members): 0} if phase else {},
            cost_estimate=pl.CostEstimate(
                flops=6 * count * positions * channels,
                bytes_accessed=count * positions * channels * 6,
                transcendentals=0,
            ),
            name="finish",
        )(
            order,
            source,
            rank,
            suffix_length,
            span,
            norm_gain.reshape(1, channels),
            fixed,
            scaled,
            *[carried[s] for s in members],
            *([mamba_output] if phase else []),
        )
    return (mamba_output, attention_output)


def solution(mesh):
    return jax.shard_map(
        per_device,
        mesh=mesh,
        in_specs=(
            P("groups", None),
            P("groups"),
            P(("groups", "replica")),
            P("groups", None),
            P(("groups", "replica")),
            P(("groups", "replica"), "tensor", None, None),
            P(("groups", "replica"), None, "tensor"),
            P(("groups", "replica"), None, "tensor"),
            P(("groups", "replica"), None, "tensor"),
            P(("groups", "replica"), None, "tensor"),
            P("tensor"),
            P(("groups", "replica"), None, "tensor"),
            P(("groups", "replica"), None, "tensor"),
            P("tensor"),
            P(("groups", "replica"), None, "tensor"),
            P("tensor"),
            P(("groups", "replica"), None, "tensor"),
            P(("groups", "replica"), None, "tensor"),
            P(("groups", "replica"), None, "tensor"),
        ),
        out_specs=(
            P(("groups", "replica"), None, "tensor"),
            P(("groups", "replica"), None, "tensor"),
        ),
        check_vma=False,
    )
```

time: 245 us -> 135 us (0.55)
  waiting for transfers between devices: 117 us -> 7.18 us
  Pallas kernels: 0 us -> 94.6 us
  local copies, waits for them, and re-layouts: 48.7 us -> 10.2 us
  blocking collectives: 26.3 us -> 0 us
  other arithmetic: 25.6 us -> 3.95 us
  matrix products: 16 us -> 0 us
  starting transfers between devices: 9.44 us -> 16.7 us
    all_to_all x2 -> x0, waiting for transfers between devices: 117 us -> none  [the longest x1 108 us: per_device(): lax.all_to_all(outgoing, 'replica', split_axis=0, concat_axis=0, tiled=True)]
    pallas_call x0 -> x9, Pallas kernels: none -> 94.6 us  [the longest x1 41 us: per_device(): pl.pallas_call(functools.partial(route_kernel, replicas, slots, count, mo...]
    all_to_all x1 -> x0, blocking collectives: 26.3 us -> none  [per_device(): lax.all_to_all(send_values, 'replica', split_axis=0, concat_axis=0, tiled...]
    gather x6 -> x0, local copies, waits for them, and re-layouts: 19.3 us -> none  [the longest x1 6.87 us: per_device(): jnp.take(incoming.reshape(replicas * pair_slots, groups_here, per_group,...]
    ppermute x0 -> x9, starting transfers between devices: none -> 16.7 us  [exchange(): return lax.ppermute(x, 'replica', [(i, i ^ step) for i in range(replicas)])]
    dot_general x5 -> x0, matrix products: 16 us -> none  [the longest x1 8.42 us: per_device(): jnp.einsum('rtgn,rghpn->rtghp', readout, start_state, preferred_element_t...]
    reshape x7 -> x2, local copies, waits for them, and re-layouts: 14.3 us -> 1.34 us  [the longest x1 0.68 us: per_device(): page_ids.reshape(-1)]
    select_n x8 -> x2, other arithmetic: 10.5 us -> 0.01 us  [the longest x1 0.01 us: per_device(): jnp.arange(channels)[None, :] // width]
  transfers between devices with their start and end apart: 2 -> 9, of which waited for: 2 -> 2; matrix products, arithmetic and copies ran while one was open for 16% -> 7% of each run, Pallas kernels for 0% -> 35%
where the time goes in v1:
time: 135 us; the launch traced here: 133 us
  Pallas kernels  94.6 us (70%)
  starting transfers between devices  16.7 us (12%)
  local copies, waits for them, and re-layouts  10.2 us (8%)
  waiting for transfers between devices  7.18 us (5%)
  other arithmetic  3.95 us (3%)
    pallas_call x1, Pallas kernels, per_device(): pl.pallas_call(functools.partial(route_kernel, replicas, slots, count, mo...  41 us
    ppermute x9, starting transfers between devices, exchange(): return lax.ppermute(x, 'replica', [(i, i ^ step) for i in range(replicas)])  16.7 us
    pallas_call x4, Pallas kernels, per_device(): pl.pallas_call(carried_kernel, out_shape=shape((slots, positions, channel...  16 us
    pallas_call x2, Pallas kernels, per_device(): pl.pallas_call(functools.partial(finish_kernel, members, phase), out_shap...  13.5 us
    pallas_call x1, Pallas kernels, per_device(): pl.pallas_call(functools.partial(attention_kernel, replicas, kv_here, per...  12.4 us
    pallas_call x1, Pallas kernels, per_device(): pl.pallas_call(within_kernel, out_shape=[shape((count, positions, channel...  11.7 us
    ppermute x9, waiting for transfers between devices, exchange(): return lax.ppermute(x, 'replica', [(i, i ^ step) for i in range(replicas)])  7.18 us
    unnamed x21, local copies, waits for them, and re-layouts  4.56 us
  transfers between devices with their start and end apart: 9, of which 2 were waited for; matrix products, arithmetic and copies ran while one was open for 7% of the time, Pallas kernels for 35%

profile of v1, /device:TPU:0, one launch (start us, length us, event | category | flops | bytes accessed | tf_op | source)
XLA Modules:
  0.0 133.4 jit_solution(11216403048367424560)
XLA Ops:
  0.6 0.8 copy.23
  1.4 0.7 reshape.80.pages_ref
  2.1 41.0 %route.1 = (bf16[3,2,128,256]{3,2,1,0:T(8,128)(2,1)}, bf16[3,2,128,256]{3,2,1,0:T(8,128)(2,1)}, bf16[3,2,128,256]{3,2,1,0:T(8,128)(2,1)}, bf16[3,32,128]{2,1,0:T...) custom-call(s32[1]{0:T(128)} %bitcast.me_ref, ...), custom_call_target="tpu_custom_call" | custom-call | tf_op jit(solution)/shard_map/route/pallas_call | solution.py:353
  43.1 0.1 collective-permute-start.4
  43.2 5.5 %collective-permute-start = (bf16[3,32,128]{2,1,0:T(8,128)(2,1)}, bf16[3,32,128]{2,1,0:T(8,128)(2,1)S(1)}, u32[]{:S(2)}, u32[]{:S(2)}) collective-permute-start(bf16[3,32,128]{2,1,0:T(8,128)(2,1)} %get-tuple-element.23), channel_id=1, source_target_pairs={{0,12},{4,8},{8,4},{12,0},{1,13},{5,9},{9,5},{13,1},{2,14},{6,10},... | collective-permute-start | bytes 73736 | tf_op jit(solution)/shard_map/ppermute | solution.py:382
  48.7 0.1 collective-permute-start.2
  48.8 2.9 %collective-permute-start.6 = (bf16[3,2,128,256]{3,2,1,0:T(8,128)(2,1)}, bf16[3,2,128,256]{3,2,1,0:T(8,128)(2,1)S(1)}, u32[]{:S(2)}, u32[]{:S(2)}) collective-permute-start(bf16[3,2,128,256]{3,2,1,0:T(8,128)(2,1)} %get-tuple-element.27), channel_id=1, source_target_pairs={{0,12},{4,8},{8,4},{12,0},{1,13},{5,9},{9,5},{13,1},{2,14},{6,10},... | collective-permute-start | bytes 1179656 | tf_op jit(solution)/shard_map/ppermute | solution.py:382
  51.7 0.0 collective-permute-start.7
  51.7 0.8 compare_convert_fusion.spread_ref
  52.6 1.5 %fusion.3 = (s32[3]{0:T(128)}, s32[3]{0:T(128)}, s32[3]{0:T(128)}, s32[3]{0:T(128)}) fusion(s32[12]{0:T(128)} %get-tuple-element.22), kind=kLoop, calls=%fused_computation.12 | loop fusion | bytes 96 | tf_op jit(solution)/shard_map/slice | solution.py:409
  54.1 0.0 collective-permute-done.4.read_ref
  54.1 1.5 %collective-permute-start.8 = (bf16[3,2,128,256]{3,2,1,0:T(8,128)(2,1)}, bf16[3,2,128,256]{3,2,1,0:T(8,128)(2,1)S(1)}, u32[]{:S(2)}, u32[]{:S(2)}) collective-permute-start(bf16[3,2,128,256]{3,2,1,0:T(8,128)(2,1)} %get-tuple-element.29), channel_id=1, source_target_pairs={{0,4},{4,0},{8,12},{12,8},{1,5},{5,1},{9,13},{13,9},{2,6},{6,2},{1... | collective-permute-start | bytes 1179656 | tf_op jit(solution)/shard_map/ppermute | solution.py:382
  55.6 0.8 constant_dynamic-slice_fusion
  56.4 0.7 broadcast_in_dim.2
  57.1 0.7 reshape_reshape.3.skip_ref
  57.8 0.0 copy-done.8
  57.8 4.1 %carried.6 = bf16[3,32,2048]{2,1,0:T(8,128)(2,1)} custom-call(s32[3]{0:T(128)} %get-tuple-element.31.slot_ref, bf16[3,32,128]{2,1,0:T(8,128)(2,1)} %copy-done.8, bf16[6,2048,128]{2,1,0:T(8,128)(2,1)} %bitcast.5), custom_call_target="tpu_custom_call" | custom-call | flops 50331648 | bytes 1966080 | tf_op jit(solution)/shard_map/carried/pallas_call | solution.py:391
  61.8 0.0 collective-permute-done.read_ref
  61.8 0.6 collective-permute-start.5
  62.5 0.0 copy-done.7
  62.5 4.1 %carried.4 = bf16[3,32,2048]{2,1,0:T(8,128)(2,1)} custom-call(s32[3]{0:T(128)} %get-tuple-element.33.slot_ref, bf16[3,32,128]{2,1,0:T(8,128)(2,1)} %copy-done.7, bf16[6,2048,128]{2,1,0:T(8,128)(2,1)} %bitcast.6), custom_call_target="tpu_custom_call" | custom-call | flops 50331648 | bytes 1966080 | tf_op jit(solution)/shard_map/carried/pallas_call | solution.py:391
  66.5 3.1 %collective-permute-done.2.read_ref = bf16[3,32,128]{2,1,0:T(8,128)(2,1)S(1)} collective-permute-done((bf16[3,32,128]{2,1,0:T(8,128)(2,1)}, bf16[3,32,128]{2,1,0:T(8,128)(2,1)S(1)}, u32[]{:S(2)}, u32[]{:S(2)}) %collective-permute-start.2) | collective-permute-done | bytes 24608 | tf_op jit(solution)/shard_map/ppermute | solution.py:382
  69.6 0.0 collective-permute-start.1
  69.6 0.6 copy-done.6
  70.2 3.6 %carried.5 = bf16[3,32,2048]{2,1,0:T(8,128)(2,1)} custom-call(s32[3]{0:T(128)} %get-tuple-element.32.slot_ref, bf16[3,32,128]{2,1,0:T(8,128)(2,1)} %copy-done.6, bf16[6,2048,128]{2,1,0:T(8,128)(2,1)} %bitcast.7), custom_call_target="tpu_custom_call" | custom-call | flops 50331648 | bytes 1966080 | tf_op jit(solution)/shard_map/carried/pallas_call | solution.py:391
  73.9 0.0 collective-permute-done.6.rest_0_
  73.9 5.9 %collective-permute-start.3 = (bf16[3,32,2048]{2,1,0:T(8,128)(2,1)}, bf16[3,32,2048]{2,1,0:T(8,128)(2,1)S(1)}, u32[]{:S(2)}, u32[]{:S(2)}) collective-permute-start(bf16[3,32,2048]{2,1,0:T(8,128)(2,1)} %carried.5), channel_id=1, source_target_pairs={{0,8},{4,12},{8,0},{12,4},{1,9},{5,13},{9,1},{13,5},{2,10},{6,14},... | collective-permute-start | bytes 1179656 | tf_op jit(solution)/shard_map/ppermute | solution.py:382
  79.8 11.7 %within.1 = (f32[11,32,2048]{2,1,0:T(8,128)}, f32[11,32,2048]{2,1,0:T(8,128)}) custom-call(f32[1,32]{1,0:T(1,128)} %bitcast.12, f32[1,2048]{1,0:T(1,128)} %reshape_reshape.3.skip_ref, bf16[64,2048]{1,0:T(8,128)(2,1)} %compare_convert_fusion.spread_ref, f32[11,32,32]{2,1,0:T(8,128)} %step_ref.1, bf16[11,32,128]{2,1,0:T(8,128)(2,1)} %read_ref.1, ...), custom_call_target="tpu_custom_call" | custom-call | flops 369098752 | bytes 8650752 | tf_op jit(solution)/shard_map/within/pallas_call | solution.py:416
  91.5 0.0 copy-done.2
  91.5 0.1 copy.24
  91.6 0.7 reshape.84.pages_ref
  92.3 4.2 %carried.7.rest_1_ = bf16[3,32,2048]{2,1,0:T(8,128)(2,1)} custom-call(s32[3]{0:T(128)} %get-tuple-element.30.slot_ref, bf16[3,32,128]{2,1,0:T(8,128)(2,1)} %get-tuple-element.26.read_ref, bf16[6,2048,128]{2,1,0:T(8,128)(2,1)} %bitcast.8), custom_call_target="tpu_custom_call" | custom-call | flops 50331648 | bytes 1966080 | tf_op jit(solution)/shard_map/carried/pallas_call | solution.py:391
  96.5 0.6 fusion.4
  97.1 1.3 pad_add_fusion.1.span_ref
  98.4 1.8 %pad_add_fusion.span_ref = s32[2]{0:T(128)} fusion(s32[1]{0:T(128)} %get-tuple-element.35, s32[1]{0:T(128)} %get-tuple-element.34), kind=kLoop, calls=%fused_computation.9 | loop fusion | flops 2 | bytes 16 | tf_op jit(solution)/shard_map/stack | solution.py:492
  100.2 4.1 %collective-permute-done.7.rest_1_ = bf16[3,2,128,256]{3,2,1,0:T(8,128)(2,1)S(1)} collective-permute-done((bf16[3,2,128,256]{3,2,1,0:T(8,128)(2,1)}, bf16[3,2,128,256]{3,2,1,0:T(8,128)(2,1)S(1)}, u32[]{:S(2)}, u32[]{:S(2)}) %collective-permute-start.7) | collective-permute-done | bytes 393248 | tf_op jit(solution)/shard_map/ppermute | solution.py:382
  104.2 0.0 collective-permute-done.8.rest_2_
  104.2 0.7 copy-done.3
  105.0 0.1 copy-done.4
  105.1 12.4 %attention.1 = bf16[11,32,2048]{2,1,0:T(8,128)(2,1)} custom-call(s32[11]{0:T(128)} %get-tuple-element.17.source_ref, s32[11]{0:T(128)} %get-tuple-element.18.rank_ref, s32[11]{0:T(128)} %count_ref.1, s32[11]{0:T(128)} %live_ref.5, s32[88]{0:T(128)} %reshape.84.pages_ref, bf16[11,32,2048]{2,1,0:T(8,128)(2,1)} %query_ref.1, bf16[11,32,256]{2,1,0:T(8,128)(2,1)} %key_ref.1, ...), custom_call_target="tpu_custom_call" | custom-call | flops 461373440 | bytes 4325376 | tf_op jit(solution)/shard_map/attention/pallas_call | solution.py:449
  117.6 0.0 collective-permute-done.5.rest_0_
  117.6 0.8 copy-done.5
  118.3 6.4 %finish.2.rest_2_ = bf16[11,32,2048]{2,1,0:T(8,128)(2,1)} custom-call(s32[11]{0:T(128)} %get-tuple-element.16.order_ref, s32[11]{0:T(128)} %get-tuple-element.17.source_ref, s32[11]{0:T(128)} %get-tuple-element.18.rank_ref, s32[11]{0:T(128)} %live_ref.5, s32[2]{0:T(128)} %pad_add_fusion.1.span_ref, f32[1,2048]{1,0:T(1,128)} %bitcast.9, ...), custom_call_target="tpu_custom_call" | custom-call | flops 4325376 | bytes 4325376 | tf_op jit(solution)/shard_map/finish/pallas_call | solution.py:498
  124.8 0.0 collective-permute-done.1.rest_0_
  124.8 0.0 collective-permute-done.3.rest_1_
  124.8 0.7 copy-done
  125.6 0.8 copy-done.1
  126.3 7.1 %finish.3 = bf16[11,32,2048]{2,1,0:T(8,128)(2,1)} custom-call(s32[11]{0:T(128)} %get-tuple-element.16.order_ref, s32[11]{0:T(128)} %get-tuple-element.17.source_ref, s32[11]{0:T(128)} %get-tuple-element.18.rank_ref, s32[11]{0:T(128)} %live_ref.5, s32[2]{0:T(128)} %pad_add_fusion.span_ref, f32[1,2048]{1,0:T(1,128)} %bitcast.10, ...), custom_call_target="tpu_custom_call", output_to_operand_aliasing={{}: (10, {})} | custom-call | flops 4325376 | bytes 4325376 | tf_op jit(solution)/shard_map/finish/pallas_call | solution.py:498
  (13 shorter events, 0.0 us)
Async XLA Ops:
  43.1 10.9 %collective-permute-start.4 = (bf16[3,32,128]{2,1,0:T(8,128)(2,1)}, bf16[3,32,128]{2,1,0:T(8,128)(2,1)S(1)}, u32[]{:S(2)}, u32[]{:S(2)}) collective-permute-start(bf16[3,32,128]{2,1,0:T(8,128)(2,1)} %get-tuple-element.25), channel_id=1, source_target_pairs={{0,4},{4,0},{8,12},{12,8},{1,5},{5,1},{9,13},{13,9},{2,6},{6,2},{1... | collective-permute-start | bytes 73736 | tf_op jit(solution)/shard_map/ppermute | solution.py:382
  43.2 18.6 %collective-permute-start = (bf16[3,32,128]{2,1,0:T(8,128)(2,1)}, bf16[3,32,128]{2,1,0:T(8,128)(2,1)S(1)}, u32[]{:S(2)}, u32[]{:S(2)}) collective-permute-start(bf16[3,32,128]{2,1,0:T(8,128)(2,1)} %get-tuple-element.23), channel_id=1, source_target_pairs={{0,12},{4,8},{8,4},{12,0},{1,13},{5,9},{9,5},{13,1},{2,14},{6,10},... | collective-permute-start | bytes 73736 | tf_op jit(solution)/shard_map/ppermute | solution.py:382
  48.7 20.9 %collective-permute-start.2 = (bf16[3,32,128]{2,1,0:T(8,128)(2,1)}, bf16[3,32,128]{2,1,0:T(8,128)(2,1)S(1)}, u32[]{:S(2)}, u32[]{:S(2)}) collective-permute-start(bf16[3,32,128]{2,1,0:T(8,128)(2,1)} %get-tuple-element.24), channel_id=1, source_target_pairs={{0,8},{4,12},{8,0},{12,4},{1,9},{5,13},{9,1},{13,5},{2,10},{6,14},... | collective-permute-start | bytes 73736 | tf_op jit(solution)/shard_map/ppermute | solution.py:382
  48.8 25.1 %collective-permute-start.6 = (bf16[3,2,128,256]{3,2,1,0:T(8,128)(2,1)}, bf16[3,2,128,256]{3,2,1,0:T(8,128)(2,1)S(1)}, u32[]{:S(2)}, u32[]{:S(2)}) collective-permute-start(bf16[3,2,128,256]{3,2,1,0:T(8,128)(2,1)} %get-tuple-element.27), channel_id=1, source_target_pairs={{0,12},{4,8},{8,4},{12,0},{1,13},{5,9},{9,5},{13,1},{2,14},{6,10},... | collective-permute-start | bytes 1179656 | tf_op jit(solution)/shard_map/ppermute | solution.py:382
  51.7 52.5 %collective-permute-start.7 = (bf16[3,2,128,256]{3,2,1,0:T(8,128)(2,1)}, bf16[3,2,128,256]{3,2,1,0:T(8,128)(2,1)S(1)}, u32[]{:S(2)}, u32[]{:S(2)}) collective-permute-start(bf16[3,2,128,256]{3,2,1,0:T(8,128)(2,1)} %get-tuple-element.28), channel_id=1, source_target_pairs={{0,8},{4,12},{8,0},{12,4},{1,9},{5,13},{9,1},{13,5},{2,10},{6,14},... | collective-permute-start | bytes 1179656 | tf_op jit(solution)/shard_map/ppermute | solution.py:382
  54.1 3.7 %copy-start.8 = (bf16[3,32,128]{2,1,0:T(8,128)(2,1)}, bf16[3,32,128]{2,1,0:T(8,128)(2,1)S(1)}, u32[]{:S(2)}) copy-start(bf16[3,32,128]{2,1,0:T(8,128)(2,1)S(1)} %collective-permute-done.4.read_ref) | copy-start | bytes 73732
  54.1 50.2 %collective-permute-start.8 = (bf16[3,2,128,256]{3,2,1,0:T(8,128)(2,1)}, bf16[3,2,128,256]{3,2,1,0:T(8,128)(2,1)S(1)}, u32[]{:S(2)}, u32[]{:S(2)}) collective-permute-start(bf16[3,2,128,256]{3,2,1,0:T(8,128)(2,1)} %get-tuple-element.29), channel_id=1, source_target_pairs={{0,4},{4,0},{8,12},{12,8},{1,5},{5,1},{9,13},{13,9},{2,6},{6,2},{1... | collective-permute-start | bytes 1179656 | tf_op jit(solution)/shard_map/ppermute | solution.py:382
  61.8 0.6 copy-start.7
  61.8 55.7 %collective-permute-start.5 = (bf16[3,32,2048]{2,1,0:T(8,128)(2,1)}, bf16[3,32,2048]{2,1,0:T(8,128)(2,1)S(1)}, u32[]{:S(2)}, u32[]{:S(2)}) collective-permute-start(bf16[3,32,2048]{2,1,0:T(8,128)(2,1)} %carried.6), channel_id=1, source_target_pairs={{0,4},{4,0},{8,12},{12,8},{1,5},{5,1},{9,13},{13,9},{2,6},{6,2},{1... | collective-permute-start | bytes 1179656 | tf_op jit(solution)/shard_map/ppermute | solution.py:382
  69.6 0.6 copy-start.6
  69.6 55.2 %collective-permute-start.1 = (bf16[3,32,2048]{2,1,0:T(8,128)(2,1)}, bf16[3,32,2048]{2,1,0:T(8,128)(2,1)S(1)}, u32[]{:S(2)}, u32[]{:S(2)}) collective-permute-start(bf16[3,32,2048]{2,1,0:T(8,128)(2,1)} %carried.4), channel_id=1, source_target_pairs={{0,12},{4,8},{8,4},{12,0},{1,13},{5,9},{9,5},{13,1},{2,14},{6,10},... | collective-permute-start | bytes 1179656 | tf_op jit(solution)/shard_map/ppermute | solution.py:382
  73.9 17.6 %copy-start.2 = (bf16[3,2,128,256]{3,2,1,0:T(8,128)(2,1)}, bf16[3,2,128,256]{3,2,1,0:T(8,128)(2,1)S(1)}, u32[]{:S(2)}) copy-start(bf16[3,2,128,256]{3,2,1,0:T(8,128)(2,1)S(1)} %collective-permute-done.6.rest_0_) | copy-start | bytes 1179652
  73.9 50.9 %collective-permute-start.3 = (bf16[3,32,2048]{2,1,0:T(8,128)(2,1)}, bf16[3,32,2048]{2,1,0:T(8,128)(2,1)S(1)}, u32[]{:S(2)}, u32[]{:S(2)}) collective-permute-start(bf16[3,32,2048]{2,1,0:T(8,128)(2,1)} %carried.5), channel_id=1, source_target_pairs={{0,8},{4,12},{8,0},{12,4},{1,9},{5,13},{9,1},{13,5},{2,10},{6,14},... | collective-permute-start | bytes 1179656 | tf_op jit(solution)/shard_map/ppermute | solution.py:382
  92.3 4.2 %copy-start.9 = (s32[4]{0:T(128)S(1)}, s32[4]{0:T(128)}, u32[]{:S(2)}) copy-start(s32[4]{0:T(128)} %get-tuple-element.19) | copy-start | bytes 52
  104.2 0.7 copy-start.3
  104.2 0.9 copy-start.4
  117.6 0.8 copy-start.5
  124.8 0.8 copy-start
  125.6 0.8 copy-start.1

commit v2 on v1

--- a/solution.py
+++ b/solution.py
@@ -13,7 +13,9 @@
 MIB = 1 << 20
 
 ANY = pl.BlockSpec(memory_space=pl.ANY)
+VMEM = pl.BlockSpec(memory_space=pltpu.VMEM)
 SMEM = pl.BlockSpec(memory_space=pltpu.SMEM)
+PARAMS = pltpu.CompilerParams(vmem_limit_bytes=56 * MIB)
 
 
 def partner_steps(replicas):
@@ -21,110 +23,127 @@
 
 
 def route_kernel(
-    replicas,
-    slots,
-    count,
-    most,
-    page_len,
-    me_ref,
-    holder_ref,
-    slot_ref,
-    pages_ref,
-    keys_ref,
-    values_ref,
-    reads_ref,
-    *outs,
+    replicas, slots, count, most, page_len, me_ref, holder_ref, pages_ref, keys_hbm, values_hbm, *rest
 ):
     steps = partner_steps(replicas)
-    page_out = dict(zip(steps, outs[: replicas - 1]))
-    read_out = dict(zip(steps + [0], outs[replicas - 1 : 2 * replicas - 1]))
-    state_slot, source, rank, order, ends = outs[2 * replicas - 1 : 2 * replicas + 4]
-    page_sem, read_sem, seen = outs[2 * replicas + 4 :]
+    page_out = dict(zip(steps, rest[: replicas - 1]))
+    token, keys, values, packed, sems = rest[replicas - 1 :]
+    loads = [
+        pltpu.make_async_copy(keys_hbm, keys, sems.at[0]),
+        pltpu.make_async_copy(values_hbm, values, sems.at[1]),
+    ]
+    for load in loads:
+        load.start()
     me = me_ref[0]
-
-    def page_copy(array, page, out, slot, kind, place):
-        return pltpu.make_async_copy(
-            array.at[page],
-            out.at[slot, kind, pl.ds(pl.multiple_of(place * page_len, page_len), page_len)],
-            page_sem,
-        )
-
-    def clear(i, carry):
-        state_slot[i] = 0
-        return carry
-
-    lax.fori_loop(0, replicas * slots, clear, 0)
-    sent = jnp.int32(0)
-    for step in steps + [0]:
+    token[0] = me
+    for load in loads:
+        load.wait()
+    copies = []
+    for at, step in enumerate(steps):
         first = lax.bitwise_xor(me, step) * count
 
-        def serve(j, rank_here, step=step, first=first):
+        def serve(j, rank_here, at=at, first=first):
             request = first + j
-            hit = holder_ref[request] == me
-            slot = jnp.minimum(rank_here, slots - 1)
+            hit = holder_ref[0, request] == me
 
             @pl.when(hit)
             def _():
-                state_slot[step * slots + slot] = slot_ref[request]
-                if step:
-                    for place in range(most):
-                        page = pages_ref[request * most + place]
-                        page_copy(keys_ref, page, page_out[step], slot, 0, place).start()
-                        page_copy(values_ref, page, page_out[step], slot, 1, place).start()
+                slot = jnp.minimum(rank_here, slots - 1)
+                for place in range(most):
+                    page = pages_ref[place, request]
+                    rows = slice(place * page_len, (place + 1) * page_len)
+                    packed[at, slot, 0, rows, :] = keys[page]
+                    packed[at, slot, 1, rows, :] = values[page]
 
             return rank_here + hit.astype(jnp.int32)
 
-        found = lax.fori_loop(0, count, serve, jnp.int32(0))
-        if step:
-            sent = sent + found
+        lax.fori_loop(0, count, serve, jnp.int32(0))
+        copies.append(pltpu.make_async_copy(packed.at[at], page_out[step], sems.at[2 + at]))
+        copies[-1].start()
+    for copy in copies:
+        copy.wait()
+
+
+def places(replicas, slots, count):
+    state = 0
+    source = state + replicas * slots
+    rank = source + count
+    order = rank + count
+    ends = order + count
+    return state, source, rank, order, ends, ends + replicas
+
+
+def plan_kernel(replicas, slots, count, me_ref, token_ref, holder_ref, slot_ref, reads_hbm, *rest):
+    steps = partner_steps(replicas)
+    read_out = dict(zip(steps, rest[: replicas - 1]))
+    plan, seen, reads, sems = rest[replicas - 1 :]
+    state, source, rank, order, ends, mine = places(replicas, slots, count)
+    load = pltpu.make_async_copy(reads_hbm, reads, sems.at[0])
+    load.start()
+    me = me_ref[0]
+    plan[mine] = me
+
+    def clear(i, carry):
+        plan[state + i] = 0
+        return carry
+
+    lax.fori_loop(0, replicas * slots, clear, 0)
 
     def clear_seen(i, carry):
         seen[i] = 0
         return carry
 
     lax.fori_loop(0, replicas, clear_seen, 0)
+    load.wait()
 
     def ask(j, carry):
-        step = lax.bitwise_xor(me, holder_ref[me * count + j])
+        step = lax.bitwise_xor(me, holder_ref[0, me * count + j])
         slot = jnp.minimum(seen[step], slots - 1)
         seen[step] = slot + 1
-        source[j] = step
-        rank[j] = slot
-        for known in steps + [0]:
+        plan[source + j] = step
+        plan[rank + j] = slot
+        for known in steps:
 
             @pl.when(step == known)
             def _(known=known):
-                pltpu.make_async_copy(reads_ref.at[j], read_out[known].at[slot], read_sem).start()
+                pltpu.make_async_copy(reads.at[j], read_out[known].at[slot], sems.at[1]).start()
 
         return carry
 
     lax.fori_loop(0, count, ask, 0)
+    for step in steps + [0]:
+        first = lax.bitwise_xor(me, step) * count
+
+        def serve(j, rank_here, step=step, first=first):
+            hit = holder_ref[0, first + j] == me
+
+            @pl.when(hit)
+            def _():
+                plan[state + step * slots + jnp.minimum(rank_here, slots - 1)] = slot_ref[first + j]
+
+            return rank_here + hit.astype(jnp.int32)
+
+        lax.fori_loop(0, count, serve, jnp.int32(0))
     place = jnp.int32(0)
     for step in range(replicas):
 
         def put(j, at, step=step):
-            hit = source[j] == step
+            hit = plan[source + j] == step
 
             @pl.when(hit)
             def _():
-                order[at] = j
+                plan[order + at] = j
 
             return at + hit.astype(jnp.int32)
 
         place = lax.fori_loop(0, count, put, place)
-        ends[step] = place
-
-    def wait_page(i, carry):
-        page_copy(keys_ref, 0, page_out[steps[0]], 0, 0, 0).wait()
+        plan[ends + step] = place
+
+    def wait_read(i, carry):
+        pltpu.make_async_copy(reads.at[0], read_out[steps[0]].at[0], sems.at[1]).wait()
         return carry
 
-    lax.fori_loop(0, sent * (2 * most), wait_page, 0)
-
-    def wait_read(i, carry):
-        pltpu.make_async_copy(reads_ref.at[0], read_out[0].at[0], read_sem).wait()
-        return carry
-
-    lax.fori_loop(0, count, wait_read, 0)
+    lax.fori_loop(0, count - plan[ends], wait_read, 0)
 
 
 def carried_kernel(slot_ref, read_ref, state_ref, out_ref):
@@ -142,8 +161,8 @@
     per_kv,
     page_len,
     most,
-    source_ref,
-    rank_ref,
+    slots,
+    plan_ref,
     count_ref,
     live_ref,
     pages_ref,
@@ -156,9 +175,11 @@
     arrived = dict(zip(steps, rest[: replicas - 1]))
     pool_keys, pool_values, out_ref, buffer, sems = rest[replicas - 1 :]
     i, total = pl.program_id(0), pl.num_programs(0)
+    _, at_source, at_rank, _, _, at_me = places(replicas, slots, count_ref.shape[0])
 
     def fetch(j, slot):
-        step, rank = source_ref[j], rank_ref[j]
+        step, rank = plan_ref[at_source + j], plan_ref[at_rank + j]
+        request = plan_ref[at_me] * count_ref.shape[0] + j
         for known in steps:
 
             @pl.when(step == known)
@@ -168,7 +189,7 @@
         @pl.when(step == 0)
         def _():
             for place in range(most):
-                page = pages_ref[j * most + place]
+                page = pages_ref[place, request]
                 rows = pl.ds(place * page_len, page_len)
                 pltpu.make_async_copy(pool_keys.at[page], buffer.at[slot, 0, rows], sems.at[slot]).start()
                 pltpu.make_async_copy(pool_values.at[page], buffer.at[slot, 1, rows], sems.at[slot]).start()
@@ -265,22 +286,30 @@
     scaled_ref[0] = gate * decay
 
 
+def span(replicas, slots, count, phase, plan):
+    ends = places(replicas, slots, count)[4]
+    middle = plan[ends + replicas // 2 - 1]
+    return (middle, plan[ends + replicas - 1]) if phase else (jnp.zeros_like(middle), middle)
+
+
 def finish_kernel(
-    members, phase, order_ref, source_ref, rank_ref, live_ref, span_ref, gain_ref, fixed_ref, scaled_ref, *rest
+    replicas, slots, members, phase, plan_ref, live_ref, gain_ref, fixed_ref, scaled_ref, *rest
 ):
+    _, at_source, at_rank, at_order, _, _ = places(replicas, slots, live_ref.shape[0])
     arrived = dict(zip(members, rest[: len(members)]))
     out_ref, buffer, sems = rest[len(members) + phase :]
     i = pl.program_id(0)
-    first, total = span_ref[0], span_ref[1] - span_ref[0]
+    first, last = span(replicas, slots, live_ref.shape[0], phase, plan_ref)
+    total = last - first
 
     def fetch(at, slot):
-        request = order_ref[first + at]
+        request = plan_ref[at_order + first + at]
         for known in members:
 
-            @pl.when(source_ref[request] == known)
+            @pl.when(plan_ref[at_source + request] == known)
             def _(known=known):
                 pltpu.make_async_copy(
-                    arrived[known].at[rank_ref[request]], buffer.at[slot], sems.at[slot]
+                    arrived[known].at[plan_ref[at_rank + request]], buffer.at[slot], sems.at[slot]
                 ).start()
 
     @pl.when((i == 0) & (total > 0))
@@ -296,7 +325,7 @@
         now = lax.rem(i, 2)
         pltpu.make_async_copy(buffer.at[now], buffer.at[now], sems.at[now]).wait()
         positions, channels = fixed_ref.shape[1:]
-        live = live_ref[order_ref[first + i]]
+        live = live_ref[plan_ref[at_order + first + i]]
         gated = fixed_ref[0] + scaled_ref[0] * buffer[now].astype(jnp.float32)
         square = jnp.sum(gated * gated, axis=1, keepdims=True) * (1.0 / channels)
         alive = lax.broadcasted_iota(jnp.int32, (positions, 1), 0) < live
@@ -307,7 +336,7 @@
 
         @pl.when((i == 0) & (total == 0))
         def _():
-            last = order_ref[order_ref.shape[0] - 1]
+            last = plan_ref[at_order + live_ref.shape[0] - 1]
             keep = pltpu.make_async_copy(rest[len(members)].at[last], out_ref.at[0], sems.at[0])
             keep.start()
             keep.wait()
@@ -350,40 +379,49 @@
     steps = partner_steps(replicas)
     shape = jax.ShapeDtypeStruct
 
+    me = myself.reshape(1)
+    holder_row = holder.T
+    page_rows = page_ids.T
     routed = pl.pallas_call(
         functools.partial(route_kernel, replicas, slots, count, most, page_len),
         out_shape=[shape((slots, 2, most * page_len, row_width), bf16)] * (replicas - 1)
-        + [shape((slots, positions, STATE), bf16)] * replicas
-        + [
-            shape((replicas * slots,), jnp.int32),
-            shape((count,), jnp.int32),
-            shape((count,), jnp.int32),
-            shape((count,), jnp.int32),
-            shape((replicas,), jnp.int32),
+        + [shape((1,), jnp.int32)],
+        in_specs=[SMEM] * 3 + [ANY] * 2,
+        out_specs=[ANY] * (replicas - 1) + [SMEM],
+        scratch_shapes=[
+            pltpu.VMEM(page_keys.shape, bf16),
+            pltpu.VMEM(page_values.shape, bf16),
+            pltpu.VMEM((replicas - 1, slots, 2, most * page_len, row_width), bf16),
+            pltpu.SemaphoreType.DMA((replicas + 1,)),
         ],
-        in_specs=[SMEM] * 4 + [ANY] * 3,
-        out_specs=[ANY] * (2 * replicas - 1) + [SMEM] * 5,
-        scratch_shapes=[pltpu.SemaphoreType.DMA, pltpu.SemaphoreType.DMA, pltpu.SMEM((replicas,), jnp.int32)],
+        compiler_params=PARAMS,
         name="route",
-    )(
-        myself.reshape(1),
-        holder.reshape(-1),
-        cache_slot,
-        page_ids.reshape(-1),
-        page_keys,
-        page_values,
-        read_map,
-    )
+    )(me, holder_row, page_rows, page_keys, page_values)
     send_pages = dict(zip(steps, routed[: replicas - 1]))
-    send_reads = dict(zip(steps + [0], routed[replicas - 1 : 2 * replicas - 1]))
-    state_slot, source, rank, order, ends = routed[2 * replicas - 1 :]
 
     def exchange(x, step):
         return lax.ppermute(x, "replica", [(i, i ^ step) for i in range(replicas)])
 
-    reads = {s: exchange(send_reads[s], s) for s in steps}
-    reads[0] = send_reads[0]
     pages = {s: exchange(send_pages[s], s) for s in steps}
+
+    at_state, at_source, at_rank, at_order, at_ends, at_me = places(replicas, slots, count)
+    planned = pl.pallas_call(
+        functools.partial(plan_kernel, replicas, slots, count),
+        out_shape=[shape((slots, positions, STATE), bf16)] * (replicas - 1)
+        + [shape((at_me + 1,), jnp.int32)],
+        in_specs=[SMEM] * 4 + [ANY],
+        out_specs=[ANY] * (replicas - 1) + [SMEM],
+        scratch_shapes=[
+            pltpu.SMEM((replicas,), jnp.int32),
+            pltpu.VMEM(read_map.shape, bf16),
+            pltpu.SemaphoreType.DMA((2,)),
+        ],
+        compiler_params=PARAMS,
+        name="plan",
+    )(me, routed[-1], holder_row, cache_slot, read_map)
+    plan = planned[-1]
+    reads = {s: exchange(x, s) for s, x in zip(steps, planned[:-1])}
+    reads[0] = read_map
 
     states = cache_states.reshape(cache_states.shape[0], channels, STATE)
     carried = {}
@@ -395,18 +433,24 @@
                 num_scalar_prefetch=1,
                 grid=(slots,),
                 in_specs=[
-                    pl.BlockSpec((1, positions, STATE), lambda i, slot: (i, 0, 0)),
-                    pl.BlockSpec((1, channels, STATE), lambda i, slot: (slot[i], 0, 0)),
+                    pl.BlockSpec(
+                        (1, positions, STATE),
+                        (lambda i, plan: (i, 0, 0)) if s else (lambda i, plan: (plan[at_order + i], 0, 0)),
+                    ),
+                    pl.BlockSpec(
+                        (1, channels, STATE), lambda i, plan, s=s: (plan[at_state + s * slots + i], 0, 0)
+                    ),
                 ],
-                out_specs=pl.BlockSpec((1, positions, channels), lambda i, slot: (i, 0, 0)),
+                out_specs=pl.BlockSpec((1, positions, channels), lambda i, plan: (i, 0, 0)),
             ),
+            compiler_params=PARAMS,
             cost_estimate=pl.CostEstimate(
                 flops=2 * slots * positions * channels * STATE,
                 bytes_accessed=2 * slots * channels * (STATE + positions),
                 transcendentals=0,
             ),
             name="carried",
-        )(lax.slice(state_slot, (s * slots,), ((s + 1) * slots,)), reads[s], states)
+        )(plan, reads[s], states)
         if s:
             carried[s] = exchange(carried[s], s)
 
@@ -433,6 +477,7 @@
             bytes_accessed=count * positions * channels * 12,
             transcendentals=count * positions * channels,
         ),
+        compiler_params=PARAMS,
         name="within",
     )(
         log_rates.reshape(1, heads),
@@ -447,10 +492,10 @@
 
     row5 = lambda i, *refs: (i, 0, 0)
     attention_output = pl.pallas_call(
-        functools.partial(attention_kernel, replicas, kv_here, per_kv, page_len, most),
+        functools.partial(attention_kernel, replicas, kv_here, per_kv, page_len, most, slots),
         out_shape=shape((count, positions, queries.shape[2]), bf16),
         grid_spec=pltpu.PrefetchScalarGridSpec(
-            num_scalar_prefetch=5,
+            num_scalar_prefetch=4,
             grid=(count,),
             in_specs=[
                 pl.BlockSpec((1, positions, queries.shape[2]), row5),
@@ -469,13 +514,13 @@
             bytes_accessed=count * (positions * queries.shape[2] * 4 + most * page_len * row_width * 4),
             transcendentals=count * positions * kv_here * per_kv * (most * page_len + positions),
         ),
+        compiler_params=PARAMS,
         name="attention",
     )(
-        source,
-        rank,
+        plan,
         prefix_pages,
         suffix_length,
-        lax.dynamic_slice_in_dim(page_ids, myself * count, count, 0).reshape(-1),
+        page_rows,
         queries,
         suffix_keys,
         suffix_values,
@@ -487,19 +532,18 @@
     mamba_output = None
     early = steps[replicas // 2 :] + [0]
     late = steps[: replicas // 2]
-    middle = ends[replicas // 2 - 1]
     for phase, members in enumerate([early, late]):
-        span = jnp.stack([middle, ends[replicas - 1]] if phase else [jnp.zeros_like(middle), middle])
-
-        def place(i, order, source, rank, live, span):
-            at = jnp.minimum(span[0] + i, jnp.maximum(span[1] - 1, 0))
-            return (order[at], 0, 0)
+
+        def place(i, plan, live, phase=phase):
+            first, last = span(replicas, slots, count, phase, plan)
+            at = jnp.minimum(first + i, jnp.maximum(last - 1, 0))
+            return (plan[at_order + at], 0, 0)
 
         mamba_output = pl.pallas_call(
-            functools.partial(finish_kernel, members, phase),
+            functools.partial(finish_kernel, replicas, slots, members, phase),
             out_shape=shape((count, positions, channels), bf16),
             grid_spec=pltpu.PrefetchScalarGridSpec(
-                num_scalar_prefetch=5,
+                num_scalar_prefetch=2,
                 grid=(min(count, slots * len(members)),),
                 in_specs=[
                     pl.BlockSpec((1, channels), lambda i, *refs: (0, 0)),
@@ -513,19 +557,17 @@
                     pltpu.SemaphoreType.DMA((2,)),
                 ],
             ),
-            input_output_aliases={8 + len(members): 0} if phase else {},
+            input_output_aliases={5 + len(members): 0} if phase else {},
             cost_estimate=pl.CostEstimate(
                 flops=6 * count * positions * channels,
                 bytes_accessed=count * positions * channels * 6,
                 transcendentals=0,
             ),
+            compiler_params=PARAMS,
             name="finish",
         )(
-            order,
-            source,
-            rank,
+            plan,
             suffix_length,
-            span,
             norm_gain.reshape(1, channels),
             fixed,
             scaled,

time: 135 us -> 92.4 us (0.68)
  Pallas kernels: 94.6 us -> 61 us
  waiting for transfers between devices: 7.18 us -> 0.02 us
  starting transfers between devices: 16.7 us -> 23.3 us
  local copies, waits for them, and re-layouts: 10.2 us -> 5.19 us
  other arithmetic: 3.95 us -> 0.82 us
    pallas_call x1, Pallas kernels: 41 us -> 3.76 us  [per_device(): pl.pallas_call(functools.partial(route_kernel, replicas, slots, count, mo...]
    ppermute x9, waiting for transfers between devices: 7.18 us -> 0.02 us  [exchange(): return lax.ppermute(x, 'replica', [(i, i ^ step) for i in range(replicas)])]
    ppermute x9, starting transfers between devices: 16.7 us -> 23.3 us  [exchange(): return lax.ppermute(x, 'replica', [(i, i ^ step) for i in range(replicas)])]
    pallas_call x2 -> x3, Pallas kernels: 13.5 us -> 16.8 us  [the longest x2 13.4 us: per_device(): pl.pallas_call(functools.partial(finish_kernel, replicas, slots, members,...]
    another operation x2 -> x0, other arithmetic: 3.11 us -> none  [per_device(): jnp.stack([middle, ends[replicas - 1]] if phase else [jnp.zeros_like(midd...]
    slice x2 -> x0, local copies, waits for them, and re-layouts: 2.07 us -> none  [the longest x1 1.48 us: per_device(): lax.slice(state_slot, (s * slots,), ((s + 1) * slots,))]
    unnamed x21 -> x20, local copies, waits for them, and re-layouts: 4.56 us -> 3.78 us
  transfers between devices with their start and end apart: 9 -> 9, of which waited for: 2 -> 0; matrix products, arithmetic and copies ran while one was open for 7% -> 2% of each run, Pallas kernels for 35% -> 55%
where the time goes in v2:
time: 92.4 us; the launch traced here: 91.1 us
  Pallas kernels  61 us (66%)
  starting transfers between devices  23.3 us (25%)
  local copies, waits for them, and re-layouts  5.19 us (6%)
    ppermute x9, starting transfers between devices, exchange(): return lax.ppermute(x, 'replica', [(i, i ^ step) for i in range(replicas)])  23.3 us
    pallas_call x4, Pallas kernels, per_device(): pl.pallas_call(carried_kernel, out_shape=shape((slots, positions, channel...  16.4 us
    pallas_call x2, Pallas kernels, per_device(): pl.pallas_call(functools.partial(finish_kernel, replicas, slots, members,...  13.4 us
    pallas_call x1, Pallas kernels, per_device(): pl.pallas_call(functools.partial(attention_kernel, replicas, kv_here, per...  12.4 us
    pallas_call x1, Pallas kernels, per_device(): pl.pallas_call(within_kernel, out_shape=[shape((count, positions, channel...  11.7 us
    unnamed x20, local copies, waits for them, and re-layouts  3.78 us
    pallas_call x1, Pallas kernels, per_device(): pl.pallas_call(functools.partial(route_kernel, replicas, slots, count, mo...  3.76 us
    pallas_call x1, Pallas kernels, per_device(): pl.pallas_call(functools.partial(plan_kernel, replicas, slots, count), ou...  3.34 us
  transfers between devices with their start and end apart: 9, of which 0 were waited for; matrix products, arithmetic and copies ran while one was open for 2% of the time, Pallas kernels for 55%

profile of v2, /device:TPU:0, one launch (start us, length us, event | category | flops | bytes accessed | tf_op | source)
XLA Modules:
  0.0 91.1 jit_solution(5509251594863321030)
XLA Ops:
  0.6 3.8 %route.1 = (bf16[3,2,128,256]{3,2,1,0:T(8,128)(2,1)}, bf16[3,2,128,256]{3,2,1,0:T(8,128)(2,1)}, bf16[3,2,128,256]{3,2,1,0:T(8,128)(2,1)}, s32[1]{0:T(128)}) custom-call(s32[1]{0:T(128)} %bitcast.me_ref, s32[1,44]{1,0:T(1,128)} %bitcast.14, s32[8,44]{1,0:T(8,128)} %bitcast.12, bf16[48,16,256]{2,1,0:T(8,128)(2,1)} %rest_3_.1, bf16[48,16,256]{2,1,0:T(8,128)(2,1)} %rest_4_.1), custom_call_target="tpu_custom_call" | custom-call | tf_op jit(solution)/shard_map/route/pallas_call | solution.py:385
  4.4 5.1 %collective-permute-start.6 = (bf16[3,2,128,256]{3,2,1,0:T(8,128)(2,1)}, bf16[3,2,128,256]{3,2,1,0:T(8,128)(2,1)S(1)}, u32[]{:S(2)}, u32[]{:S(2)}) collective-permute-start(bf16[3,2,128,256]{3,2,1,0:T(8,128)(2,1)} %get-tuple-element.19), channel_id=1, source_target_pairs={{0,12},{4,8},{8,4},{12,0},{1,13},{5,9},{9,5},{13,1},{2,14},{6,10},... | collective-permute-start | bytes 1179656 | tf_op jit(solution)/shard_map/ppermute | solution.py:403
  9.5 3.3 %plan.1 = (bf16[3,32,128]{2,1,0:T(8,128)(2,1)}, bf16[3,32,128]{2,1,0:T(8,128)(2,1)}, bf16[3,32,128]{2,1,0:T(8,128)(2,1)}, s32[50]{0:T(128)}) custom-call(s32[1]{0:T(128)} %bitcast.me_ref, s32[1]{0:T(128)} %get-tuple-element.12.token_ref, s32[1,44]{1,0:T(1,128)} %bitcast.15, s32[44]{0:T(128)} %slot_ref.1, bf16[11,32,128]{2,1,0:T(8,128)(2,1)} %read_ref.3), custom_call_target="tpu_custom_call" | custom-call | tf_op jit(solution)/shard_map/plan/pallas_call | solution.py:408
  12.8 0.1 collective-permute-start.4
  12.9 0.9 collective-permute-start
  13.8 2.6 %collective-permute-start.2 = (bf16[3,32,128]{2,1,0:T(8,128)(2,1)}, bf16[3,32,128]{2,1,0:T(8,128)(2,1)S(1)}, u32[]{:S(2)}, u32[]{:S(2)}) collective-permute-start(bf16[3,32,128]{2,1,0:T(8,128)(2,1)} %get-tuple-element.17), channel_id=1, source_target_pairs={{0,8},{4,12},{8,0},{12,4},{1,9},{5,13},{9,1},{13,5},{2,10},{6,14},... | collective-permute-start | bytes 73736 | tf_op jit(solution)/shard_map/ppermute | solution.py:403
  16.4 0.3 collective-permute-start.7
  16.7 0.7 broadcast_in_dim.2
  17.4 0.7 reshape_reshape.3.skip_ref
  18.1 0.0 copy-start.9
  18.1 4.2 %carried.7.rest_1_ = bf16[3,32,2048]{2,1,0:T(8,128)(2,1)} custom-call(s32[50]{0:T(128)} %get-tuple-element.13.slot_ref.plan_ref, bf16[11,32,128]{2,1,0:T(8,128)(2,1)} %read_ref.3, bf16[6,2048,128]{2,1,0:T(8,128)(2,1)} %bitcast.6), custom_call_target="tpu_custom_call" | custom-call | flops 50331648 | bytes 1966080 | tf_op jit(solution)/shard_map/carried/pallas_call | solution.py:429
  22.3 0.0 collective-permute-done.4.read_ref
  22.3 0.0 copy-start.8
  22.3 0.0 copy-done.9
  22.3 1.2 %collective-permute-start.8 = (bf16[3,2,128,256]{3,2,1,0:T(8,128)(2,1)S(1)}, bf16[3,2,128,256]{3,2,1,0:T(8,128)(2,1)S(1)}, u32[]{:S(2)}, u32[]{:S(2)}) collective-permute-start(bf16[3,2,128,256]{3,2,1,0:T(8,128)(2,1)S(1)} %copy-done.9), channel_id=1, source_target_pairs={{0,4},{4,0},{8,12},{12,8},{1,5},{5,1},{9,13},{13,9},{2,6},{6,2},{1... | collective-permute-start | bytes 1179656 | tf_op jit(solution)/shard_map/ppermute | solution.py:403
  23.5 0.0 copy-done.8
  23.5 4.1 %carried.6 = bf16[3,32,2048]{2,1,0:T(8,128)(2,1)} custom-call(s32[50]{0:T(128)} %get-tuple-element.13.slot_ref.plan_ref, bf16[3,32,128]{2,1,0:T(8,128)(2,1)} %copy-done.8, bf16[6,2048,128]{2,1,0:T(8,128)(2,1)} %bitcast.7), custom_call_target="tpu_custom_call" | custom-call | flops 50331648 | bytes 1966080 | tf_op jit(solution)/shard_map/carried/pallas_call | solution.py:429
  27.6 0.0 collective-permute-done.read_ref
  27.6 0.0 copy-start.7
  27.6 10.3 %collective-permute-start.5 = (bf16[3,32,2048]{2,1,0:T(8,128)(2,1)}, bf16[3,32,2048]{2,1,0:T(8,128)(2,1)S(1)}, u32[]{:S(2)}, u32[]{:S(2)}) collective-permute-start(bf16[3,32,2048]{2,1,0:T(8,128)(2,1)} %carried.6), channel_id=1, source_target_pairs={{0,4},{4,0},{8,12},{12,8},{1,5},{5,1},{9,13},{13,9},{2,6},{6,2},{1... | collective-permute-start | bytes 1179656 | tf_op jit(solution)/shard_map/ppermute | solution.py:403
  37.9 0.0 copy-done.7
  37.9 4.1 %carried.4 = bf16[3,32,2048]{2,1,0:T(8,128)(2,1)} custom-call(s32[50]{0:T(128)} %get-tuple-element.13.slot_ref.plan_ref, bf16[3,32,128]{2,1,0:T(8,128)(2,1)} %copy-done.7, bf16[6,2048,128]{2,1,0:T(8,128)(2,1)} %bitcast.8), custom_call_target="tpu_custom_call" | custom-call | flops 50331648 | bytes 1966080 | tf_op jit(solution)/shard_map/carried/pallas_call | solution.py:429
  42.0 0.0 collective-permute-done.2.read_ref
  42.0 0.0 copy-start.6
  42.0 2.7 %collective-permute-start.1 = (bf16[3,32,2048]{2,1,0:T(8,128)(2,1)}, bf16[3,32,2048]{2,1,0:T(8,128)(2,1)S(1)}, u32[]{:S(2)}, u32[]{:S(2)}) collective-permute-start(bf16[3,32,2048]{2,1,0:T(8,128)(2,1)} %carried.4), channel_id=1, source_target_pairs={{0,12},{4,8},{8,4},{12,0},{1,13},{5,9},{9,5},{13,1},{2,14},{6,10},... | collective-permute-start | bytes 1179656 | tf_op jit(solution)/shard_map/ppermute | solution.py:403
  44.7 0.0 copy-done.6
  44.7 4.1 %carried.5 = bf16[3,32,2048]{2,1,0:T(8,128)(2,1)} custom-call(s32[50]{0:T(128)} %get-tuple-element.13.slot_ref.plan_ref, bf16[3,32,128]{2,1,0:T(8,128)(2,1)} %copy-done.6, bf16[6,2048,128]{2,1,0:T(8,128)(2,1)} %bitcast.9), custom_call_target="tpu_custom_call" | custom-call | flops 50331648 | bytes 1966080 | tf_op jit(solution)/shard_map/carried/pallas_call | solution.py:429
  48.8 0.0 collective-permute-done.6.rest_0_
  48.8 0.1 collective-permute-start.3
  48.9 0.8 compare_convert_fusion.spread_ref
  49.7 11.7 %within.1 = (f32[11,32,2048]{2,1,0:T(8,128)}, f32[11,32,2048]{2,1,0:T(8,128)}) custom-call(f32[1,32]{1,0:T(1,128)} %bitcast.16, f32[1,2048]{1,0:T(1,128)} %reshape_reshape.3.skip_ref, bf16[64,2048]{1,0:T(8,128)(2,1)} %compare_convert_fusion.spread_ref, f32[11,32,32]{2,1,0:T(8,128)} %step_ref.1, bf16[11,32,128]{2,1,0:T(8,128)(2,1)} %read_ref.3, ...), custom_call_target="tpu_custom_call" | custom-call | flops 369098752 | bytes 8650752 | tf_op jit(solution)/shard_map/within/pallas_call | solution.py:460
  61.3 0.0 copy-done.3
  61.4 0.0 collective-permute-done.7.rest_1_
  61.4 0.0 copy-start.4
  61.4 0.0 collective-permute-done.8.rest_2_
  61.4 0.7 copy-done.4
  62.1 0.8 copy-done.5
  62.9 12.4 %attention.1 = bf16[11,32,2048]{2,1,0:T(8,128)(2,1)} custom-call(s32[50]{0:T(128)} %get-tuple-element.13.slot_ref.plan_ref, s32[11]{0:T(128)} %count_ref.1, s32[11]{0:T(128)} %live_ref.5, s32[8,44]{1,0:T(8,128)} %bitcast.13, bf16[11,32,2048]{2,1,0:T(8,128)(2,1)} %query_ref.1, bf16[11,32,256]{2,1,0:T(8,128)(2,1)} %key_ref.1, bf16[11,32,256]{2,1,0:T(8,128)(2,1)} %value_ref.1, ...), custom_call_target="tpu_custom_call" | custom-call | flops 461373440 | bytes 4325376 | tf_op jit(solution)/shard_map/attention/pallas_call | solution.py:494
  75.3 0.0 collective-permute-done.5.rest_0_
  75.4 0.0 copy-start.1
  75.4 0.7 copy-done.1
  76.1 6.4 %finish.2.rest_2_ = bf16[11,32,2048]{2,1,0:T(8,128)(2,1)} custom-call(s32[50]{0:T(128)} %get-tuple-element.13.slot_ref.plan_ref, s32[11]{0:T(128)} %live_ref.5, f32[1,2048]{1,0:T(1,128)} %bitcast.10, f32[11,32,2048]{2,1,0:T(8,128)} %get-tuple-element.14.fixed_ref, f32[11,32,2048]{2,1,0:T(8,128)} %get-tuple-element.15.scaled_ref, ...), custom_call_target="tpu_custom_call" | custom-call | flops 4325376 | bytes 4325376 | tf_op jit(solution)/shard_map/finish/pallas_call | solution.py:542
  82.5 0.0 collective-permute-done.1.rest_0_
  82.5 0.0 copy-start
  82.6 0.0 collective-permute-done.3.rest_1_
  82.6 0.7 copy-done
  83.3 0.8 copy-done.2
  84.1 7.0 %finish.3 = bf16[11,32,2048]{2,1,0:T(8,128)(2,1)} custom-call(s32[50]{0:T(128)} %get-tuple-element.13.slot_ref.plan_ref, s32[11]{0:T(128)} %live_ref.5, f32[1,2048]{1,0:T(1,128)} %bitcast.11, f32[11,32,2048]{2,1,0:T(8,128)} %get-tuple-element.14.fixed_ref, f32[11,32,2048]{2,1,0:T(8,128)} %get-tuple-element.15.scaled_ref, ...), custom_call_target="tpu_custom_call", output_to_operand_aliasing={{}: (7, {})} | custom-call | flops 4325376 | bytes 4325376 | tf_op jit(solution)/shard_map/finish/pallas_call | solution.py:542
  (5 shorter events, 0.0 us)
Async XLA Ops:
  4.4 44.4 %collective-permute-start.6 = (bf16[3,2,128,256]{3,2,1,0:T(8,128)(2,1)}, bf16[3,2,128,256]{3,2,1,0:T(8,128)(2,1)S(1)}, u32[]{:S(2)}, u32[]{:S(2)}) collective-permute-start(bf16[3,2,128,256]{3,2,1,0:T(8,128)(2,1)} %get-tuple-element.19), channel_id=1, source_target_pairs={{0,12},{4,8},{8,4},{12,0},{1,13},{5,9},{9,5},{13,1},{2,14},{6,10},... | collective-permute-start | bytes 1179656 | tf_op jit(solution)/shard_map/ppermute | solution.py:403
  12.8 9.5 %collective-permute-start.4 = (bf16[3,32,128]{2,1,0:T(8,128)(2,1)}, bf16[3,32,128]{2,1,0:T(8,128)(2,1)S(1)}, u32[]{:S(2)}, u32[]{:S(2)}) collective-permute-start(bf16[3,32,128]{2,1,0:T(8,128)(2,1)} %get-tuple-element.18), channel_id=1, source_target_pairs={{0,4},{4,0},{8,12},{12,8},{1,5},{5,1},{9,13},{13,9},{2,6},{6,2},{1... | collective-permute-start | bytes 73736 | tf_op jit(solution)/shard_map/ppermute | solution.py:403
  12.9 14.7 %collective-permute-start = (bf16[3,32,128]{2,1,0:T(8,128)(2,1)}, bf16[3,32,128]{2,1,0:T(8,128)(2,1)S(1)}, u32[]{:S(2)}, u32[]{:S(2)}) collective-permute-start(bf16[3,32,128]{2,1,0:T(8,128)(2,1)} %get-tuple-element.16), channel_id=1, source_target_pairs={{0,12},{4,8},{8,4},{12,0},{1,13},{5,9},{9,5},{13,1},{2,14},{6,10},... | collective-permute-start | bytes 73736 | tf_op jit(solution)/shard_map/ppermute | solution.py:403
  13.8 28.2 %collective-permute-start.2 = (bf16[3,32,128]{2,1,0:T(8,128)(2,1)}, bf16[3,32,128]{2,1,0:T(8,128)(2,1)S(1)}, u32[]{:S(2)}, u32[]{:S(2)}) collective-permute-start(bf16[3,32,128]{2,1,0:T(8,128)(2,1)} %get-tuple-element.17), channel_id=1, source_target_pairs={{0,8},{4,12},{8,0},{12,4},{1,9},{5,13},{9,1},{13,5},{2,10},{6,14},... | collective-permute-start | bytes 73736 | tf_op jit(solution)/shard_map/ppermute | solution.py:403
  16.4 45.0 %collective-permute-start.7 = (bf16[3,2,128,256]{3,2,1,0:T(8,128)(2,1)}, bf16[3,2,128,256]{3,2,1,0:T(8,128)(2,1)S(1)}, u32[]{:S(2)}, u32[]{:S(2)}) collective-permute-start(bf16[3,2,128,256]{3,2,1,0:T(8,128)(2,1)} %get-tuple-element.20), channel_id=1, source_target_pairs={{0,8},{4,12},{8,0},{12,4},{1,9},{5,13},{9,1},{13,5},{2,10},{6,14},... | collective-permute-start | bytes 1179656 | tf_op jit(solution)/shard_map/ppermute | solution.py:403
  18.1 4.2 %copy-start.9 = (bf16[3,2,128,256]{3,2,1,0:T(8,128)(2,1)S(1)}, bf16[3,2,128,256]{3,2,1,0:T(8,128)(2,1)}, u32[]{:S(2)}) copy-start(bf16[3,2,128,256]{3,2,1,0:T(8,128)(2,1)} %get-tuple-element.21) | copy-start | bytes 1179652
  22.3 1.2 %copy-start.8 = (bf16[3,32,128]{2,1,0:T(8,128)(2,1)}, bf16[3,32,128]{2,1,0:T(8,128)(2,1)S(1)}, u32[]{:S(2)}) copy-start(bf16[3,32,128]{2,1,0:T(8,128)(2,1)S(1)} %collective-permute-done.4.read_ref) | copy-start | bytes 73732
  22.3 39.1 %collective-permute-start.8 = (bf16[3,2,128,256]{3,2,1,0:T(8,128)(2,1)S(1)}, bf16[3,2,128,256]{3,2,1,0:T(8,128)(2,1)S(1)}, u32[]{:S(2)}, u32[]{:S(2)}) collective-permute-start(bf16[3,2,128,256]{3,2,1,0:T(8,128)(2,1)S(1)} %copy-done.9), channel_id=1, source_target_pairs={{0,4},{4,0},{8,12},{12,8},{1,5},{5,1},{9,13},{13,9},{2,6},{6,2},{1... | collective-permute-start | bytes 1179656 | tf_op jit(solution)/shard_map/ppermute | solution.py:403
  27.6 10.3 %copy-start.7 = (bf16[3,32,128]{2,1,0:T(8,128)(2,1)}, bf16[3,32,128]{2,1,0:T(8,128)(2,1)S(1)}, u32[]{:S(2)}) copy-start(bf16[3,32,128]{2,1,0:T(8,128)(2,1)S(1)} %collective-permute-done.read_ref) | copy-start | bytes 73732
  27.6 47.8 %collective-permute-start.5 = (bf16[3,32,2048]{2,1,0:T(8,128)(2,1)}, bf16[3,32,2048]{2,1,0:T(8,128)(2,1)S(1)}, u32[]{:S(2)}, u32[]{:S(2)}) collective-permute-start(bf16[3,32,2048]{2,1,0:T(8,128)(2,1)} %carried.6), channel_id=1, source_target_pairs={{0,4},{4,0},{8,12},{12,8},{1,5},{5,1},{9,13},{13,9},{2,6},{6,2},{1... | collective-permute-start | bytes 1179656 | tf_op jit(solution)/shard_map/ppermute | solution.py:403
  42.0 2.7 %copy-start.6 = (bf16[3,32,128]{2,1,0:T(8,128)(2,1)}, bf16[3,32,128]{2,1,0:T(8,128)(2,1)S(1)}, u32[]{:S(2)}) copy-start(bf16[3,32,128]{2,1,0:T(8,128)(2,1)S(1)} %collective-permute-done.2.read_ref) | copy-start | bytes 73732
  42.0 40.6 %collective-permute-start.1 = (bf16[3,32,2048]{2,1,0:T(8,128)(2,1)}, bf16[3,32,2048]{2,1,0:T(8,128)(2,1)S(1)}, u32[]{:S(2)}, u32[]{:S(2)}) collective-permute-start(bf16[3,32,2048]{2,1,0:T(8,128)(2,1)} %carried.4), channel_id=1, source_target_pairs={{0,12},{4,8},{8,4},{12,0},{1,13},{5,9},{9,5},{13,1},{2,14},{6,10},... | collective-permute-start | bytes 1179656 | tf_op jit(solution)/shard_map/ppermute | solution.py:403
  48.8 12.6 %copy-start.3 = (bf16[3,2,128,256]{3,2,1,0:T(8,128)(2,1)}, bf16[3,2,128,256]{3,2,1,0:T(8,128)(2,1)S(1)}, u32[]{:S(2)}) copy-start(bf16[3,2,128,256]{3,2,1,0:T(8,128)(2,1)S(1)} %collective-permute-done.6.rest_0_) | copy-start | bytes 1179652
  48.8 33.8 %collective-permute-start.3 = (bf16[3,32,2048]{2,1,0:T(8,128)(2,1)}, bf16[3,32,2048]{2,1,0:T(8,128)(2,1)S(1)}, u32[]{:S(2)}, u32[]{:S(2)}) collective-permute-start(bf16[3,32,2048]{2,1,0:T(8,128)(2,1)} %carried.5), channel_id=1, source_target_pairs={{0,8},{4,12},{8,0},{12,4},{1,9},{5,13},{9,1},{13,5},{2,10},{6,14},... | collective-permute-start | bytes 1179656 | tf_op jit(solution)/shard_map/ppermute | solution.py:403
  61.4 0.7 copy-start.4
  62.1 0.8 copy-start.5
  75.4 0.8 copy-start.1
  82.5 0.7 copy-start
  83.3 0.8 copy-start.2

commit v3 on v2

--- a/solution.py
+++ b/solution.py
@@ -15,19 +15,46 @@
 ANY = pl.BlockSpec(memory_space=pl.ANY)
 VMEM = pl.BlockSpec(memory_space=pltpu.VMEM)
 SMEM = pl.BlockSpec(memory_space=pltpu.SMEM)
-PARAMS = pltpu.CompilerParams(vmem_limit_bytes=56 * MIB)
+WIDE = pltpu.CompilerParams(vmem_limit_bytes=60 * MIB)
+PARAMS = pltpu.CompilerParams(vmem_limit_bytes=24 * MIB)
 
 
 def partner_steps(replicas):
     return list(range(replicas - 1, 0, -1))
 
 
+def places(replicas, slots, count):
+    state = 0
+    source = state + replicas * slots
+    rank = source + count
+    order = rank + count
+    ends = order + count
+    return state, source, rank, order, ends, ends + replicas
+
+
 def route_kernel(
-    replicas, slots, count, most, page_len, me_ref, holder_ref, pages_ref, keys_hbm, values_hbm, *rest
+    replicas,
+    slots,
+    count,
+    most,
+    page_len,
+    me_ref,
+    holder_ref,
+    slot_ref,
+    pages_ref,
+    keys_hbm,
+    values_hbm,
+    reads_hbm,
+    *rest,
 ):
     steps = partner_steps(replicas)
-    page_out = dict(zip(steps, rest[: replicas - 1]))
-    token, keys, values, packed, sems = rest[replicas - 1 :]
+    read_out = dict(zip(steps, rest[: replicas - 1]))
+    page_out = dict(zip(steps, rest[replicas - 1 : 2 * replicas - 2]))
+    plan, keys, values, packed, seen, reads, sems = rest[2 * replicas - 2 :]
+    read_sem = sems.at[replicas + 1]
+    load_reads = pltpu.make_async_copy(reads_hbm, reads, sems.at[replicas + 2])
+    load_reads.start()
+    state, source, rank, order, ends, mine = places(replicas, slots, count)
     loads = [
         pltpu.make_async_copy(keys_hbm, keys, sems.at[0]),
         pltpu.make_async_copy(values_hbm, values, sems.at[1]),
@@ -35,52 +62,6 @@
     for load in loads:
         load.start()
     me = me_ref[0]
-    token[0] = me
-    for load in loads:
-        load.wait()
-    copies = []
-    for at, step in enumerate(steps):
-        first = lax.bitwise_xor(me, step) * count
-
-        def serve(j, rank_here, at=at, first=first):
-            request = first + j
-            hit = holder_ref[0, request] == me
-
-            @pl.when(hit)
-            def _():
-                slot = jnp.minimum(rank_here, slots - 1)
-                for place in range(most):
-                    page = pages_ref[place, request]
-                    rows = slice(place * page_len, (place + 1) * page_len)
-                    packed[at, slot, 0, rows, :] = keys[page]
-                    packed[at, slot, 1, rows, :] = values[page]
-
-            return rank_here + hit.astype(jnp.int32)
-
-        lax.fori_loop(0, count, serve, jnp.int32(0))
-        copies.append(pltpu.make_async_copy(packed.at[at], page_out[step], sems.at[2 + at]))
-        copies[-1].start()
-    for copy in copies:
-        copy.wait()
-
-
-def places(replicas, slots, count):
-    state = 0
-    source = state + replicas * slots
-    rank = source + count
-    order = rank + count
-    ends = order + count
-    return state, source, rank, order, ends, ends + replicas
-
-
-def plan_kernel(replicas, slots, count, me_ref, token_ref, holder_ref, slot_ref, reads_hbm, *rest):
-    steps = partner_steps(replicas)
-    read_out = dict(zip(steps, rest[: replicas - 1]))
-    plan, seen, reads, sems = rest[replicas - 1 :]
-    state, source, rank, order, ends, mine = places(replicas, slots, count)
-    load = pltpu.make_async_copy(reads_hbm, reads, sems.at[0])
-    load.start()
-    me = me_ref[0]
     plan[mine] = me
 
     def clear(i, carry):
@@ -94,7 +75,7 @@
         return carry
 
     lax.fori_loop(0, replicas, clear_seen, 0)
-    load.wait()
+    load_reads.wait()
 
     def ask(j, carry):
         step = lax.bitwise_xor(me, holder_ref[0, me * count + j])
@@ -106,24 +87,39 @@
 
             @pl.when(step == known)
             def _(known=known):
-                pltpu.make_async_copy(reads.at[j], read_out[known].at[slot], sems.at[1]).start()
-
-        return carry
-
-    lax.fori_loop(0, count, ask, 0)
-    for step in steps + [0]:
+                pltpu.make_async_copy(reads.at[j], read_out[known].at[slot], read_sem).start()
+
+        return carry + (step != 0).astype(jnp.int32)
+
+    asked = lax.fori_loop(0, count, ask, jnp.int32(0))
+    for load in loads:
+        load.wait()
+    copies = []
+    for at, step in enumerate(steps + [0]):
         first = lax.bitwise_xor(me, step) * count
 
-        def serve(j, rank_here, step=step, first=first):
-            hit = holder_ref[0, first + j] == me
+        def serve(j, rank_here, at=at, step=step, first=first):
+            request = first + j
+            hit = holder_ref[0, request] == me
 
             @pl.when(hit)
             def _():
-                plan[state + step * slots + jnp.minimum(rank_here, slots - 1)] = slot_ref[first + j]
+                slot = jnp.minimum(rank_here, slots - 1)
+                plan[state + step * slots + slot] = slot_ref[request]
+                if step:
+                    for place in range(most):
+                        page = pages_ref[place, request]
+                        rows = slice(place * page_len, (place + 1) * page_len)
+                        packed[at, slot, 0, rows, :] = keys[page]
+                        packed[at, slot, 1, rows, :] = values[page]
 
             return rank_here + hit.astype(jnp.int32)
 
         lax.fori_loop(0, count, serve, jnp.int32(0))
+        if step:
+            copies.append(pltpu.make_async_copy(packed.at[at], page_out[step], sems.at[2 + at]))
+            copies[-1].start()
+
     place = jnp.int32(0)
     for step in range(replicas):
 
@@ -140,19 +136,59 @@
         plan[ends + step] = place
 
     def wait_read(i, carry):
-        pltpu.make_async_copy(reads.at[0], read_out[steps[0]].at[0], sems.at[1]).wait()
+        pltpu.make_async_copy(reads.at[0], read_out[steps[0]].at[0], read_sem).wait()
         return carry
 
-    lax.fori_loop(0, count - plan[ends], wait_read, 0)
-
-
-def carried_kernel(slot_ref, read_ref, state_ref, out_ref):
-    out_ref[0] = lax.dot_general(
-        read_ref[0],
-        state_ref[0],
-        (((1,), (1,)), ((), ())),
-        preferred_element_type=jnp.float32,
-    ).astype(out_ref.dtype)
+    lax.fori_loop(0, asked, wait_read, 0)
+    for copy in copies:
+        copy.wait()
+
+
+def carried_kernel(replicas, slots, count, steps, plan_ref, *rest):
+    at_state, _, _, at_order, _, _ = places(replicas, slots, count)
+    reads_hbm, states_hbm = rest[: len(steps)], rest[len(steps)]
+    outs = rest[-3 - len(steps) : -3]
+    reads, states, sems = rest[-3:]
+    channels = states.shape[1]
+    positions = reads.shape[2]
+    copies = []
+    for n, step in enumerate(steps):
+        copies.append([])
+        for k in range(slots):
+            which = k if step else plan_ref[at_order + k]
+            state = plan_ref[at_state + step * slots + k]
+            copies[n].append(pltpu.make_async_copy(reads_hbm[n].at[which], reads.at[n, k], sems.at[n, 2 * k]))
+            copies[n].append(
+                pltpu.make_async_copy(
+                    states_hbm.at[state],
+                    states.at[n, :, k * STATE : (k + 1) * STATE],
+                    sems.at[n, 2 * k + 1],
+                )
+            )
+        for copy in copies[n]:
+            copy.start()
+    blank = jnp.zeros((positions, STATE), jnp.bfloat16)
+    spare = STATE - slots * positions
+    tile = 512
+    for n in range(len(steps)):
+        for copy in copies[n]:
+            copy.wait()
+        rows = [
+            jnp.concatenate([reads[n, k] if j == k else blank for j in range(slots)], axis=1)
+            for k in range(slots)
+        ]
+        if spare:
+            rows.append(jnp.zeros((spare, slots * STATE), jnp.bfloat16))
+        maps = jnp.concatenate(rows, axis=0)
+        for first in range(0, channels, tile):
+            product = lax.dot_general(
+                states[n, first : first + tile],
+                maps,
+                (((1,), (1,)), ((), ())),
+                preferred_element_type=jnp.float32,
+            ).T.astype(jnp.bfloat16)
+            for k in range(slots):
+                outs[n][k, :, first : first + tile] = product[k * positions : (k + 1) * positions]
 
 
 def attention_kernel(
@@ -286,60 +322,44 @@
     scaled_ref[0] = gate * decay
 
 
-def span(replicas, slots, count, phase, plan):
-    ends = places(replicas, slots, count)[4]
-    middle = plan[ends + replicas // 2 - 1]
-    return (middle, plan[ends + replicas - 1]) if phase else (jnp.zeros_like(middle), middle)
-
-
 def finish_kernel(
-    replicas, slots, members, phase, plan_ref, live_ref, gain_ref, fixed_ref, scaled_ref, *rest
+    replicas, slots, members, chained, plan_ref, live_ref, gain_ref, fixed_ref, scaled_ref, *rest
 ):
-    _, at_source, at_rank, at_order, _, _ = places(replicas, slots, live_ref.shape[0])
+    count = live_ref.shape[0]
+    _, at_source, at_rank, at_order, at_ends, _ = places(replicas, slots, count)
     arrived = dict(zip(members, rest[: len(members)]))
-    out_ref, buffer, sems = rest[len(members) + phase :]
-    i = pl.program_id(0)
-    first, last = span(replicas, slots, live_ref.shape[0], phase, plan_ref)
-    total = last - first
-
-    def fetch(at, slot):
-        request = plan_ref[at_order + first + at]
+    out_ref, ready, sem = rest[len(members) + chained :]
+    positions, channels = fixed_ref.shape[1:]
+    first = plan_ref[at_ends + members[0] - 1] if members[0] else 0
+    last = plan_ref[at_ends + members[-1]]
+
+    def copy(i):
+        request = plan_ref[at_order + i]
+        return pltpu.make_async_copy(ready.at[request], out_ref.at[request], sem)
+
+    def finish(i, carry):
+        request = plan_ref[at_order + i]
+        alive = lax.broadcasted_iota(jnp.int32, (positions, 1), 0) < live_ref[request]
         for known in members:
 
             @pl.when(plan_ref[at_source + request] == known)
             def _(known=known):
-                pltpu.make_async_copy(
-                    arrived[known].at[plan_ref[at_rank + request]], buffer.at[slot], sems.at[slot]
-                ).start()
-
-    @pl.when((i == 0) & (total > 0))
-    def _():
-        fetch(i, 0)
-
-    @pl.when(i + 1 < total)
-    def _():
-        fetch(i + 1, lax.rem(i + 1, 2))
-
-    @pl.when(i < total)
-    def _():
-        now = lax.rem(i, 2)
-        pltpu.make_async_copy(buffer.at[now], buffer.at[now], sems.at[now]).wait()
-        positions, channels = fixed_ref.shape[1:]
-        live = live_ref[plan_ref[at_order + first + i]]
-        gated = fixed_ref[0] + scaled_ref[0] * buffer[now].astype(jnp.float32)
-        square = jnp.sum(gated * gated, axis=1, keepdims=True) * (1.0 / channels)
-        alive = lax.broadcasted_iota(jnp.int32, (positions, 1), 0) < live
-        factor = lax.rsqrt(square + 1e-05)
-        out_ref[0] = jnp.where(alive, gated * factor * gain_ref[...], 0.0).astype(out_ref.dtype)
-
-    if phase:
-
-        @pl.when((i == 0) & (total == 0))
-        def _():
-            last = plan_ref[at_order + live_ref.shape[0] - 1]
-            keep = pltpu.make_async_copy(rest[len(members)].at[last], out_ref.at[0], sems.at[0])
-            keep.start()
-            keep.wait()
+                carried = arrived[known][plan_ref[at_rank + request]].astype(jnp.float32)
+                gated = fixed_ref[request] + scaled_ref[request] * carried
+                square = jnp.sum(gated * gated, axis=1, keepdims=True) * (1.0 / channels)
+                factor = jnp.where(alive, lax.rsqrt(square + 1e-05), 0.0)
+                ready[request] = (gated * factor * gain_ref[...]).astype(out_ref.dtype)
+
+        copy(i).start()
+        return carry
+
+    lax.fori_loop(first, last, finish, 0)
+
+    def wait(i, carry):
+        copy(i).wait()
+        return carry
+
+    lax.fori_loop(first, last, wait, 0)
 
 
 def per_device(
@@ -382,79 +402,66 @@
     me = myself.reshape(1)
     holder_row = holder.T
     page_rows = page_ids.T
+    def exchange(x, step):
+        return lax.ppermute(x, "replica", [(i, i ^ step) for i in range(replicas)])
+
+    at_state, at_source, at_rank, at_order, at_ends, at_me = places(replicas, slots, count)
     routed = pl.pallas_call(
         functools.partial(route_kernel, replicas, slots, count, most, page_len),
-        out_shape=[shape((slots, 2, most * page_len, row_width), bf16)] * (replicas - 1)
-        + [shape((1,), jnp.int32)],
-        in_specs=[SMEM] * 3 + [ANY] * 2,
-        out_specs=[ANY] * (replicas - 1) + [SMEM],
+        out_shape=[shape((slots, positions, STATE), bf16)] * (replicas - 1)
+        + [shape((slots, 2, most * page_len, row_width), bf16)] * (replicas - 1)
+        + [shape((at_me + 1,), jnp.int32)],
+        in_specs=[SMEM] * 4 + [ANY] * 3,
+        out_specs=[ANY] * (2 * replicas - 2) + [SMEM],
         scratch_shapes=[
             pltpu.VMEM(page_keys.shape, bf16),
             pltpu.VMEM(page_values.shape, bf16),
             pltpu.VMEM((replicas - 1, slots, 2, most * page_len, row_width), bf16),
-            pltpu.SemaphoreType.DMA((replicas + 1,)),
-        ],
-        compiler_params=PARAMS,
-        name="route",
-    )(me, holder_row, page_rows, page_keys, page_values)
-    send_pages = dict(zip(steps, routed[: replicas - 1]))
-
-    def exchange(x, step):
-        return lax.ppermute(x, "replica", [(i, i ^ step) for i in range(replicas)])
-
-    pages = {s: exchange(send_pages[s], s) for s in steps}
-
-    at_state, at_source, at_rank, at_order, at_ends, at_me = places(replicas, slots, count)
-    planned = pl.pallas_call(
-        functools.partial(plan_kernel, replicas, slots, count),
-        out_shape=[shape((slots, positions, STATE), bf16)] * (replicas - 1)
-        + [shape((at_me + 1,), jnp.int32)],
-        in_specs=[SMEM] * 4 + [ANY],
-        out_specs=[ANY] * (replicas - 1) + [SMEM],
-        scratch_shapes=[
             pltpu.SMEM((replicas,), jnp.int32),
             pltpu.VMEM(read_map.shape, bf16),
-            pltpu.SemaphoreType.DMA((2,)),
+            pltpu.SemaphoreType.DMA((replicas + 3,)),
         ],
-        compiler_params=PARAMS,
-        name="plan",
-    )(me, routed[-1], holder_row, cache_slot, read_map)
-    plan = planned[-1]
-    reads = {s: exchange(x, s) for s, x in zip(steps, planned[:-1])}
+        compiler_params=WIDE,
+        name="route",
+    )(me, holder_row, cache_slot, page_rows, page_keys, page_values, read_map)
+    reads = {s: exchange(x, s) for s, x in zip(steps, routed[: replicas - 1])}
     reads[0] = read_map
+    pages = {s: exchange(x, s) for s, x in zip(steps, routed[replicas - 1 : -1])}
+    plan = routed[-1]
 
     states = cache_states.reshape(cache_states.shape[0], channels, STATE)
     carried = {}
-    for s in steps + [0]:
-        carried[s] = pl.pallas_call(
-            carried_kernel,
-            out_shape=shape((slots, positions, channels), bf16),
+    token = []
+    half = max(1, replicas // 2)
+    for served in (steps + [0],):
+        results = pl.pallas_call(
+            functools.partial(carried_kernel, replicas, slots, count, served),
+            out_shape=[shape((slots, positions, channels), bf16)] * len(served),
             grid_spec=pltpu.PrefetchScalarGridSpec(
                 num_scalar_prefetch=1,
-                grid=(slots,),
-                in_specs=[
-                    pl.BlockSpec(
-                        (1, positions, STATE),
-                        (lambda i, plan: (i, 0, 0)) if s else (lambda i, plan: (plan[at_order + i], 0, 0)),
-                    ),
-                    pl.BlockSpec(
-                        (1, channels, STATE), lambda i, plan, s=s: (plan[at_state + s * slots + i], 0, 0)
-                    ),
+                grid=(1,),
+                in_specs=[ANY] * (len(served) + 1 + len(token)),
+                out_specs=[pl.BlockSpec((slots, positions, channels), lambda i, plan: (0, 0, 0))] * len(served),
+                scratch_shapes=[
+                    pltpu.VMEM((len(served), slots, positions, STATE), bf16),
+                    pltpu.VMEM((len(served), channels, slots * STATE), bf16),
+                    pltpu.SemaphoreType.DMA((len(served), 2 * slots)),
                 ],
-                out_specs=pl.BlockSpec((1, positions, channels), lambda i, plan: (i, 0, 0)),
             ),
-            compiler_params=PARAMS,
+            compiler_params=WIDE,
             cost_estimate=pl.CostEstimate(
-                flops=2 * slots * positions * channels * STATE,
-                bytes_accessed=2 * slots * channels * (STATE + positions),
+                flops=64 * len(served) * slots * positions * channels * STATE,
+                bytes_accessed=2 * len(served) * slots * channels * (STATE + positions),
                 transcendentals=0,
             ),
             name="carried",
-        )(plan, reads[s], states)
-        if s:
-            carried[s] = exchange(carried[s], s)
+        )(plan, *[reads[s] for s in served], states, *token)
+        token = [results[0]]
+        for s, x in zip(served, results):
+            carried[s] = exchange(x, s) if s else x
 
     spread = (jnp.arange(2 * heads)[:, None] % heads == jnp.arange(channels)[None, :] // width).astype(bf16)
+    skip_wide = jnp.repeat(skip_gain, width).reshape(1, channels)
     row = lambda i: (i, 0, 0)
     whole = lambda i: (0, 0)
     fixed, scaled = pl.pallas_call(
@@ -481,7 +488,7 @@
         name="within",
     )(
         log_rates.reshape(1, heads),
-        jnp.repeat(skip_gain, width).reshape(1, channels),
+        skip_wide,
         spread,
         step_sizes,
         read_map,
@@ -530,40 +537,21 @@
     )
 
     mamba_output = None
-    early = steps[replicas // 2 :] + [0]
-    late = steps[: replicas // 2]
-    for phase, members in enumerate([early, late]):
-
-        def place(i, plan, live, phase=phase):
-            first, last = span(replicas, slots, count, phase, plan)
-            at = jnp.minimum(first + i, jnp.maximum(last - 1, 0))
-            return (plan[at_order + at], 0, 0)
-
+    for members in (list(range(half)), list(range(half, replicas))):
+        chained = 0 if mamba_output is None else 1
         mamba_output = pl.pallas_call(
-            functools.partial(finish_kernel, replicas, slots, members, phase),
+            functools.partial(finish_kernel, replicas, slots, members, chained),
             out_shape=shape((count, positions, channels), bf16),
-            grid_spec=pltpu.PrefetchScalarGridSpec(
-                num_scalar_prefetch=2,
-                grid=(min(count, slots * len(members)),),
-                in_specs=[
-                    pl.BlockSpec((1, channels), lambda i, *refs: (0, 0)),
-                    pl.BlockSpec((1, positions, channels), place),
-                    pl.BlockSpec((1, positions, channels), place),
-                ]
-                + [ANY] * (len(members) + phase),
-                out_specs=pl.BlockSpec((1, positions, channels), place),
-                scratch_shapes=[
-                    pltpu.VMEM((2, positions, channels), bf16),
-                    pltpu.SemaphoreType.DMA((2,)),
-                ],
-            ),
-            input_output_aliases={5 + len(members): 0} if phase else {},
+            in_specs=[SMEM] * 2 + [VMEM] * (3 + len(members)) + [ANY] * chained,
+            out_specs=ANY,
+            scratch_shapes=[pltpu.VMEM((count, positions, channels), bf16), pltpu.SemaphoreType.DMA],
+            input_output_aliases={5 + len(members): 0} if chained else {},
+            compiler_params=PARAMS,
             cost_estimate=pl.CostEstimate(
-                flops=6 * count * positions * channels,
-                bytes_accessed=count * positions * channels * 6,
+                flops=len(members) * slots * positions * channels * 8,
+                bytes_accessed=len(members) * slots * positions * channels * 12,
                 transcendentals=0,
             ),
-            compiler_params=PARAMS,
             name="finish",
         )(
             plan,
@@ -572,7 +560,7 @@
             fixed,
             scaled,
             *[carried[s] for s in members],
-            *([mamba_output] if phase else []),
+            *([mamba_output] if chained else []),
         )
     return (mamba_output, attention_output)
 

time: 92.4 us -> 81.1 us (0.88)
  Pallas kernels: 61 us -> 32.9 us
  waiting for transfers between devices: 0.02 us -> 28 us
  starting transfers between devices: 23.3 us -> 14.6 us
  local copies, waits for them, and re-layouts: 5.19 us -> 4.2 us
    ppermute x9, waiting for transfers between devices: 0.02 us -> 28 us  [exchange(): return lax.ppermute(x, 'replica', [(i, i ^ step) for i in range(replicas)])]
    pallas_call x5 -> x1, Pallas kernels: 19.7 us -> 6.37 us  [per_device(): pl.pallas_call(functools.partial(carried_kernel, replicas, slots, count,...]
    pallas_call x2, Pallas kernels: 13.4 us -> 4.3 us  [per_device(): pl.pallas_call(functools.partial(finish_kernel, replicas, slots, members,...]
    ppermute x9, starting transfers between devices: 23.3 us -> 14.6 us  [exchange(): return lax.ppermute(x, 'replica', [(i, i ^ step) for i in range(replicas)])]
    pallas_call x1, Pallas kernels: 11.7 us -> 7.5 us  [per_device(): pl.pallas_call(within_kernel, out_shape=[shape((count, positions, channel...]
    pallas_call x1, Pallas kernels: 12.4 us -> 10.8 us  [per_device(): pl.pallas_call(functools.partial(attention_kernel, replicas, kv_here, per...]
    unnamed x20 -> x40, local copies, waits for them, and re-layouts: 3.78 us -> 3.39 us
  transfers between devices with their start and end apart: 9 -> 9, of which waited for: 0 -> 2; matrix products, arithmetic and copies ran while one was open for 2% -> 1% of each run, Pallas kernels for 55% -> 33%
where the time goes in v3:
time: 81.1 us; the launch traced here: 80.7 us
  Pallas kernels  32.9 us (41%)
  waiting for transfers between devices  28 us (35%)
  starting transfers between devices  14.6 us (18%)
  local copies, waits for them, and re-layouts  4.2 us (5%)
  between operations  0.92 us (1%)
    ppermute x9, waiting for transfers between devices, exchange(): return lax.ppermute(x, 'replica', [(i, i ^ step) for i in range(replicas)])  28 us
    ppermute x9, starting transfers between devices, exchange(): return lax.ppermute(x, 'replica', [(i, i ^ step) for i in range(replicas)])  14.6 us
    pallas_call x1, Pallas kernels, per_device(): pl.pallas_call(functools.partial(attention_kernel, replicas, kv_here, per...  10.8 us
    pallas_call x1, Pallas kernels, per_device(): pl.pallas_call(within_kernel, out_shape=[shape((count, positions, channel...  7.5 us
    pallas_call x1, Pallas kernels, per_device(): pl.pallas_call(functools.partial(carried_kernel, replicas, slots, count,...  6.37 us
    pallas_call x2, Pallas kernels, per_device(): pl.pallas_call(functools.partial(finish_kernel, replicas, slots, members,...  4.3 us
    pallas_call x1, Pallas kernels, per_device(): pl.pallas_call(functools.partial(route_kernel, replicas, slots, count, mo...  3.85 us
    unnamed x40, local copies, waits for them, and re-layouts  3.39 us
  transfers between devices with their start and end apart: 9, of which 2 were waited for; matrix products, arithmetic and copies ran while one was open for 1% of the time, Pallas kernels for 33%

profile of v3, /device:TPU:0, one launch (start us, length us, event | category | flops | bytes accessed | tf_op | source)
XLA Modules:
  0.0 80.7 jit_solution(18086127613409451082)
XLA Ops:
  0.6 3.9 %route.1 = (bf16[3,32,128]{2,1,0:T(8,128)(2,1)}, bf16[3,32,128]{2,1,0:T(8,128)(2,1)}, bf16[3,32,128]{2,1,0:T(8,128)(2,1)}, bf16[3,2,128,256]{3,2,1,0:T(8,128)(2,...) custom-call(s32[1]{0:T(128)} %bitcast.me_ref, s32[1,44]{1,0:T(1,128)} %bitcast.11, ...), custom_call_target="tpu_custom_call" | custom-call | tf_op jit(solution)/shard_map/route/pallas_call | solution.py:409
  4.5 5.1 %collective-permute-start = (bf16[3,32,128]{2,1,0:T(8,128)(2,1)}, bf16[3,32,128]{2,1,0:T(8,128)(2,1)S(1)}, u32[]{:S(2)}, u32[]{:S(2)}) collective-permute-start(bf16[3,32,128]{2,1,0:T(8,128)(2,1)} %get-tuple-element.18), channel_id=1, source_target_pairs={{0,12},{4,8},{8,4},{12,0},{1,13},{5,9},{9,5},{13,1},{2,14},{6,10},... | collective-permute-start | bytes 73736 | tf_op jit(solution)/shard_map/ppermute | solution.py:406
  9.6 0.0 collective-permute-start.1
  9.6 0.6 collective-permute-start.2
  10.2 3.7 %collective-permute-start.6 = (bf16[3,2,128,256]{3,2,1,0:T(8,128)(2,1)}, bf16[3,2,128,256]{3,2,1,0:T(8,128)(2,1)S(1)}, u32[]{:S(2)}, u32[]{:S(2)}) collective-permute-start(bf16[3,2,128,256]{3,2,1,0:T(8,128)(2,1)} %get-tuple-element.25), channel_id=1, source_target_pairs={{0,12},{4,8},{8,4},{12,0},{1,13},{5,9},{9,5},{13,1},{2,14},{6,10},... | collective-permute-start | bytes 1179656 | tf_op jit(solution)/shard_map/ppermute | solution.py:406
  13.9 0.0 collective-permute-start.7
  14.0 0.7 broadcast_in_dim.2
  14.7 0.1 reshape_reshape.3.skip_ref
  14.8 0.0 collective-permute-done.rest_0_
  14.8 0.0 copy-start.17
  14.8 0.7 collective-permute-start.8
  15.5 14.7 %collective-permute-done.1.rest_1_ = bf16[3,32,128]{2,1,0:T(8,128)(2,1)S(1)} collective-permute-done((bf16[3,32,128]{2,1,0:T(8,128)(2,1)}, bf16[3,32,128]{2,1,0:T(8,128)(2,1)S(1)}, u32[]{:S(2)}, u32[]{:S(2)}) %collective-permute-start.1) | collective-permute-done | bytes 24608 | tf_op jit(solution)/shard_map/ppermute | solution.py:406
  30.2 0.0 collective-permute-done.2.rest_2_
  30.2 0.6 copy-done.18
  30.8 0.0 copy-done.19
  30.8 0.0 copy-done.17
  30.8 6.4 %carried.1 = (bf16[3,32,2048]{2,1,0:T(8,128)(2,1)}, bf16[3,32,2048]{2,1,0:T(8,128)(2,1)}, bf16[3,32,2048]{2,1,0:T(8,128)(2,1)}, bf16[3,32,2048]{2,1,0:T(8,128)(2,1)}) custom-call(s32[50]{0:T(128)} %get-tuple-element.15.plan_ref, bf16[3,32,128]{2,1,0:T(8,128)(2,1)} %copy-done.17, bf16[3,32,128]{2,1,0:T(8,128)(2,1)} %copy-done.18, ...), custom_call_target="tpu_custom_call" | custom-call | flops 6442450944 | bytes 7864320 | tf_op jit(solution)/shard_map/carried/pallas_call | solution.py:437
  37.2 0.1 collective-permute-start.5
  37.3 0.1 collective-permute-start.3
  37.4 0.0 collective-permute-done.6.rest_0_
  37.4 4.3 %collective-permute-start.4 = (bf16[3,32,2048]{2,1,0:T(8,128)(2,1)}, bf16[3,32,2048]{2,1,0:T(8,128)(2,1)S(1)}, u32[]{:S(2)}, u32[]{:S(2)}) collective-permute-start(bf16[3,32,2048]{2,1,0:T(8,128)(2,1)} %get-tuple-element.22), channel_id=1, source_target_pairs={{0,12},{4,8},{8,4},{12,0},{1,13},{5,9},{9,5},{13,1},{2,14},{6,10},... | collective-permute-start | bytes 1179656 | tf_op jit(solution)/shard_map/ppermute | solution.py:406
  41.7 0.1 compare_convert_fusion.spread_ref
  41.8 0.0 copy-done.2
  41.8 0.0 copy-done.3
  41.8 0.0 copy-done.15
  41.8 0.0 copy-start.6
  41.8 0.9 %copy-done.6 = bf16[11,32,128]{2,1,0:T(8,128)(2,1)S(1)} copy-done((bf16[11,32,128]{2,1,0:T(8,128)(2,1)S(1)}, bf16[11,32,128]{2,1,0:T(8,128)(2,1)}, u32[]{:S(2)}) %copy-start.6) | copy-done | bytes 90136
  42.7 0.9 %copy-done.7 = f32[11,32,32]{2,1,0:T(8,128)S(1)} copy-done((f32[11,32,32]{2,1,0:T(8,128)S(1)}, f32[11,32,32]{2,1,0:T(8,128)}, u32[]{:S(2)}) %copy-start.7) | copy-done | bytes 45080
  43.6 0.9 %copy-done.10 = bf16[11,32,128]{2,1,0:T(8,128)(2,1)S(1)} copy-done((bf16[11,32,128]{2,1,0:T(8,128)(2,1)S(1)}, bf16[11,32,128]{2,1,0:T(8,128)(2,1)}, u32[]{:S(2)}) %copy-start.10) | copy-done | bytes 90136
  44.5 0.0 copy-start.9
  44.5 0.0 copy-start.12
  44.5 0.0 copy-start.13
  44.6 0.0 copy-start.14
  44.6 0.0 copy-start.16
  44.6 7.5 %within.1 = (f32[11,32,2048]{2,1,0:T(8,128)S(1)}, f32[11,32,2048]{2,1,0:T(8,128)S(1)}) custom-call(f32[1,32]{1,0:T(1,128)S(1)} %bitcast.10, f32[1,2048]{1,0:T(1,128)S(1)} %reshape_reshape.3.skip_ref, bf16[64,2048]{1,0:T(8,128)(2,1)S(1)} %compare_convert_fusion.spread_ref, f32[11,32,32]{2,1,0:T(8,128)S(1)} %copy-done.7, bf16[11,32,128]{2,1,0:T(8,128)(2,1)S(1)} %copy-done.6, ...), custom_call_target="tpu_custom_call" | custom-call | flops 369098752 | bytes 8650752 | tf_op jit(solution)/shard_map/within/pallas_call | solution.py:467
  52.1 0.0 copy-start.5
  52.1 0.0 copy-start.11
  52.1 13.3 %collective-permute-done.7.rest_1_ = bf16[3,2,128,256]{3,2,1,0:T(8,128)(2,1)S(1)} collective-permute-done((bf16[3,2,128,256]{3,2,1,0:T(8,128)(2,1)}, bf16[3,2,128,256]{3,2,1,0:T(8,128)(2,1)S(1)}, u32[]{:S(2)}, u32[]{:S(2)}) %collective-permute-start.7) | collective-permute-done | bytes 393248 | tf_op jit(solution)/shard_map/ppermute | solution.py:406
  65.4 0.0 collective-permute-done.8.rest_2_
  65.4 0.0 copy-done
  65.5 10.8 %attention.1 = bf16[11,32,2048]{2,1,0:T(8,128)(2,1)} custom-call(s32[50]{0:T(128)S(1)} %copy-done.14, s32[11]{0:T(128)S(1)} %copy-done.16, s32[11]{0:T(128)S(1)} %copy-done.13, s32[8,44]{1,0:T(8,128)S(1)} %bitcast.9, bf16[11,32,2048]{2,1,0:T(8,128)(2,1)S(1)} %copy-done.4, bf16[11,32,256]{2,1,0:T(8,128)(2,1)S(1)} %copy-done.8, ...), custom_call_target="tpu_custom_call" | custom-call | flops 461373440 | bytes 4325376 | tf_op jit(solution)/shard_map/attention/pallas_call | solution.py:501
  76.3 0.0 collective-permute-done.5.rest_1_
  76.3 0.0 copy-done.5
  76.4 0.0 copy-done.11
  76.4 2.2 %finish.2.rest_2_ = bf16[11,32,2048]{2,1,0:T(8,128)(2,1)} custom-call(s32[50]{0:T(128)S(1)} %copy-done.14, s32[11]{0:T(128)S(1)} %copy-done.13, f32[1,2048]{1,0:T(1,128)S(1)} %bitcast.6, f32[11,32,2048]{2,1,0:T(8,128)S(1)} %get-tuple-element.16.fixed_ref, f32[11,32,2048]{2,1,0:T(8,128)S(1)} %get-tuple-element.17.scaled_ref, ...), custom_call_target="tpu_custom_call" | custom-call | flops 3145728 | bytes 4718592 | tf_op jit(solution)/shard_map/finish/pallas_call | solution.py:542
  78.6 0.0 collective-permute-done.3.rest_0_
  78.6 0.0 collective-permute-done.4.rest_1_
  78.6 2.1 %finish.3 = bf16[11,32,2048]{2,1,0:T(8,128)(2,1)} custom-call(s32[50]{0:T(128)S(1)} %copy-done.14, s32[11]{0:T(128)S(1)} %copy-done.13, f32[1,2048]{1,0:T(1,128)S(1)} %bitcast.7, f32[11,32,2048]{2,1,0:T(8,128)S(1)} %get-tuple-element.16.fixed_ref, f32[11,32,2048]{2,1,0:T(8,128)S(1)} %get-tuple-element.17.scaled_ref, ...), custom_call_target="tpu_custom_call", output_to_operand_aliasing={{}: (7, {})} | custom-call | flops 3145728 | bytes 4718592 | tf_op jit(solution)/shard_map/finish/pallas_call | solution.py:542
  (21 shorter events, 0.0 us)
Async XLA Ops:
  4.5 10.3 %collective-permute-start = (bf16[3,32,128]{2,1,0:T(8,128)(2,1)}, bf16[3,32,128]{2,1,0:T(8,128)(2,1)S(1)}, u32[]{:S(2)}, u32[]{:S(2)}) collective-permute-start(bf16[3,32,128]{2,1,0:T(8,128)(2,1)} %get-tuple-element.18), channel_id=1, source_target_pairs={{0,12},{4,8},{8,4},{12,0},{1,13},{5,9},{9,5},{13,1},{2,14},{6,10},... | collective-permute-start | bytes 73736 | tf_op jit(solution)/shard_map/ppermute | solution.py:406
  9.6 20.6 %collective-permute-start.1 = (bf16[3,32,128]{2,1,0:T(8,128)(2,1)}, bf16[3,32,128]{2,1,0:T(8,128)(2,1)S(1)}, u32[]{:S(2)}, u32[]{:S(2)}) collective-permute-start(bf16[3,32,128]{2,1,0:T(8,128)(2,1)} %get-tuple-element.19), channel_id=1, source_target_pairs={{0,8},{4,12},{8,0},{12,4},{1,9},{5,13},{9,1},{13,5},{2,10},{6,14},... | collective-permute-start | bytes 73736 | tf_op jit(solution)/shard_map/ppermute | solution.py:406
  9.6 20.6 %collective-permute-start.2 = (bf16[3,32,128]{2,1,0:T(8,128)(2,1)}, bf16[3,32,128]{2,1,0:T(8,128)(2,1)S(1)}, u32[]{:S(2)}, u32[]{:S(2)}) collective-permute-start(bf16[3,32,128]{2,1,0:T(8,128)(2,1)} %get-tuple-element.20), channel_id=1, source_target_pairs={{0,4},{4,0},{8,12},{12,8},{1,5},{5,1},{9,13},{13,9},{2,6},{6,2},{1... | collective-permute-start | bytes 73736 | tf_op jit(solution)/shard_map/ppermute | solution.py:406
  10.2 27.2 %collective-permute-start.6 = (bf16[3,2,128,256]{3,2,1,0:T(8,128)(2,1)}, bf16[3,2,128,256]{3,2,1,0:T(8,128)(2,1)S(1)}, u32[]{:S(2)}, u32[]{:S(2)}) collective-permute-start(bf16[3,2,128,256]{3,2,1,0:T(8,128)(2,1)} %get-tuple-element.25), channel_id=1, source_target_pairs={{0,12},{4,8},{8,4},{12,0},{1,13},{5,9},{9,5},{13,1},{2,14},{6,10},... | collective-permute-start | bytes 1179656 | tf_op jit(solution)/shard_map/ppermute | solution.py:406
  13.9 51.5 %collective-permute-start.7 = (bf16[3,2,128,256]{3,2,1,0:T(8,128)(2,1)}, bf16[3,2,128,256]{3,2,1,0:T(8,128)(2,1)S(1)}, u32[]{:S(2)}, u32[]{:S(2)}) collective-permute-start(bf16[3,2,128,256]{3,2,1,0:T(8,128)(2,1)} %get-tuple-element.26), channel_id=1, source_target_pairs={{0,8},{4,12},{8,0},{12,4},{1,9},{5,13},{9,1},{13,5},{2,10},{6,14},... | collective-permute-start | bytes 1179656 | tf_op jit(solution)/shard_map/ppermute | solution.py:406
  14.8 16.0 %copy-start.17 = (bf16[3,32,128]{2,1,0:T(8,128)(2,1)}, bf16[3,32,128]{2,1,0:T(8,128)(2,1)S(1)}, u32[]{:S(2)}) copy-start(bf16[3,32,128]{2,1,0:T(8,128)(2,1)S(1)} %collective-permute-done.rest_0_) | copy-start | bytes 73732
  14.8 50.6 %collective-permute-start.8 = (bf16[3,2,128,256]{3,2,1,0:T(8,128)(2,1)}, bf16[3,2,128,256]{3,2,1,0:T(8,128)(2,1)S(1)}, u32[]{:S(2)}, u32[]{:S(2)}) collective-permute-start(bf16[3,2,128,256]{3,2,1,0:T(8,128)(2,1)} %get-tuple-element.27), channel_id=1, source_target_pairs={{0,4},{4,0},{8,12},{12,8},{1,5},{5,1},{9,13},{13,9},{2,6},{6,2},{1... | collective-permute-start | bytes 1179656 | tf_op jit(solution)/shard_map/ppermute | solution.py:406
  30.2 0.6 copy-start.18
  30.2 0.6 copy-start.19
  30.8 11.0 %copy-start.2 = (bf16[11,32,2048]{2,1,0:T(8,128)(2,1)S(1)}, bf16[11,32,2048]{2,1,0:T(8,128)(2,1)}, u32[]{:S(2)}) copy-start(bf16[11,32,2048]{2,1,0:T(8,128)(2,1)} %input_ref.1) | copy-start | bytes 4325380
  30.8 11.0 %copy-start.3 = (bf16[11,32,2048]{2,1,0:T(8,128)(2,1)S(1)}, bf16[11,32,2048]{2,1,0:T(8,128)(2,1)}, u32[]{:S(2)}) copy-start(bf16[11,32,2048]{2,1,0:T(8,128)(2,1)} %gate_ref.1) | copy-start | bytes 4325380
  30.8 11.0 %copy-start.15 = (f32[32]{0:T(128)S(1)}, f32[32]{0:T(128)}, u32[]{:S(2)}) copy-start(f32[32]{0:T(128)} %param.29) | copy-start | bytes 388
  37.2 39.1 %collective-permute-start.5 = (bf16[3,32,2048]{2,1,0:T(8,128)(2,1)}, bf16[3,32,2048]{2,1,0:T(8,128)(2,1)S(1)}, u32[]{:S(2)}, u32[]{:S(2)}) collective-permute-start(bf16[3,32,2048]{2,1,0:T(8,128)(2,1)} %get-tuple-element.24), channel_id=1, source_target_pairs={{0,4},{4,0},{8,12},{12,8},{1,5},{5,1},{9,13},{13,9},{2,6},{6,2},{1... | collective-permute-start | bytes 1179656 | tf_op jit(solution)/shard_map/ppermute | solution.py:406
  37.3 41.3 %collective-permute-start.3 = (bf16[3,32,2048]{2,1,0:T(8,128)(2,1)}, bf16[3,32,2048]{2,1,0:T(8,128)(2,1)S(1)}, u32[]{:S(2)}, u32[]{:S(2)}) collective-permute-start(bf16[3,32,2048]{2,1,0:T(8,128)(2,1)} %get-tuple-element.21), channel_id=1, source_target_pairs={{0,8},{4,12},{8,0},{12,4},{1,9},{5,13},{9,1},{13,5},{2,10},{6,14},... | collective-permute-start | bytes 1179656 | tf_op jit(solution)/shard_map/ppermute | solution.py:406
  37.4 41.2 %collective-permute-start.4 = (bf16[3,32,2048]{2,1,0:T(8,128)(2,1)}, bf16[3,32,2048]{2,1,0:T(8,128)(2,1)S(1)}, u32[]{:S(2)}, u32[]{:S(2)}) collective-permute-start(bf16[3,32,2048]{2,1,0:T(8,128)(2,1)} %get-tuple-element.22), channel_id=1, source_target_pairs={{0,12},{4,8},{8,4},{12,0},{1,13},{5,9},{9,5},{13,1},{2,14},{6,10},... | collective-permute-start | bytes 1179656 | tf_op jit(solution)/shard_map/ppermute | solution.py:406
  41.8 0.9 %copy-start.6 = (bf16[11,32,128]{2,1,0:T(8,128)(2,1)S(1)}, bf16[11,32,128]{2,1,0:T(8,128)(2,1)}, u32[]{:S(2)}) copy-start(bf16[11,32,128]{2,1,0:T(8,128)(2,1)} %rest_3_.2) | copy-start | bytes 270340
  42.7 0.9 %copy-start.7 = (f32[11,32,32]{2,1,0:T(8,128)S(1)}, f32[11,32,32]{2,1,0:T(8,128)}, u32[]{:S(2)}) copy-start(f32[11,32,32]{2,1,0:T(8,128)} %step_ref.1) | copy-start | bytes 135172
  43.6 0.9 %copy-start.10 = (bf16[11,32,128]{2,1,0:T(8,128)(2,1)S(1)}, bf16[11,32,128]{2,1,0:T(8,128)(2,1)}, u32[]{:S(2)}) copy-start(bf16[11,32,128]{2,1,0:T(8,128)(2,1)} %write_ref.1) | copy-start | bytes 270340
  44.5 20.9 %copy-start = (bf16[48,16,256]{2,1,0:T(8,128)(2,1)S(1)}, bf16[48,16,256]{2,1,0:T(8,128)(2,1)}, u32[]{:S(2)}) copy-start(bf16[48,16,256]{2,1,0:T(8,128)(2,1)} %rest_3_.3) | copy-start | bytes 1179652
  44.5 20.9 %copy-start.1 = (bf16[48,16,256]{2,1,0:T(8,128)(2,1)S(1)}, bf16[48,16,256]{2,1,0:T(8,128)(2,1)}, u32[]{:S(2)}) copy-start(bf16[48,16,256]{2,1,0:T(8,128)(2,1)} %rest_4_.1) | copy-start | bytes 1179652
  44.5 20.9 %copy-start.4 = (bf16[11,32,2048]{2,1,0:T(8,128)(2,1)S(1)}, bf16[11,32,2048]{2,1,0:T(8,128)(2,1)}, u32[]{:S(2)}) copy-start(bf16[11,32,2048]{2,1,0:T(8,128)(2,1)} %query_ref.1) | copy-start | bytes 4325380
  44.5 20.9 %copy-start.8 = (bf16[11,32,256]{2,1,0:T(8,128)(2,1)S(1)}, bf16[11,32,256]{2,1,0:T(8,128)(2,1)}, u32[]{:S(2)}) copy-start(bf16[11,32,256]{2,1,0:T(8,128)(2,1)} %key_ref.1) | copy-start | bytes 540676
  44.5 20.9 %copy-start.9 = (bf16[11,32,256]{2,1,0:T(8,128)(2,1)S(1)}, bf16[11,32,256]{2,1,0:T(8,128)(2,1)}, u32[]{:S(2)}) copy-start(bf16[11,32,256]{2,1,0:T(8,128)(2,1)} %value_ref.1) | copy-start | bytes 540676
  44.5 20.9 %copy-start.12 = (s32[44,8]{0,1:T(8,128)S(1)}, s32[44,8]{0,1:T(8,128)}, u32[]{:S(2)}) copy-start(s32[44,8]{0,1:T(8,128)} %param.22) | copy-start | bytes 4228
  44.5 20.9 %copy-start.13 = (s32[11]{0:T(128)S(1)}, s32[11]{0:T(128)}, u32[]{:S(2)}) copy-start(s32[11]{0:T(128)} %live_ref.5) | copy-start | bytes 136
  44.6 20.9 %copy-start.14 = (s32[50]{0:T(128)S(1)}, s32[50]{0:T(128)}, u32[]{:S(2)}) copy-start(s32[50]{0:T(128)} %get-tuple-element.15.plan_ref) | copy-start | bytes 604
  44.6 20.9 %copy-start.16 = (s32[11]{0:T(128)S(1)}, s32[11]{0:T(128)}, u32[]{:S(2)}) copy-start(s32[11]{0:T(128)} %count_ref.1) | copy-start | bytes 136
  52.1 24.3 %copy-start.5 = (bf16[3,32,2048]{2,1,0:T(8,128)(2,1)S(1)}, bf16[3,32,2048]{2,1,0:T(8,128)(2,1)}, u32[]{:S(2)}) copy-start(bf16[3,32,2048]{2,1,0:T(8,128)(2,1)} %get-tuple-element.23.rest_0_) | copy-start | bytes 1179652
  52.1 24.3 %copy-start.11 = (f32[2048]{0:T(1024)S(1)}, f32[2048]{0:T(1024)}, u32[]{:S(2)}) copy-start(f32[2048]{0:T(1024)} %param.34) | copy-start | bytes 24580

commit v4 on v3

--- a/solution.py
+++ b/solution.py
@@ -32,15 +32,50 @@
     return state, source, rank, order, ends, ends + replicas
 
 
-def route_kernel(
+def pack_pages(replicas, slots, count, most, page_len, steps, me, holder_ref, pages_ref, pools, packed, outs, sems):
+    keys, values = pools
+    copies = []
+    for at, step in enumerate(steps):
+        first = lax.bitwise_xor(me, step) * count
+
+        def serve(j, rank_here, at=at, first=first):
+            request = first + j
+            hit = holder_ref[0, request] == me
+
+            @pl.when(hit)
+            def _():
+                slot = jnp.minimum(rank_here, slots - 1)
+                for place in range(most):
+                    page = pages_ref[place, request]
+                    rows = slice(place * page_len, (place + 1) * page_len)
+                    packed[at, slot, 0, rows, :] = keys[page]
+                    packed[at, slot, 1, rows, :] = values[page]
+
+            return rank_here + hit.astype(jnp.int32)
+
+        lax.fori_loop(0, count, serve, jnp.int32(0))
+        copies.append(pltpu.make_async_copy(packed.at[at], outs[at], sems.at[at]))
+        copies[-1].start()
+    return copies
+
+
+def clear(ref, length):
+    def body(i, carry):
+        ref[i] = 0
+        return carry
+
+    lax.fori_loop(0, length, body, 0)
+
+
+def first_kernel(
     replicas,
     slots,
     count,
     most,
     page_len,
+    far,
     me_ref,
     holder_ref,
-    slot_ref,
     pages_ref,
     keys_hbm,
     values_hbm,
@@ -48,12 +83,65 @@
     *rest,
 ):
     steps = partner_steps(replicas)
-    read_out = dict(zip(steps, rest[: replicas - 1]))
-    page_out = dict(zip(steps, rest[replicas - 1 : 2 * replicas - 2]))
-    plan, keys, values, packed, seen, reads, sems = rest[2 * replicas - 2 :]
-    read_sem = sems.at[replicas + 1]
-    load_reads = pltpu.make_async_copy(reads_hbm, reads, sems.at[replicas + 2])
-    load_reads.start()
+    page_out, rest = rest[: len(far)], rest[len(far) :]
+    read_out, rest = dict(zip(steps, rest[: replicas - 1])), rest[replicas - 1 :]
+    keys, values, packed, seen, reads, sems, page_sems = rest
+    loads = [
+        pltpu.make_async_copy(keys_hbm, keys, sems.at[0]),
+        pltpu.make_async_copy(values_hbm, values, sems.at[1]),
+        pltpu.make_async_copy(reads_hbm, reads, sems.at[2]),
+    ]
+    for load in loads:
+        load.start()
+    me = me_ref[0]
+    clear(seen, replicas)
+    for load in loads:
+        load.wait()
+    copies = pack_pages(
+        replicas, slots, count, most, page_len, far, me, holder_ref, pages_ref, (keys, values), packed, page_out, page_sems
+    )
+
+    def ask(j, sent):
+        step = lax.bitwise_xor(me, holder_ref[0, me * count + j])
+        slot = jnp.minimum(seen[step], slots - 1)
+        seen[step] = slot + 1
+        for known in steps:
+
+            @pl.when(step == known)
+            def _(known=known):
+                pltpu.make_async_copy(reads.at[j], read_out[known].at[slot], sems.at[3]).start()
+
+        return sent + (step != 0).astype(jnp.int32)
+
+    sent = lax.fori_loop(0, count, ask, jnp.int32(0))
+
+    def wait_read(i, carry):
+        pltpu.make_async_copy(reads.at[0], read_out[steps[0]].at[0], sems.at[3]).wait()
+        return carry
+
+    lax.fori_loop(0, sent, wait_read, 0)
+    for copy in copies:
+        copy.wait()
+
+
+def second_kernel(
+    replicas,
+    slots,
+    count,
+    most,
+    page_len,
+    near,
+    waited,
+    me_ref,
+    holder_ref,
+    slot_ref,
+    pages_ref,
+    keys_hbm,
+    values_hbm,
+    *rest,
+):
+    page_out = rest[waited : waited + len(near)]
+    plan, keys, values, packed, seen, sems, page_sems = rest[waited + len(near) :]
     state, source, rank, order, ends, mine = places(replicas, slots, count)
     loads = [
         pltpu.make_async_copy(keys_hbm, keys, sems.at[0]),
@@ -63,19 +151,26 @@
         load.start()
     me = me_ref[0]
     plan[mine] = me
-
-    def clear(i, carry):
-        plan[state + i] = 0
-        return carry
-
-    lax.fori_loop(0, replicas * slots, clear, 0)
-
-    def clear_seen(i, carry):
-        seen[i] = 0
-        return carry
-
-    lax.fori_loop(0, replicas, clear_seen, 0)
-    load_reads.wait()
+    clear(plan, replicas * slots)
+    clear(seen, replicas)
+    for load in loads:
+        load.wait()
+    copies = pack_pages(
+        replicas, slots, count, most, page_len, near, me, holder_ref, pages_ref, (keys, values), packed, page_out, page_sems
+    )
+    for step in range(replicas):
+        first = lax.bitwise_xor(me, step) * count
+
+        def serve(j, rank_here, step=step, first=first):
+            hit = holder_ref[0, first + j] == me
+
+            @pl.when(hit)
+            def _():
+                plan[state + step * slots + jnp.minimum(rank_here, slots - 1)] = slot_ref[first + j]
+
+            return rank_here + hit.astype(jnp.int32)
+
+        lax.fori_loop(0, count, serve, jnp.int32(0))
 
     def ask(j, carry):
         step = lax.bitwise_xor(me, holder_ref[0, me * count + j])
@@ -83,43 +178,9 @@
         seen[step] = slot + 1
         plan[source + j] = step
         plan[rank + j] = slot
-        for known in steps:
-
-            @pl.when(step == known)
-            def _(known=known):
-                pltpu.make_async_copy(reads.at[j], read_out[known].at[slot], read_sem).start()
-
-        return carry + (step != 0).astype(jnp.int32)
-
-    asked = lax.fori_loop(0, count, ask, jnp.int32(0))
-    for load in loads:
-        load.wait()
-    copies = []
-    for at, step in enumerate(steps + [0]):
-        first = lax.bitwise_xor(me, step) * count
-
-        def serve(j, rank_here, at=at, step=step, first=first):
-            request = first + j
-            hit = holder_ref[0, request] == me
-
-            @pl.when(hit)
-            def _():
-                slot = jnp.minimum(rank_here, slots - 1)
-                plan[state + step * slots + slot] = slot_ref[request]
-                if step:
-                    for place in range(most):
-                        page = pages_ref[place, request]
-                        rows = slice(place * page_len, (place + 1) * page_len)
-                        packed[at, slot, 0, rows, :] = keys[page]
-                        packed[at, slot, 1, rows, :] = values[page]
-
-            return rank_here + hit.astype(jnp.int32)
-
-        lax.fori_loop(0, count, serve, jnp.int32(0))
-        if step:
-            copies.append(pltpu.make_async_copy(packed.at[at], page_out[step], sems.at[2 + at]))
-            copies[-1].start()
-
+        return carry
+
+    lax.fori_loop(0, count, ask, 0)
     place = jnp.int32(0)
     for step in range(replicas):
 
@@ -134,12 +195,6 @@
 
         place = lax.fori_loop(0, count, put, place)
         plan[ends + step] = place
-
-    def wait_read(i, carry):
-        pltpu.make_async_copy(reads.at[0], read_out[steps[0]].at[0], read_sem).wait()
-        return carry
-
-    lax.fori_loop(0, asked, wait_read, 0)
     for copy in copies:
         copy.wait()
 
@@ -406,28 +461,48 @@
         return lax.ppermute(x, "replica", [(i, i ^ step) for i in range(replicas)])
 
     at_state, at_source, at_rank, at_order, at_ends, at_me = places(replicas, slots, count)
-    routed = pl.pallas_call(
-        functools.partial(route_kernel, replicas, slots, count, most, page_len),
-        out_shape=[shape((slots, positions, STATE), bf16)] * (replicas - 1)
-        + [shape((slots, 2, most * page_len, row_width), bf16)] * (replicas - 1)
-        + [shape((at_me + 1,), jnp.int32)],
-        in_specs=[SMEM] * 4 + [ANY] * 3,
-        out_specs=[ANY] * (2 * replicas - 2) + [SMEM],
+    third = max(1, (replicas - 1) // 3)
+    far, near = steps[:third], steps[third:]
+    page_shape = shape((slots, 2, most * page_len, row_width), bf16)
+    first = pl.pallas_call(
+        functools.partial(first_kernel, replicas, slots, count, most, page_len, far),
+        out_shape=[page_shape] * len(far) + [shape((slots, positions, STATE), bf16)] * (replicas - 1),
+        in_specs=[SMEM] * 3 + [ANY] * 3,
+        out_specs=[ANY] * (len(far) + replicas - 1),
         scratch_shapes=[
             pltpu.VMEM(page_keys.shape, bf16),
             pltpu.VMEM(page_values.shape, bf16),
-            pltpu.VMEM((replicas - 1, slots, 2, most * page_len, row_width), bf16),
+            pltpu.VMEM((len(far), *page_shape.shape), bf16),
             pltpu.SMEM((replicas,), jnp.int32),
             pltpu.VMEM(read_map.shape, bf16),
-            pltpu.SemaphoreType.DMA((replicas + 3,)),
+            pltpu.SemaphoreType.DMA((4,)),
+            pltpu.SemaphoreType.DMA((len(far),)),
         ],
         compiler_params=WIDE,
-        name="route",
-    )(me, holder_row, cache_slot, page_rows, page_keys, page_values, read_map)
-    reads = {s: exchange(x, s) for s, x in zip(steps, routed[: replicas - 1])}
+        name="first",
+    )(me, holder_row, page_rows, page_keys, page_values, read_map)
+    pages = {s: exchange(x, s) for s, x in zip(far, first)}
+    reads = {s: exchange(x, s) for s, x in zip(steps, first[len(far) :])}
+    waited = []
+    second = pl.pallas_call(
+        functools.partial(second_kernel, replicas, slots, count, most, page_len, near, len(waited)),
+        out_shape=[page_shape] * len(near) + [shape((at_me + 1,), jnp.int32)],
+        in_specs=[SMEM] * 4 + [ANY] * (2 + len(waited)),
+        out_specs=[ANY] * len(near) + [SMEM],
+        scratch_shapes=[
+            pltpu.VMEM(page_keys.shape, bf16),
+            pltpu.VMEM(page_values.shape, bf16),
+            pltpu.VMEM((len(near), *page_shape.shape), bf16),
+            pltpu.SMEM((replicas,), jnp.int32),
+            pltpu.SemaphoreType.DMA((2,)),
+            pltpu.SemaphoreType.DMA((len(near),)),
+        ],
+        compiler_params=WIDE,
+        name="second",
+    )(me, holder_row, cache_slot, page_rows, page_keys, page_values, *waited)
+    pages.update({s: exchange(x, s) for s, x in zip(near, second[:-1])})
     reads[0] = read_map
-    pages = {s: exchange(x, s) for s, x in zip(steps, routed[replicas - 1 : -1])}
-    plan = routed[-1]
+    plan = second[-1]
 
     states = cache_states.reshape(cache_states.shape[0], channels, STATE)
     carried = {}

time: 81.1 us -> 80.2 us (0.989)
  waiting for transfers between devices: 28 us -> 24.9 us
  Pallas kernels: 32.9 us -> 35.6 us
    ppermute x9, waiting for transfers between devices: 28 us -> 24.9 us  [exchange(): return lax.ppermute(x, 'replica', [(i, i ^ step) for i in range(replicas)])]
    pallas_call x1 -> x2, Pallas kernels: 3.85 us -> 6.64 us  [the longest x1 3.8 us: per_device(): pl.pallas_call(functools.partial(second_kernel, replicas, slots, count, m...]
    unnamed x40 -> x42, local copies, waits for them, and re-layouts: 3.39 us -> 3.38 us
  transfers between devices with their start and end apart: 9 -> 9, of which waited for: 2 -> 2; matrix products, arithmetic and copies ran while one was open for 1% -> 0% of each run, Pallas kernels for 33% -> 38%
where the time goes in v4:
time: 80.2 us; the launch traced here: 79.8 us
  Pallas kernels  35.6 us (44%)
  waiting for transfers between devices  24.9 us (31%)
  starting transfers between devices  14.7 us (18%)
  local copies, waits for them, and re-layouts  3.54 us (4%)
  between operations  0.96 us (1%)
    ppermute x9, waiting for transfers between devices, exchange(): return lax.ppermute(x, 'replica', [(i, i ^ step) for i in range(replicas)])  24.9 us
    ppermute x9, starting transfers between devices, exchange(): return lax.ppermute(x, 'replica', [(i, i ^ step) for i in range(replicas)])  14.7 us
    pallas_call x1, Pallas kernels, per_device(): pl.pallas_call(functools.partial(attention_kernel, replicas, kv_here, per...  10.8 us
    pallas_call x1, Pallas kernels, per_device(): pl.pallas_call(within_kernel, out_shape=[shape((count, positions, channel...  7.49 us
    pallas_call x1, Pallas kernels, per_device(): pl.pallas_call(functools.partial(carried_kernel, replicas, slots, count,...  6.31 us
    pallas_call x2, Pallas kernels, per_device(): pl.pallas_call(functools.partial(finish_kernel, replicas, slots, members,...  4.3 us
    pallas_call x1, Pallas kernels, per_device(): pl.pallas_call(functools.partial(second_kernel, replicas, slots, count, m...  3.8 us
    unnamed x42, local copies, waits for them, and re-layouts  3.38 us
  transfers between devices with their start and end apart: 9, of which 2 were waited for; matrix products, arithmetic and copies ran while one was open for 0% of the time, Pallas kernels for 38%

profile of v4, /device:TPU:0, one launch (start us, length us, event | category | flops | bytes accessed | tf_op | source)
XLA Modules:
  0.0 79.8 jit_solution(3195552186440124628)
XLA Ops:
  0.6 0.0 copy-start.17
  0.6 2.8 %first.1 = (bf16[3,2,128,256]{3,2,1,0:T(8,128)(2,1)}, bf16[3,32,128]{2,1,0:T(8,128)(2,1)}, bf16[3,32,128]{2,1,0:T(8,128)(2,1)}, bf16[3,32,128]{2,1,0:T(8,128)(2,1)}) custom-call(s32[1]{0:T(128)} %bitcast.me_ref, s32[1,44]{1,0:T(1,128)} %bitcast.12, s32[8,44]{1,0:T(8,128)} %bitcast.6, bf16[48,16,256]{2,1,0:T(8,128)(2,1)} %rest_3_.3, ...), custom_call_target="tpu_custom_call" | custom-call | tf_op jit(solution)/shard_map/first/pallas_call | solution.py:467
  3.5 5.1 %collective-permute-start = (bf16[3,32,128]{2,1,0:T(8,128)(2,1)}, bf16[3,32,128]{2,1,0:T(8,128)(2,1)S(1)}, u32[]{:S(2)}, u32[]{:S(2)}) collective-permute-start(bf16[3,32,128]{2,1,0:T(8,128)(2,1)} %get-tuple-element.18), channel_id=1, source_target_pairs={{0,12},{4,8},{8,4},{12,0},{1,13},{5,9},{9,5},{13,1},{2,14},{6,10},... | collective-permute-start | bytes 73736 | tf_op jit(solution)/shard_map/ppermute | solution.py:461
  8.6 0.0 collective-permute-start.1
  8.7 0.6 collective-permute-start.2
  9.3 3.7 %collective-permute-start.6 = (bf16[3,2,128,256]{3,2,1,0:T(8,128)(2,1)}, bf16[3,2,128,256]{3,2,1,0:T(8,128)(2,1)S(1)}, u32[]{:S(2)}, u32[]{:S(2)}) collective-permute-start(bf16[3,2,128,256]{3,2,1,0:T(8,128)(2,1)} %get-tuple-element.25), channel_id=1, source_target_pairs={{0,12},{4,8},{8,4},{12,0},{1,13},{5,9},{9,5},{13,1},{2,14},{6,10},... | collective-permute-start | bytes 1179656 | tf_op jit(solution)/shard_map/ppermute | solution.py:461
  13.0 3.8 %second.1 = (bf16[3,2,128,256]{3,2,1,0:T(8,128)(2,1)}, bf16[3,2,128,256]{3,2,1,0:T(8,128)(2,1)}, s32[50]{0:T(128)}) custom-call(s32[1]{0:T(128)} %bitcast.me_ref, s32[1,44]{1,0:T(1,128)} %bitcast.13, s32[44]{0:T(128)} %slot_ref.1, s32[8,44]{1,0:T(8,128)} %bitcast.7, bf16[48,16,256]{2,1,0:T(8,128)(2,1)} %rest_3_.3, bf16[48,16,256]{2,1,0:T(8,128)(2,1)} %rest_4_.1), custom_call_target="tpu_custom_call" | custom-call | tf_op jit(solution)/shard_map/second/pallas_call | solution.py:487
  16.8 0.1 collective-permute-start.7
  16.9 0.0 copy-done.17
  16.9 0.1 broadcast_in_dim.2
  17.0 0.1 reshape_reshape.3.skip_ref
  17.1 0.0 collective-permute-done.rest_0_
  17.1 0.0 copy-start.18
  17.1 0.7 collective-permute-start.8
  17.8 11.4 %collective-permute-done.1.rest_1_ = bf16[3,32,128]{2,1,0:T(8,128)(2,1)S(1)} collective-permute-done((bf16[3,32,128]{2,1,0:T(8,128)(2,1)}, bf16[3,32,128]{2,1,0:T(8,128)(2,1)S(1)}, u32[]{:S(2)}, u32[]{:S(2)}) %collective-permute-start.1) | collective-permute-done | bytes 24608 | tf_op jit(solution)/shard_map/ppermute | solution.py:461
  29.2 0.0 collective-permute-done.2.rest_2_
  29.2 0.6 copy-done.19
  29.8 0.0 copy-done.20
  29.8 0.0 copy-done.18
  29.9 6.3 %carried.1 = (bf16[3,32,2048]{2,1,0:T(8,128)(2,1)}, bf16[3,32,2048]{2,1,0:T(8,128)(2,1)}, bf16[3,32,2048]{2,1,0:T(8,128)(2,1)}, bf16[3,32,2048]{2,1,0:T(8,128)(2,1)}) custom-call(s32[50]{0:T(128)} %get-tuple-element.15.plan_ref, bf16[3,32,128]{2,1,0:T(8,128)(2,1)} %copy-done.18, bf16[3,32,128]{2,1,0:T(8,128)(2,1)} %copy-done.19, ...), custom_call_target="tpu_custom_call" | custom-call | flops 6442450944 | bytes 7864320 | tf_op jit(solution)/shard_map/carried/pallas_call | solution.py:512
  36.2 0.1 collective-permute-start.5
  36.2 0.1 collective-permute-start.3
  36.3 0.0 collective-permute-done.6.rest_0_
  36.3 4.3 %collective-permute-start.4 = (bf16[3,32,2048]{2,1,0:T(8,128)(2,1)}, bf16[3,32,2048]{2,1,0:T(8,128)(2,1)S(1)}, u32[]{:S(2)}, u32[]{:S(2)}) collective-permute-start(bf16[3,32,2048]{2,1,0:T(8,128)(2,1)} %get-tuple-element.22), channel_id=1, source_target_pairs={{0,12},{4,8},{8,4},{12,0},{1,13},{5,9},{9,5},{13,1},{2,14},{6,10},... | collective-permute-start | bytes 1179656 | tf_op jit(solution)/shard_map/ppermute | solution.py:461
  40.6 0.1 compare_convert_fusion.spread_ref
  40.7 0.0 copy-done.2
  40.8 0.0 copy-done.3
  40.8 0.0 copy-start.6
  40.8 0.9 %copy-done.6 = bf16[11,32,128]{2,1,0:T(8,128)(2,1)S(1)} copy-done((bf16[11,32,128]{2,1,0:T(8,128)(2,1)S(1)}, bf16[11,32,128]{2,1,0:T(8,128)(2,1)}, u32[]{:S(2)}) %copy-start.6) | copy-done | bytes 90136
  41.7 0.9 %copy-done.7 = f32[11,32,32]{2,1,0:T(8,128)S(1)} copy-done((f32[11,32,32]{2,1,0:T(8,128)S(1)}, f32[11,32,32]{2,1,0:T(8,128)}, u32[]{:S(2)}) %copy-start.7) | copy-done | bytes 45080
  42.6 0.9 %copy-done.10 = bf16[11,32,128]{2,1,0:T(8,128)(2,1)S(1)} copy-done((bf16[11,32,128]{2,1,0:T(8,128)(2,1)S(1)}, bf16[11,32,128]{2,1,0:T(8,128)(2,1)}, u32[]{:S(2)}) %copy-start.10) | copy-done | bytes 90136
  43.5 0.0 copy-start.9
  43.5 0.0 copy-start.11
  43.5 0.0 copy-start.13
  43.5 0.0 copy-start.16
  43.6 7.5 %within.1 = (f32[11,32,2048]{2,1,0:T(8,128)S(1)}, f32[11,32,2048]{2,1,0:T(8,128)S(1)}) custom-call(f32[1,32]{1,0:T(1,128)S(1)} %bitcast.11, f32[1,2048]{1,0:T(1,128)S(1)} %reshape_reshape.3.skip_ref, bf16[64,2048]{1,0:T(8,128)(2,1)S(1)} %compare_convert_fusion.spread_ref, f32[11,32,32]{2,1,0:T(8,128)S(1)} %copy-done.7, bf16[11,32,128]{2,1,0:T(8,128)(2,1)S(1)} %copy-done.6, ...), custom_call_target="tpu_custom_call" | custom-call | flops 369098752 | bytes 8650752 | tf_op jit(solution)/shard_map/within/pallas_call | solution.py:542
  51.1 0.0 copy-start.12
  51.1 13.4 %collective-permute-done.7.rest_1_ = bf16[3,2,128,256]{3,2,1,0:T(8,128)(2,1)S(1)} collective-permute-done((bf16[3,2,128,256]{3,2,1,0:T(8,128)(2,1)}, bf16[3,2,128,256]{3,2,1,0:T(8,128)(2,1)S(1)}, u32[]{:S(2)}, u32[]{:S(2)}) %collective-permute-start.7) | collective-permute-done | bytes 393248 | tf_op jit(solution)/shard_map/ppermute | solution.py:461
  64.5 0.0 collective-permute-done.8.rest_2_
  64.5 0.0 copy-done
  64.6 10.8 %attention.1 = bf16[11,32,2048]{2,1,0:T(8,128)(2,1)} custom-call(s32[50]{0:T(128)S(1)} %copy-done.14, s32[11]{0:T(128)S(1)} %copy-done.16, s32[11]{0:T(128)S(1)} %copy-done.13, s32[8,44]{1,0:T(8,128)S(1)} %bitcast.8, bf16[11,32,2048]{2,1,0:T(8,128)(2,1)S(1)} %copy-done.4, bf16[11,32,256]{2,1,0:T(8,128)(2,1)S(1)} %copy-done.8, ...), custom_call_target="tpu_custom_call" | custom-call | flops 461373440 | bytes 4325376 | tf_op jit(solution)/shard_map/attention/pallas_call | solution.py:576
  75.4 0.0 collective-permute-done.5.rest_1_
  75.4 0.0 copy-done.5
  75.4 0.0 copy-done.12
  75.4 2.1 %finish.2.rest_2_ = bf16[11,32,2048]{2,1,0:T(8,128)(2,1)} custom-call(s32[50]{0:T(128)S(1)} %copy-done.14, s32[11]{0:T(128)S(1)} %copy-done.13, f32[1,2048]{1,0:T(1,128)S(1)} %bitcast.9, f32[11,32,2048]{2,1,0:T(8,128)S(1)} %get-tuple-element.16.fixed_ref, f32[11,32,2048]{2,1,0:T(8,128)S(1)} %get-tuple-element.17.scaled_ref, ...), custom_call_target="tpu_custom_call" | custom-call | flops 3145728 | bytes 4718592 | tf_op jit(solution)/shard_map/finish/pallas_call | solution.py:617
  77.5 0.0 collective-permute-done.3.rest_0_
  77.5 0.0 collective-permute-done.4.rest_1_
  77.5 2.2 %finish.3 = bf16[11,32,2048]{2,1,0:T(8,128)(2,1)} custom-call(s32[50]{0:T(128)S(1)} %copy-done.14, s32[11]{0:T(128)S(1)} %copy-done.13, f32[1,2048]{1,0:T(1,128)S(1)} %bitcast.10, f32[11,32,2048]{2,1,0:T(8,128)S(1)} %get-tuple-element.16.fixed_ref, f32[11,32,2048]{2,1,0:T(8,128)S(1)} %get-tuple-element.17.scaled_ref, ...), custom_call_target="tpu_custom_call", output_to_operand_aliasing={{}: (7, {})} | custom-call | flops 3145728 | bytes 4718592 | tf_op jit(solution)/shard_map/finish/pallas_call | solution.py:617
  (24 shorter events, 0.0 us)
Async XLA Ops:
  0.6 16.3 %copy-start.17 = (f32[32]{0:T(128)S(1)}, f32[32]{0:T(128)}, u32[]{:S(2)}) copy-start(f32[32]{0:T(128)} %param.32) | copy-start | bytes 388
  3.5 13.6 %collective-permute-start = (bf16[3,32,128]{2,1,0:T(8,128)(2,1)}, bf16[3,32,128]{2,1,0:T(8,128)(2,1)S(1)}, u32[]{:S(2)}, u32[]{:S(2)}) collective-permute-start(bf16[3,32,128]{2,1,0:T(8,128)(2,1)} %get-tuple-element.18), channel_id=1, source_target_pairs={{0,12},{4,8},{8,4},{12,0},{1,13},{5,9},{9,5},{13,1},{2,14},{6,10},... | collective-permute-start | bytes 73736 | tf_op jit(solution)/shard_map/ppermute | solution.py:461
  8.6 20.6 %collective-permute-start.1 = (bf16[3,32,128]{2,1,0:T(8,128)(2,1)}, bf16[3,32,128]{2,1,0:T(8,128)(2,1)S(1)}, u32[]{:S(2)}, u32[]{:S(2)}) collective-permute-start(bf16[3,32,128]{2,1,0:T(8,128)(2,1)} %get-tuple-element.19), channel_id=1, source_target_pairs={{0,8},{4,12},{8,0},{12,4},{1,9},{5,13},{9,1},{13,5},{2,10},{6,14},... | collective-permute-start | bytes 73736 | tf_op jit(solution)/shard_map/ppermute | solution.py:461
  8.7 20.6 %collective-permute-start.2 = (bf16[3,32,128]{2,1,0:T(8,128)(2,1)}, bf16[3,32,128]{2,1,0:T(8,128)(2,1)S(1)}, u32[]{:S(2)}, u32[]{:S(2)}) collective-permute-start(bf16[3,32,128]{2,1,0:T(8,128)(2,1)} %get-tuple-element.20), channel_id=1, source_target_pairs={{0,4},{4,0},{8,12},{12,8},{1,5},{5,1},{9,13},{13,9},{2,6},{6,2},{1... | collective-permute-start | bytes 73736 | tf_op jit(solution)/shard_map/ppermute | solution.py:461
  9.3 27.0 %collective-permute-start.6 = (bf16[3,2,128,256]{3,2,1,0:T(8,128)(2,1)}, bf16[3,2,128,256]{3,2,1,0:T(8,128)(2,1)S(1)}, u32[]{:S(2)}, u32[]{:S(2)}) collective-permute-start(bf16[3,2,128,256]{3,2,1,0:T(8,128)(2,1)} %get-tuple-element.25), channel_id=1, source_target_pairs={{0,12},{4,8},{8,4},{12,0},{1,13},{5,9},{9,5},{13,1},{2,14},{6,10},... | collective-permute-start | bytes 1179656 | tf_op jit(solution)/shard_map/ppermute | solution.py:461
  16.8 47.6 %collective-permute-start.7 = (bf16[3,2,128,256]{3,2,1,0:T(8,128)(2,1)}, bf16[3,2,128,256]{3,2,1,0:T(8,128)(2,1)S(1)}, u32[]{:S(2)}, u32[]{:S(2)}) collective-permute-start(bf16[3,2,128,256]{3,2,1,0:T(8,128)(2,1)} %get-tuple-element.26), channel_id=1, source_target_pairs={{0,8},{4,12},{8,0},{12,4},{1,9},{5,13},{9,1},{13,5},{2,10},{6,14},... | collective-permute-start | bytes 1179656 | tf_op jit(solution)/shard_map/ppermute | solution.py:461
  17.1 12.7 %copy-start.18 = (bf16[3,32,128]{2,1,0:T(8,128)(2,1)}, bf16[3,32,128]{2,1,0:T(8,128)(2,1)S(1)}, u32[]{:S(2)}) copy-start(bf16[3,32,128]{2,1,0:T(8,128)(2,1)S(1)} %collective-permute-done.rest_0_) | copy-start | bytes 73732
  17.1 47.4 %collective-permute-start.8 = (bf16[3,2,128,256]{3,2,1,0:T(8,128)(2,1)}, bf16[3,2,128,256]{3,2,1,0:T(8,128)(2,1)S(1)}, u32[]{:S(2)}, u32[]{:S(2)}) collective-permute-start(bf16[3,2,128,256]{3,2,1,0:T(8,128)(2,1)} %get-tuple-element.27), channel_id=1, source_target_pairs={{0,4},{4,0},{8,12},{12,8},{1,5},{5,1},{9,13},{13,9},{2,6},{6,2},{1... | collective-permute-start | bytes 1179656 | tf_op jit(solution)/shard_map/ppermute | solution.py:461
  29.2 0.6 copy-start.19
  29.2 0.6 copy-start.20
  29.8 10.9 %copy-start.2 = (bf16[11,32,2048]{2,1,0:T(8,128)(2,1)S(1)}, bf16[11,32,2048]{2,1,0:T(8,128)(2,1)}, u32[]{:S(2)}) copy-start(bf16[11,32,2048]{2,1,0:T(8,128)(2,1)} %input_ref.1) | copy-start | bytes 4325380
  29.8 10.9 %copy-start.3 = (bf16[11,32,2048]{2,1,0:T(8,128)(2,1)S(1)}, bf16[11,32,2048]{2,1,0:T(8,128)(2,1)}, u32[]{:S(2)}) copy-start(bf16[11,32,2048]{2,1,0:T(8,128)(2,1)} %gate_ref.1) | copy-start | bytes 4325380
  29.9 10.9 %copy-start.15 = (f32[32]{0:T(128)S(1)}, f32[32]{0:T(128)}, u32[]{:S(2)}) copy-start(f32[32]{0:T(128)} %param.29) | copy-start | bytes 388
  36.2 39.2 %collective-permute-start.5 = (bf16[3,32,2048]{2,1,0:T(8,128)(2,1)}, bf16[3,32,2048]{2,1,0:T(8,128)(2,1)S(1)}, u32[]{:S(2)}, u32[]{:S(2)}) collective-permute-start(bf16[3,32,2048]{2,1,0:T(8,128)(2,1)} %get-tuple-element.24), channel_id=1, source_target_pairs={{0,4},{4,0},{8,12},{12,8},{1,5},{5,1},{9,13},{13,9},{2,6},{6,2},{1... | collective-permute-start | bytes 1179656 | tf_op jit(solution)/shard_map/ppermute | solution.py:461
  36.2 41.3 %collective-permute-start.3 = (bf16[3,32,2048]{2,1,0:T(8,128)(2,1)}, bf16[3,32,2048]{2,1,0:T(8,128)(2,1)S(1)}, u32[]{:S(2)}, u32[]{:S(2)}) collective-permute-start(bf16[3,32,2048]{2,1,0:T(8,128)(2,1)} %get-tuple-element.21), channel_id=1, source_target_pairs={{0,8},{4,12},{8,0},{12,4},{1,9},{5,13},{9,1},{13,5},{2,10},{6,14},... | collective-permute-start | bytes 1179656 | tf_op jit(solution)/shard_map/ppermute | solution.py:461
  36.3 41.2 %collective-permute-start.4 = (bf16[3,32,2048]{2,1,0:T(8,128)(2,1)}, bf16[3,32,2048]{2,1,0:T(8,128)(2,1)S(1)}, u32[]{:S(2)}, u32[]{:S(2)}) collective-permute-start(bf16[3,32,2048]{2,1,0:T(8,128)(2,1)} %get-tuple-element.22), channel_id=1, source_target_pairs={{0,12},{4,8},{8,4},{12,0},{1,13},{5,9},{9,5},{13,1},{2,14},{6,10},... | collective-permute-start | bytes 1179656 | tf_op jit(solution)/shard_map/ppermute | solution.py:461
  40.8 0.9 %copy-start.6 = (bf16[11,32,128]{2,1,0:T(8,128)(2,1)S(1)}, bf16[11,32,128]{2,1,0:T(8,128)(2,1)}, u32[]{:S(2)}) copy-start(bf16[11,32,128]{2,1,0:T(8,128)(2,1)} %rest_3_.2) | copy-start | bytes 270340
  41.7 0.9 %copy-start.7 = (f32[11,32,32]{2,1,0:T(8,128)S(1)}, f32[11,32,32]{2,1,0:T(8,128)}, u32[]{:S(2)}) copy-start(f32[11,32,32]{2,1,0:T(8,128)} %step_ref.1) | copy-start | bytes 135172
  42.6 0.9 %copy-start.10 = (bf16[11,32,128]{2,1,0:T(8,128)(2,1)S(1)}, bf16[11,32,128]{2,1,0:T(8,128)(2,1)}, u32[]{:S(2)}) copy-start(bf16[11,32,128]{2,1,0:T(8,128)(2,1)} %write_ref.1) | copy-start | bytes 270340
  43.5 21.0 %copy-start = (bf16[48,16,256]{2,1,0:T(8,128)(2,1)S(1)}, bf16[48,16,256]{2,1,0:T(8,128)(2,1)}, u32[]{:S(2)}) copy-start(bf16[48,16,256]{2,1,0:T(8,128)(2,1)} %rest_3_.3) | copy-start | bytes 1179652
  43.5 21.0 %copy-start.1 = (bf16[48,16,256]{2,1,0:T(8,128)(2,1)S(1)}, bf16[48,16,256]{2,1,0:T(8,128)(2,1)}, u32[]{:S(2)}) copy-start(bf16[48,16,256]{2,1,0:T(8,128)(2,1)} %rest_4_.1) | copy-start | bytes 1179652
  43.5 21.0 %copy-start.4 = (bf16[11,32,2048]{2,1,0:T(8,128)(2,1)S(1)}, bf16[11,32,2048]{2,1,0:T(8,128)(2,1)}, u32[]{:S(2)}) copy-start(bf16[11,32,2048]{2,1,0:T(8,128)(2,1)} %query_ref.1) | copy-start | bytes 4325380
  43.5 21.0 %copy-start.8 = (bf16[11,32,256]{2,1,0:T(8,128)(2,1)S(1)}, bf16[11,32,256]{2,1,0:T(8,128)(2,1)}, u32[]{:S(2)}) copy-start(bf16[11,32,256]{2,1,0:T(8,128)(2,1)} %key_ref.1) | copy-start | bytes 540676
  43.5 21.0 %copy-start.9 = (bf16[11,32,256]{2,1,0:T(8,128)(2,1)S(1)}, bf16[11,32,256]{2,1,0:T(8,128)(2,1)}, u32[]{:S(2)}) copy-start(bf16[11,32,256]{2,1,0:T(8,128)(2,1)} %value_ref.1) | copy-start | bytes 540676
  43.5 21.0 %copy-start.11 = (s32[44,8]{0,1:T(8,128)S(1)}, s32[44,8]{0,1:T(8,128)}, u32[]{:S(2)}) copy-start(s32[44,8]{0,1:T(8,128)} %param.22) | copy-start | bytes 4228
  43.5 21.0 %copy-start.13 = (s32[11]{0:T(128)S(1)}, s32[11]{0:T(128)}, u32[]{:S(2)}) copy-start(s32[11]{0:T(128)} %live_ref.5) | copy-start | bytes 136
  43.5 21.0 %copy-start.14 = (s32[50]{0:T(128)S(1)}, s32[50]{0:T(128)}, u32[]{:S(2)}) copy-start(s32[50]{0:T(128)} %get-tuple-element.15.plan_ref) | copy-start | bytes 604
  43.5 21.0 %copy-start.16 = (s32[11]{0:T(128)S(1)}, s32[11]{0:T(128)}, u32[]{:S(2)}) copy-start(s32[11]{0:T(128)} %count_ref.1) | copy-start | bytes 136
  51.1 24.4 %copy-start.5 = (bf16[3,32,2048]{2,1,0:T(8,128)(2,1)S(1)}, bf16[3,32,2048]{2,1,0:T(8,128)(2,1)}, u32[]{:S(2)}) copy-start(bf16[3,32,2048]{2,1,0:T(8,128)(2,1)} %get-tuple-element.23.rest_0_) | copy-start | bytes 1179652
  51.1 24.4 %copy-start.12 = (f32[2048]{0:T(1024)S(1)}, f32[2048]{0:T(1024)}, u32[]{:S(2)}) copy-start(f32[2048]{0:T(1024)} %param.34) | copy-start | bytes 24580

commit v5 on v4

--- a/solution.py
+++ b/solution.py
@@ -20,7 +20,7 @@
 
 
 def partner_steps(replicas):
-    return list(range(replicas - 1, 0, -1))
+    return [s ^ 1 if s > 1 else s for s in range(replicas - 1, 0, -1)]
 
 
 def places(replicas, slots, count):
@@ -300,7 +300,7 @@
     rows = per_kv * positions
     cached = most * page_len
     live = live_ref[i]
-    scale = 1.0 / math.sqrt(HEAD_DIM)
+    scale = math.log2(math.e) / math.sqrt(HEAD_DIM)
     column = lax.broadcasted_iota(jnp.int32, (rows, cached), 1)
     ahead = column < count_ref[i] * page_len
     row = lax.broadcasted_iota(jnp.int32, (rows, positions), 0) & (positions - 1)
@@ -313,12 +313,12 @@
         query = jnp.concatenate([query_ref[0, :, h : h + HEAD_DIM] for h in heads], axis=0)
         old_keys, old_values = buffer[now, 0, :, lanes], buffer[now, 1, :, lanes]
         new_keys, new_values = key_ref[0, :, lanes], value_ref[0, :, lanes]
-        old = lax.dot_general(query, old_keys, contract, preferred_element_type=jnp.float32) * scale
-        new = lax.dot_general(query, new_keys, contract, preferred_element_type=jnp.float32) * scale
+        old = lax.dot_general(query, old_keys, contract, preferred_element_type=jnp.float32)
+        new = lax.dot_general(query, new_keys, contract, preferred_element_type=jnp.float32)
         old = jnp.where(ahead, old, -1e30)
         new = jnp.where(causal, new, -1e30)
         top = jnp.maximum(jnp.max(old, axis=1, keepdims=True), jnp.max(new, axis=1, keepdims=True))
-        old, new = jnp.exp(old - top), jnp.exp(new - top)
+        old, new = jnp.exp2((old - top) * scale), jnp.exp2((new - top) * scale)
         share = 1.0 / (jnp.sum(old, axis=1, keepdims=True) + jnp.sum(new, axis=1, keepdims=True))
         old, new = (old * share).astype(jnp.bfloat16), (new * share).astype(jnp.bfloat16)
         result = jnp.dot(old, old_values, preferred_element_type=jnp.float32) + jnp.dot(

time: 80.2 us -> 80.2 us (level)
  the two profiles are of different devices: /device:TPU:0 before, /device:TPU:12 now
where the time goes in v5:
time: 80.2 us; the launch traced here: 79.9 us
  Pallas kernels  35.6 us (44%)
  waiting for transfers between devices  26.8 us (33%)
  starting transfers between devices  12.9 us (16%)
  local copies, waits for them, and re-layouts  3.53 us (4%)
  between operations  0.94 us (1%)
    ppermute x9, waiting for transfers between devices, exchange(): return lax.ppermute(x, 'replica', [(i, i ^ step) for i in range(replicas)])  26.8 us
    ppermute x9, starting transfers between devices, exchange(): return lax.ppermute(x, 'replica', [(i, i ^ step) for i in range(replicas)])  12.9 us
    pallas_call x1, Pallas kernels, per_device(): pl.pallas_call(functools.partial(attention_kernel, replicas, kv_here, per...  10.8 us
    pallas_call x1, Pallas kernels, per_device(): pl.pallas_call(within_kernel, out_shape=[shape((count, positions, channel...  7.5 us
    pallas_call x1, Pallas kernels, per_device(): pl.pallas_call(functools.partial(carried_kernel, replicas, slots, count,...  6.42 us
    pallas_call x2, Pallas kernels, per_device(): pl.pallas_call(functools.partial(finish_kernel, replicas, slots, members,...  4.29 us
    pallas_call x1, Pallas kernels, per_device(): pl.pallas_call(functools.partial(second_kernel, replicas, slots, count, m...  3.75 us
    unnamed x42, local copies, waits for them, and re-layouts  3.37 us
  transfers between devices with their start and end apart: 9, of which 3 were waited for; matrix products, arithmetic and copies ran while one was open for 0% of the time, Pallas kernels for 38%

profile of v5, /device:TPU:12, one launch (start us, length us, event | category | flops | bytes accessed | tf_op | source)
XLA Modules:
  0.0 79.9 jit_solution(10930399538925646612)
XLA Ops:
  0.6 0.0 copy-start.17
  0.6 2.9 %first.1 = (bf16[3,2,128,256]{3,2,1,0:T(8,128)(2,1)}, bf16[3,32,128]{2,1,0:T(8,128)(2,1)}, bf16[3,32,128]{2,1,0:T(8,128)(2,1)}, bf16[3,32,128]{2,1,0:T(8,128)(2,1)}) custom-call(s32[1]{0:T(128)} %bitcast.me_ref, s32[1,44]{1,0:T(1,128)} %bitcast.12, s32[8,44]{1,0:T(8,128)} %bitcast.6, bf16[48,16,256]{2,1,0:T(8,128)(2,1)} %rest_3_.3, ...), custom_call_target="tpu_custom_call" | custom-call | tf_op jit(solution)/shard_map/first/pallas_call | solution.py:467
  3.5 2.6 %collective-permute-start = (bf16[3,32,128]{2,1,0:T(8,128)(2,1)}, bf16[3,32,128]{2,1,0:T(8,128)(2,1)S(1)}, u32[]{:S(2)}, u32[]{:S(2)}) collective-permute-start(bf16[3,32,128]{2,1,0:T(8,128)(2,1)} %get-tuple-element.18), channel_id=1, source_target_pairs={{0,8},{4,12},{8,0},{12,4},{1,9},{5,13},{9,1},{13,5},{2,10},{6,14},... | collective-permute-start | bytes 73736 | tf_op jit(solution)/shard_map/ppermute | solution.py:461
  6.1 0.0 collective-permute-start.1
  6.1 1.8 %collective-permute-start.2 = (bf16[3,32,128]{2,1,0:T(8,128)(2,1)}, bf16[3,32,128]{2,1,0:T(8,128)(2,1)S(1)}, u32[]{:S(2)}, u32[]{:S(2)}) collective-permute-start(bf16[3,32,128]{2,1,0:T(8,128)(2,1)} %get-tuple-element.20), channel_id=1, source_target_pairs={{0,4},{4,0},{8,12},{12,8},{1,5},{5,1},{9,13},{13,9},{2,6},{6,2},{1... | collective-permute-start | bytes 73736 | tf_op jit(solution)/shard_map/ppermute | solution.py:461
  8.0 1.7 %collective-permute-start.6 = (bf16[3,2,128,256]{3,2,1,0:T(8,128)(2,1)}, bf16[3,2,128,256]{3,2,1,0:T(8,128)(2,1)S(1)}, u32[]{:S(2)}, u32[]{:S(2)}) collective-permute-start(bf16[3,2,128,256]{3,2,1,0:T(8,128)(2,1)} %get-tuple-element.25), channel_id=1, source_target_pairs={{0,8},{4,12},{8,0},{12,4},{1,9},{5,13},{9,1},{13,5},{2,10},{6,14},... | collective-permute-start | bytes 1179656 | tf_op jit(solution)/shard_map/ppermute | solution.py:461
  9.6 3.8 %second.1 = (bf16[3,2,128,256]{3,2,1,0:T(8,128)(2,1)}, bf16[3,2,128,256]{3,2,1,0:T(8,128)(2,1)}, s32[50]{0:T(128)}) custom-call(s32[1]{0:T(128)} %bitcast.me_ref, s32[1,44]{1,0:T(1,128)} %bitcast.13, s32[44]{0:T(128)} %slot_ref.1, s32[8,44]{1,0:T(8,128)} %bitcast.7, bf16[48,16,256]{2,1,0:T(8,128)(2,1)} %rest_3_.3, bf16[48,16,256]{2,1,0:T(8,128)(2,1)} %rest_4_.1), custom_call_target="tpu_custom_call" | custom-call | tf_op jit(solution)/shard_map/second/pallas_call | solution.py:487
  13.4 0.1 collective-permute-start.7
  13.5 0.1 broadcast_in_dim.2
  13.6 0.1 reshape_reshape.3.skip_ref
  13.6 0.0 collective-permute-done.rest_0_
  13.7 2.9 %collective-permute-start.8 = (bf16[3,2,128,256]{3,2,1,0:T(8,128)(2,1)}, bf16[3,2,128,256]{3,2,1,0:T(8,128)(2,1)S(1)}, u32[]{:S(2)}, u32[]{:S(2)}) collective-permute-start(bf16[3,2,128,256]{3,2,1,0:T(8,128)(2,1)} %get-tuple-element.27), channel_id=1, source_target_pairs={{0,4},{4,0},{8,12},{12,8},{1,5},{5,1},{9,13},{13,9},{2,6},{6,2},{1... | collective-permute-start | bytes 1179656 | tf_op jit(solution)/shard_map/ppermute | solution.py:461
  16.5 0.0 collective-permute-done.1.rest_1_
  16.5 0.0 collective-permute-done.2.rest_2_
  16.5 0.6 copy-done.19
  17.1 0.0 copy-done.20
  17.1 0.0 copy-done.18
  17.2 6.4 %carried.1 = (bf16[3,32,2048]{2,1,0:T(8,128)(2,1)}, bf16[3,32,2048]{2,1,0:T(8,128)(2,1)}, bf16[3,32,2048]{2,1,0:T(8,128)(2,1)}, bf16[3,32,2048]{2,1,0:T(8,128)(2,1)}) custom-call(s32[50]{0:T(128)} %get-tuple-element.15.plan_ref, bf16[3,32,128]{2,1,0:T(8,128)(2,1)} %copy-done.18, bf16[3,32,128]{2,1,0:T(8,128)(2,1)} %copy-done.19, ...), custom_call_target="tpu_custom_call" | custom-call | flops 6442450944 | bytes 7864320 | tf_op jit(solution)/shard_map/carried/pallas_call | solution.py:512
  23.6 0.2 collective-permute-start.5
  23.8 2.9 %collective-permute-start.3 = (bf16[3,32,2048]{2,1,0:T(8,128)(2,1)}, bf16[3,32,2048]{2,1,0:T(8,128)(2,1)S(1)}, u32[]{:S(2)}, u32[]{:S(2)}) collective-permute-start(bf16[3,32,2048]{2,1,0:T(8,128)(2,1)} %get-tuple-element.21), channel_id=1, source_target_pairs={{0,8},{4,12},{8,0},{12,4},{1,9},{5,13},{9,1},{13,5},{2,10},{6,14},... | collective-permute-start | bytes 1179656 | tf_op jit(solution)/shard_map/ppermute | solution.py:461
  26.7 8.6 %collective-permute-done.6.rest_0_ = bf16[3,2,128,256]{3,2,1,0:T(8,128)(2,1)S(1)} collective-permute-done((bf16[3,2,128,256]{3,2,1,0:T(8,128)(2,1)}, bf16[3,2,128,256]{3,2,1,0:T(8,128)(2,1)S(1)}, u32[]{:S(2)}, u32[]{:S(2)}) %collective-permute-start.6) | collective-permute-done | bytes 393248 | tf_op jit(solution)/shard_map/ppermute | solution.py:461
  35.3 0.7 collective-permute-start.4
  36.1 0.1 compare_convert_fusion.spread_ref
  36.2 0.0 copy-start.6
  36.2 0.9 %copy-done.6 = bf16[11,32,128]{2,1,0:T(8,128)(2,1)S(1)} copy-done((bf16[11,32,128]{2,1,0:T(8,128)(2,1)S(1)}, bf16[11,32,128]{2,1,0:T(8,128)(2,1)}, u32[]{:S(2)}) %copy-start.6) | copy-done | bytes 90136
  37.1 0.9 %copy-done.7 = f32[11,32,32]{2,1,0:T(8,128)S(1)} copy-done((f32[11,32,32]{2,1,0:T(8,128)S(1)}, f32[11,32,32]{2,1,0:T(8,128)}, u32[]{:S(2)}) %copy-start.7) | copy-done | bytes 45080
  38.0 0.9 %copy-done.10 = bf16[11,32,128]{2,1,0:T(8,128)(2,1)S(1)} copy-done((bf16[11,32,128]{2,1,0:T(8,128)(2,1)S(1)}, bf16[11,32,128]{2,1,0:T(8,128)(2,1)}, u32[]{:S(2)}) %copy-start.10) | copy-done | bytes 90136
  38.9 0.0 copy-start.9
  38.9 0.0 copy-start.11
  39.0 0.0 copy-start.13
  39.0 0.0 copy-start.16
  39.0 7.5 %within.1 = (f32[11,32,2048]{2,1,0:T(8,128)S(1)}, f32[11,32,2048]{2,1,0:T(8,128)S(1)}) custom-call(f32[1,32]{1,0:T(1,128)S(1)} %bitcast.11, f32[1,2048]{1,0:T(1,128)S(1)} %reshape_reshape.3.skip_ref, bf16[64,2048]{1,0:T(8,128)(2,1)S(1)} %compare_convert_fusion.spread_ref, f32[11,32,32]{2,1,0:T(8,128)S(1)} %copy-done.7, bf16[11,32,128]{2,1,0:T(8,128)(2,1)S(1)} %copy-done.6, ...), custom_call_target="tpu_custom_call" | custom-call | flops 369098752 | bytes 8650752 | tf_op jit(solution)/shard_map/within/pallas_call | solution.py:542
  46.5 0.0 copy-start.12
  46.5 0.0 collective-permute-done.7.rest_1_
  46.5 0.0 collective-permute-done.8.rest_2_
  46.5 0.0 copy-done
  46.5 0.0 copy-done.1
  46.6 0.0 copy-done.4
  46.6 0.0 copy-done.8
  46.6 0.0 copy-done.9
  46.6 0.0 copy-done.11
  46.6 0.0 copy-done.13
  46.6 10.8 %attention.1 = bf16[11,32,2048]{2,1,0:T(8,128)(2,1)} custom-call(s32[50]{0:T(128)S(1)} %copy-done.14, s32[11]{0:T(128)S(1)} %copy-done.16, s32[11]{0:T(128)S(1)} %copy-done.13, s32[8,44]{1,0:T(8,128)S(1)} %bitcast.8, bf16[11,32,2048]{2,1,0:T(8,128)(2,1)S(1)} %copy-done.4, bf16[11,32,256]{2,1,0:T(8,128)(2,1)S(1)} %copy-done.8, ...), custom_call_target="tpu_custom_call" | custom-call | flops 461373440 | bytes 4325376 | tf_op jit(solution)/shard_map/attention/pallas_call | solution.py:576
  57.4 0.0 collective-permute-done.5.rest_1_
  57.5 2.1 %finish.2.rest_2_ = bf16[11,32,2048]{2,1,0:T(8,128)(2,1)} custom-call(s32[50]{0:T(128)S(1)} %copy-done.14, s32[11]{0:T(128)S(1)} %copy-done.13, f32[1,2048]{1,0:T(1,128)S(1)} %bitcast.9, f32[11,32,2048]{2,1,0:T(8,128)S(1)} %get-tuple-element.16.fixed_ref, f32[11,32,2048]{2,1,0:T(8,128)S(1)} %get-tuple-element.17.scaled_ref, ...), custom_call_target="tpu_custom_call" | custom-call | flops 3145728 | bytes 4718592 | tf_op jit(solution)/shard_map/finish/pallas_call | solution.py:617
  59.5 9.5 %collective-permute-done.3.rest_0_ = bf16[3,32,2048]{2,1,0:T(8,128)(2,1)S(1)} collective-permute-done((bf16[3,32,2048]{2,1,0:T(8,128)(2,1)}, bf16[3,32,2048]{2,1,0:T(8,128)(2,1)S(1)}, u32[]{:S(2)}, u32[]{:S(2)}) %collective-permute-start.3) | collective-permute-done | bytes 393248 | tf_op jit(solution)/shard_map/ppermute | solution.py:461
  69.0 8.6 %collective-permute-done.4.rest_1_ = bf16[3,32,2048]{2,1,0:T(8,128)(2,1)S(1)} collective-permute-done((bf16[3,32,2048]{2,1,0:T(8,128)(2,1)}, bf16[3,32,2048]{2,1,0:T(8,128)(2,1)S(1)}, u32[]{:S(2)}, u32[]{:S(2)}) %collective-permute-start.4) | collective-permute-done | bytes 393248 | tf_op jit(solution)/shard_map/ppermute | solution.py:461
  77.7 2.2 %finish.3 = bf16[11,32,2048]{2,1,0:T(8,128)(2,1)} custom-call(s32[50]{0:T(128)S(1)} %copy-done.14, s32[11]{0:T(128)S(1)} %copy-done.13, f32[1,2048]{1,0:T(1,128)S(1)} %bitcast.10, f32[11,32,2048]{2,1,0:T(8,128)S(1)} %get-tuple-element.16.fixed_ref, f32[11,32,2048]{2,1,0:T(8,128)S(1)} %get-tuple-element.17.scaled_ref, ...), custom_call_target="tpu_custom_call", output_to_operand_aliasing={{}: (7, {})} | custom-call | flops 3145728 | bytes 4718592 | tf_op jit(solution)/shard_map/finish/pallas_call | solution.py:617
  (24 shorter events, 0.0 us)
Async XLA Ops:
  0.6 12.9 %copy-start.17 = (f32[32]{0:T(128)S(1)}, f32[32]{0:T(128)}, u32[]{:S(2)}) copy-start(f32[32]{0:T(128)} %param.32) | copy-start | bytes 388
  3.5 10.1 %collective-permute-start = (bf16[3,32,128]{2,1,0:T(8,128)(2,1)}, bf16[3,32,128]{2,1,0:T(8,128)(2,1)S(1)}, u32[]{:S(2)}, u32[]{:S(2)}) collective-permute-start(bf16[3,32,128]{2,1,0:T(8,128)(2,1)} %get-tuple-element.18), channel_id=1, source_target_pairs={{0,8},{4,12},{8,0},{12,4},{1,9},{5,13},{9,1},{13,5},{2,10},{6,14},... | collective-permute-start | bytes 73736 | tf_op jit(solution)/shard_map/ppermute | solution.py:461
  6.1 10.4 %collective-permute-start.1 = (bf16[3,32,128]{2,1,0:T(8,128)(2,1)}, bf16[3,32,128]{2,1,0:T(8,128)(2,1)S(1)}, u32[]{:S(2)}, u32[]{:S(2)}) collective-permute-start(bf16[3,32,128]{2,1,0:T(8,128)(2,1)} %get-tuple-element.19), channel_id=1, source_target_pairs={{0,12},{4,8},{8,4},{12,0},{1,13},{5,9},{9,5},{13,1},{2,14},{6,10},... | collective-permute-start | bytes 73736 | tf_op jit(solution)/shard_map/ppermute | solution.py:461
  6.1 10.4 %collective-permute-start.2 = (bf16[3,32,128]{2,1,0:T(8,128)(2,1)}, bf16[3,32,128]{2,1,0:T(8,128)(2,1)S(1)}, u32[]{:S(2)}, u32[]{:S(2)}) collective-permute-start(bf16[3,32,128]{2,1,0:T(8,128)(2,1)} %get-tuple-element.20), channel_id=1, source_target_pairs={{0,4},{4,0},{8,12},{12,8},{1,5},{5,1},{9,13},{13,9},{2,6},{6,2},{1... | collective-permute-start | bytes 73736 | tf_op jit(solution)/shard_map/ppermute | solution.py:461
  8.0 27.4 %collective-permute-start.6 = (bf16[3,2,128,256]{3,2,1,0:T(8,128)(2,1)}, bf16[3,2,128,256]{3,2,1,0:T(8,128)(2,1)S(1)}, u32[]{:S(2)}, u32[]{:S(2)}) collective-permute-start(bf16[3,2,128,256]{3,2,1,0:T(8,128)(2,1)} %get-tuple-element.25), channel_id=1, source_target_pairs={{0,8},{4,12},{8,0},{12,4},{1,9},{5,13},{9,1},{13,5},{2,10},{6,14},... | collective-permute-start | bytes 1179656 | tf_op jit(solution)/shard_map/ppermute | solution.py:461
  13.4 33.1 %collective-permute-start.7 = (bf16[3,2,128,256]{3,2,1,0:T(8,128)(2,1)}, bf16[3,2,128,256]{3,2,1,0:T(8,128)(2,1)S(1)}, u32[]{:S(2)}, u32[]{:S(2)}) collective-permute-start(bf16[3,2,128,256]{3,2,1,0:T(8,128)(2,1)} %get-tuple-element.26), channel_id=1, source_target_pairs={{0,12},{4,8},{8,4},{12,0},{1,13},{5,9},{9,5},{13,1},{2,14},{6,10},... | collective-permute-start | bytes 1179656 | tf_op jit(solution)/shard_map/ppermute | solution.py:461
  13.7 3.5 %copy-start.18 = (bf16[3,32,128]{2,1,0:T(8,128)(2,1)}, bf16[3,32,128]{2,1,0:T(8,128)(2,1)S(1)}, u32[]{:S(2)}) copy-start(bf16[3,32,128]{2,1,0:T(8,128)(2,1)S(1)} %collective-permute-done.rest_0_) | copy-start | bytes 73732
  13.7 32.9 %collective-permute-start.8 = (bf16[3,2,128,256]{3,2,1,0:T(8,128)(2,1)}, bf16[3,2,128,256]{3,2,1,0:T(8,128)(2,1)S(1)}, u32[]{:S(2)}, u32[]{:S(2)}) collective-permute-start(bf16[3,2,128,256]{3,2,1,0:T(8,128)(2,1)} %get-tuple-element.27), channel_id=1, source_target_pairs={{0,4},{4,0},{8,12},{12,8},{1,5},{5,1},{9,13},{13,9},{2,6},{6,2},{1... | collective-permute-start | bytes 1179656 | tf_op jit(solution)/shard_map/ppermute | solution.py:461
  16.5 0.6 copy-start.19
  16.5 0.6 copy-start.20
  17.1 19.0 %copy-start.2 = (bf16[11,32,2048]{2,1,0:T(8,128)(2,1)S(1)}, bf16[11,32,2048]{2,1,0:T(8,128)(2,1)}, u32[]{:S(2)}) copy-start(bf16[11,32,2048]{2,1,0:T(8,128)(2,1)} %input_ref.1) | copy-start | bytes 4325380
  17.1 19.1 %copy-start.3 = (bf16[11,32,2048]{2,1,0:T(8,128)(2,1)S(1)}, bf16[11,32,2048]{2,1,0:T(8,128)(2,1)}, u32[]{:S(2)}) copy-start(bf16[11,32,2048]{2,1,0:T(8,128)(2,1)} %gate_ref.1) | copy-start | bytes 4325380
  17.1 19.1 %copy-start.15 = (f32[32]{0:T(128)S(1)}, f32[32]{0:T(128)}, u32[]{:S(2)}) copy-start(f32[32]{0:T(128)} %param.29) | copy-start | bytes 388
  23.6 33.8 %collective-permute-start.5 = (bf16[3,32,2048]{2,1,0:T(8,128)(2,1)}, bf16[3,32,2048]{2,1,0:T(8,128)(2,1)S(1)}, u32[]{:S(2)}, u32[]{:S(2)}) collective-permute-start(bf16[3,32,2048]{2,1,0:T(8,128)(2,1)} %get-tuple-element.24), channel_id=1, source_target_pairs={{0,4},{4,0},{8,12},{12,8},{1,5},{5,1},{9,13},{13,9},{2,6},{6,2},{1... | collective-permute-start | bytes 1179656 | tf_op jit(solution)/shard_map/ppermute | solution.py:461
  23.8 45.3 %collective-permute-start.3 = (bf16[3,32,2048]{2,1,0:T(8,128)(2,1)}, bf16[3,32,2048]{2,1,0:T(8,128)(2,1)S(1)}, u32[]{:S(2)}, u32[]{:S(2)}) collective-permute-start(bf16[3,32,2048]{2,1,0:T(8,128)(2,1)} %get-tuple-element.21), channel_id=1, source_target_pairs={{0,8},{4,12},{8,0},{12,4},{1,9},{5,13},{9,1},{13,5},{2,10},{6,14},... | collective-permute-start | bytes 1179656 | tf_op jit(solution)/shard_map/ppermute | solution.py:461
  35.3 42.3 %collective-permute-start.4 = (bf16[3,32,2048]{2,1,0:T(8,128)(2,1)}, bf16[3,32,2048]{2,1,0:T(8,128)(2,1)S(1)}, u32[]{:S(2)}, u32[]{:S(2)}) collective-permute-start(bf16[3,32,2048]{2,1,0:T(8,128)(2,1)} %get-tuple-element.22), channel_id=1, source_target_pairs={{0,12},{4,8},{8,4},{12,0},{1,13},{5,9},{9,5},{13,1},{2,14},{6,10},... | collective-permute-start | bytes 1179656 | tf_op jit(solution)/shard_map/ppermute | solution.py:461
  36.2 0.9 %copy-start.6 = (bf16[11,32,128]{2,1,0:T(8,128)(2,1)S(1)}, bf16[11,32,128]{2,1,0:T(8,128)(2,1)}, u32[]{:S(2)}) copy-start(bf16[11,32,128]{2,1,0:T(8,128)(2,1)} %rest_3_.2) | copy-start | bytes 270340
  37.1 0.9 %copy-start.7 = (f32[11,32,32]{2,1,0:T(8,128)S(1)}, f32[11,32,32]{2,1,0:T(8,128)}, u32[]{:S(2)}) copy-start(f32[11,32,32]{2,1,0:T(8,128)} %step_ref.1) | copy-start | bytes 135172
  38.0 0.9 %copy-start.10 = (bf16[11,32,128]{2,1,0:T(8,128)(2,1)S(1)}, bf16[11,32,128]{2,1,0:T(8,128)(2,1)}, u32[]{:S(2)}) copy-start(bf16[11,32,128]{2,1,0:T(8,128)(2,1)} %write_ref.1) | copy-start | bytes 270340
  38.9 7.6 %copy-start = (bf16[48,16,256]{2,1,0:T(8,128)(2,1)S(1)}, bf16[48,16,256]{2,1,0:T(8,128)(2,1)}, u32[]{:S(2)}) copy-start(bf16[48,16,256]{2,1,0:T(8,128)(2,1)} %rest_3_.3) | copy-start | bytes 1179652
  38.9 7.6 %copy-start.1 = (bf16[48,16,256]{2,1,0:T(8,128)(2,1)S(1)}, bf16[48,16,256]{2,1,0:T(8,128)(2,1)}, u32[]{:S(2)}) copy-start(bf16[48,16,256]{2,1,0:T(8,128)(2,1)} %rest_4_.1) | copy-start | bytes 1179652
  38.9 7.6 %copy-start.4 = (bf16[11,32,2048]{2,1,0:T(8,128)(2,1)S(1)}, bf16[11,32,2048]{2,1,0:T(8,128)(2,1)}, u32[]{:S(2)}) copy-start(bf16[11,32,2048]{2,1,0:T(8,128)(2,1)} %query_ref.1) | copy-start | bytes 4325380
  38.9 7.6 %copy-start.8 = (bf16[11,32,256]{2,1,0:T(8,128)(2,1)S(1)}, bf16[11,32,256]{2,1,0:T(8,128)(2,1)}, u32[]{:S(2)}) copy-start(bf16[11,32,256]{2,1,0:T(8,128)(2,1)} %key_ref.1) | copy-start | bytes 540676
  38.9 7.6 %copy-start.9 = (bf16[11,32,256]{2,1,0:T(8,128)(2,1)S(1)}, bf16[11,32,256]{2,1,0:T(8,128)(2,1)}, u32[]{:S(2)}) copy-start(bf16[11,32,256]{2,1,0:T(8,128)(2,1)} %value_ref.1) | copy-start | bytes 540676
  38.9 7.6 %copy-start.11 = (s32[44,8]{0,1:T(8,128)S(1)}, s32[44,8]{0,1:T(8,128)}, u32[]{:S(2)}) copy-start(s32[44,8]{0,1:T(8,128)} %param.22) | copy-start | bytes 4228
  39.0 7.6 %copy-start.13 = (s32[11]{0:T(128)S(1)}, s32[11]{0:T(128)}, u32[]{:S(2)}) copy-start(s32[11]{0:T(128)} %live_ref.5) | copy-start | bytes 136
  39.0 7.6 %copy-start.14 = (s32[50]{0:T(128)S(1)}, s32[50]{0:T(128)}, u32[]{:S(2)}) copy-start(s32[50]{0:T(128)} %get-tuple-element.15.plan_ref) | copy-start | bytes 604
  39.0 7.6 %copy-start.16 = (s32[11]{0:T(128)S(1)}, s32[11]{0:T(128)}, u32[]{:S(2)}) copy-start(s32[11]{0:T(128)} %count_ref.1) | copy-start | bytes 136
  46.5 10.9 %copy-start.5 = (bf16[3,32,2048]{2,1,0:T(8,128)(2,1)S(1)}, bf16[3,32,2048]{2,1,0:T(8,128)(2,1)}, u32[]{:S(2)}) copy-start(bf16[3,32,2048]{2,1,0:T(8,128)(2,1)} %get-tuple-element.23.rest_0_) | copy-start | bytes 1179652
  46.5 10.9 %copy-start.12 = (f32[2048]{0:T(1024)S(1)}, f32[2048]{0:T(1024)}, u32[]{:S(2)}) copy-start(f32[2048]{0:T(1024)} %param.34) | copy-start | bytes 24580

commit v6 on v5

--- a/solution.py
+++ b/solution.py
@@ -20,7 +20,7 @@
 
 
 def partner_steps(replicas):
-    return [s ^ 1 if s > 1 else s for s in range(replicas - 1, 0, -1)]
+    return list(range(replicas - 1, 0, -1))
 
 
 def places(replicas, slots, count):

time: 80.2 us -> 80.3 us (level)
  the two profiles are of different devices: /device:TPU:12 before, /device:TPU:0 now
where the time goes in v6:
time: 80.3 us; the launch traced here: 79.7 us
  Pallas kernels  35.4 us (44%)
  waiting for transfers between devices  24.9 us (31%)
  starting transfers between devices  14.7 us (18%)
  local copies, waits for them, and re-layouts  3.54 us (4%)
  between operations  0.96 us (1%)
    ppermute x9, waiting for transfers between devices, exchange(): return lax.ppermute(x, 'replica', [(i, i ^ step) for i in range(replicas)])  24.9 us
    ppermute x9, starting transfers between devices, exchange(): return lax.ppermute(x, 'replica', [(i, i ^ step) for i in range(replicas)])  14.7 us
    pallas_call x1, Pallas kernels, per_device(): pl.pallas_call(functools.partial(attention_kernel, replicas, kv_here, per...  10.8 us
    pallas_call x1, Pallas kernels, per_device(): pl.pallas_call(within_kernel, out_shape=[shape((count, positions, channel...  7.49 us
    pallas_call x1, Pallas kernels, per_device(): pl.pallas_call(functools.partial(carried_kernel, replicas, slots, count,...  6.18 us
    pallas_call x2, Pallas kernels, per_device(): pl.pallas_call(functools.partial(finish_kernel, replicas, slots, members,...  4.3 us
    pallas_call x1, Pallas kernels, per_device(): pl.pallas_call(functools.partial(second_kernel, replicas, slots, count, m...  3.81 us
    unnamed x42, local copies, waits for them, and re-layouts  3.38 us
  transfers between devices with their start and end apart: 9, of which 2 were waited for; matrix products, arithmetic and copies ran while one was open for 0% of the time, Pallas kernels for 38%

profile of v6, /device:TPU:0, one launch (start us, length us, event | category | flops | bytes accessed | tf_op | source)
XLA Modules:
  0.0 79.7 jit_solution(7173176153699588672)
XLA Ops:
  0.6 2.8 %first.1 = (bf16[3,2,128,256]{3,2,1,0:T(8,128)(2,1)}, bf16[3,32,128]{2,1,0:T(8,128)(2,1)}, bf16[3,32,128]{2,1,0:T(8,128)(2,1)}, bf16[3,32,128]{2,1,0:T(8,128)(2,1)}) custom-call(s32[1]{0:T(128)} %bitcast.me_ref, s32[1,44]{1,0:T(1,128)} %bitcast.12, s32[8,44]{1,0:T(8,128)} %bitcast.6, bf16[48,16,256]{2,1,0:T(8,128)(2,1)} %rest_3_.3, ...), custom_call_target="tpu_custom_call" | custom-call | tf_op jit(solution)/shard_map/first/pallas_call | solution.py:467
  3.4 5.2 %collective-permute-start = (bf16[3,32,128]{2,1,0:T(8,128)(2,1)}, bf16[3,32,128]{2,1,0:T(8,128)(2,1)S(1)}, u32[]{:S(2)}, u32[]{:S(2)}) collective-permute-start(bf16[3,32,128]{2,1,0:T(8,128)(2,1)} %get-tuple-element.18), channel_id=1, source_target_pairs={{0,12},{4,8},{8,4},{12,0},{1,13},{5,9},{9,5},{13,1},{2,14},{6,10},... | collective-permute-start | bytes 73736 | tf_op jit(solution)/shard_map/ppermute | solution.py:461
  8.6 0.0 collective-permute-start.1
  8.6 0.6 collective-permute-start.2
  9.3 3.7 %collective-permute-start.6 = (bf16[3,2,128,256]{3,2,1,0:T(8,128)(2,1)}, bf16[3,2,128,256]{3,2,1,0:T(8,128)(2,1)S(1)}, u32[]{:S(2)}, u32[]{:S(2)}) collective-permute-start(bf16[3,2,128,256]{3,2,1,0:T(8,128)(2,1)} %get-tuple-element.25), channel_id=1, source_target_pairs={{0,12},{4,8},{8,4},{12,0},{1,13},{5,9},{9,5},{13,1},{2,14},{6,10},... | collective-permute-start | bytes 1179656 | tf_op jit(solution)/shard_map/ppermute | solution.py:461
  13.0 3.8 %second.1 = (bf16[3,2,128,256]{3,2,1,0:T(8,128)(2,1)}, bf16[3,2,128,256]{3,2,1,0:T(8,128)(2,1)}, s32[50]{0:T(128)}) custom-call(s32[1]{0:T(128)} %bitcast.me_ref, s32[1,44]{1,0:T(1,128)} %bitcast.13, s32[44]{0:T(128)} %slot_ref.1, s32[8,44]{1,0:T(8,128)} %bitcast.7, bf16[48,16,256]{2,1,0:T(8,128)(2,1)} %rest_3_.3, bf16[48,16,256]{2,1,0:T(8,128)(2,1)} %rest_4_.1), custom_call_target="tpu_custom_call" | custom-call | tf_op jit(solution)/shard_map/second/pallas_call | solution.py:487
  16.8 0.1 collective-permute-start.7
  16.9 0.1 broadcast_in_dim.2
  17.0 0.1 reshape_reshape.3.skip_ref
  17.1 0.0 collective-permute-done.rest_0_
  17.1 0.7 collective-permute-start.8
  17.8 11.4 %collective-permute-done.1.rest_1_ = bf16[3,32,128]{2,1,0:T(8,128)(2,1)S(1)} collective-permute-done((bf16[3,32,128]{2,1,0:T(8,128)(2,1)}, bf16[3,32,128]{2,1,0:T(8,128)(2,1)S(1)}, u32[]{:S(2)}, u32[]{:S(2)}) %collective-permute-start.1) | collective-permute-done | bytes 24608 | tf_op jit(solution)/shard_map/ppermute | solution.py:461
  29.2 0.0 collective-permute-done.2.rest_2_
  29.2 0.6 copy-done.19
  29.8 0.0 copy-done.20
  29.8 0.0 copy-done.18
  29.8 6.2 %carried.1 = (bf16[3,32,2048]{2,1,0:T(8,128)(2,1)}, bf16[3,32,2048]{2,1,0:T(8,128)(2,1)}, bf16[3,32,2048]{2,1,0:T(8,128)(2,1)}, bf16[3,32,2048]{2,1,0:T(8,128)(2,1)}) custom-call(s32[50]{0:T(128)} %get-tuple-element.15.plan_ref, bf16[3,32,128]{2,1,0:T(8,128)(2,1)} %copy-done.18, bf16[3,32,128]{2,1,0:T(8,128)(2,1)} %copy-done.19, ...), custom_call_target="tpu_custom_call" | custom-call | flops 6442450944 | bytes 7864320 | tf_op jit(solution)/shard_map/carried/pallas_call | solution.py:512
  36.0 0.1 collective-permute-start.5
  36.1 0.1 collective-permute-start.3
  36.2 0.0 collective-permute-done.6.rest_0_
  36.2 4.3 %collective-permute-start.4 = (bf16[3,32,2048]{2,1,0:T(8,128)(2,1)}, bf16[3,32,2048]{2,1,0:T(8,128)(2,1)S(1)}, u32[]{:S(2)}, u32[]{:S(2)}) collective-permute-start(bf16[3,32,2048]{2,1,0:T(8,128)(2,1)} %get-tuple-element.22), channel_id=1, source_target_pairs={{0,12},{4,8},{8,4},{12,0},{1,13},{5,9},{9,5},{13,1},{2,14},{6,10},... | collective-permute-start | bytes 1179656 | tf_op jit(solution)/shard_map/ppermute | solution.py:461
  40.5 0.1 compare_convert_fusion.spread_ref
  40.6 0.0 copy-start.6
  40.6 0.9 %copy-done.6 = bf16[11,32,128]{2,1,0:T(8,128)(2,1)S(1)} copy-done((bf16[11,32,128]{2,1,0:T(8,128)(2,1)S(1)}, bf16[11,32,128]{2,1,0:T(8,128)(2,1)}, u32[]{:S(2)}) %copy-start.6) | copy-done | bytes 90136
  41.5 0.9 %copy-done.7 = f32[11,32,32]{2,1,0:T(8,128)S(1)} copy-done((f32[11,32,32]{2,1,0:T(8,128)S(1)}, f32[11,32,32]{2,1,0:T(8,128)}, u32[]{:S(2)}) %copy-start.7) | copy-done | bytes 45080
  42.4 0.9 %copy-done.10 = bf16[11,32,128]{2,1,0:T(8,128)(2,1)S(1)} copy-done((bf16[11,32,128]{2,1,0:T(8,128)(2,1)S(1)}, bf16[11,32,128]{2,1,0:T(8,128)(2,1)}, u32[]{:S(2)}) %copy-start.10) | copy-done | bytes 90136
  43.3 0.0 copy-start.9
  43.3 0.0 copy-start.11
  43.3 0.0 copy-start.13
  43.4 0.0 copy-start.14
  43.4 0.0 copy-start.16
  43.4 7.5 %within.1 = (f32[11,32,2048]{2,1,0:T(8,128)S(1)}, f32[11,32,2048]{2,1,0:T(8,128)S(1)}) custom-call(f32[1,32]{1,0:T(1,128)S(1)} %bitcast.11, f32[1,2048]{1,0:T(1,128)S(1)} %reshape_reshape.3.skip_ref, bf16[64,2048]{1,0:T(8,128)(2,1)S(1)} %compare_convert_fusion.spread_ref, f32[11,32,32]{2,1,0:T(8,128)S(1)} %copy-done.7, bf16[11,32,128]{2,1,0:T(8,128)(2,1)S(1)} %copy-done.6, ...), custom_call_target="tpu_custom_call" | custom-call | flops 369098752 | bytes 8650752 | tf_op jit(solution)/shard_map/within/pallas_call | solution.py:542
  50.9 0.0 copy-start.12
  50.9 13.5 %collective-permute-done.7.rest_1_ = bf16[3,2,128,256]{3,2,1,0:T(8,128)(2,1)S(1)} collective-permute-done((bf16[3,2,128,256]{3,2,1,0:T(8,128)(2,1)}, bf16[3,2,128,256]{3,2,1,0:T(8,128)(2,1)S(1)}, u32[]{:S(2)}, u32[]{:S(2)}) %collective-permute-start.7) | collective-permute-done | bytes 393248 | tf_op jit(solution)/shard_map/ppermute | solution.py:461
  64.4 0.0 collective-permute-done.8.rest_2_
  64.5 0.0 copy-done.4
  64.5 0.0 copy-done.8
  64.5 0.0 copy-done.9
  64.5 0.0 copy-done.11
  64.5 0.0 copy-done.13
  64.5 0.0 copy-done.14
  64.5 0.0 copy-done.16
  64.5 10.8 %attention.1 = bf16[11,32,2048]{2,1,0:T(8,128)(2,1)} custom-call(s32[50]{0:T(128)S(1)} %copy-done.14, s32[11]{0:T(128)S(1)} %copy-done.16, s32[11]{0:T(128)S(1)} %copy-done.13, s32[8,44]{1,0:T(8,128)S(1)} %bitcast.8, bf16[11,32,2048]{2,1,0:T(8,128)(2,1)S(1)} %copy-done.4, bf16[11,32,256]{2,1,0:T(8,128)(2,1)S(1)} %copy-done.8, ...), custom_call_target="tpu_custom_call" | custom-call | flops 461373440 | bytes 4325376 | tf_op jit(solution)/shard_map/attention/pallas_call | solution.py:576
  75.4 0.0 collective-permute-done.5.rest_1_
  75.4 2.1 %finish.2.rest_2_ = bf16[11,32,2048]{2,1,0:T(8,128)(2,1)} custom-call(s32[50]{0:T(128)S(1)} %copy-done.14, s32[11]{0:T(128)S(1)} %copy-done.13, f32[1,2048]{1,0:T(1,128)S(1)} %bitcast.9, f32[11,32,2048]{2,1,0:T(8,128)S(1)} %get-tuple-element.16.fixed_ref, f32[11,32,2048]{2,1,0:T(8,128)S(1)} %get-tuple-element.17.scaled_ref, ...), custom_call_target="tpu_custom_call" | custom-call | flops 3145728 | bytes 4718592 | tf_op jit(solution)/shard_map/finish/pallas_call | solution.py:617
  77.5 0.0 collective-permute-done.3.rest_0_
  77.5 0.0 collective-permute-done.4.rest_1_
  77.5 2.2 %finish.3 = bf16[11,32,2048]{2,1,0:T(8,128)(2,1)} custom-call(s32[50]{0:T(128)S(1)} %copy-done.14, s32[11]{0:T(128)S(1)} %copy-done.13, f32[1,2048]{1,0:T(1,128)S(1)} %bitcast.10, f32[11,32,2048]{2,1,0:T(8,128)S(1)} %get-tuple-element.16.fixed_ref, f32[11,32,2048]{2,1,0:T(8,128)S(1)} %get-tuple-element.17.scaled_ref, ...), custom_call_target="tpu_custom_call", output_to_operand_aliasing={{}: (7, {})} | custom-call | flops 3145728 | bytes 4718592 | tf_op jit(solution)/shard_map/finish/pallas_call | solution.py:617
  (24 shorter events, 0.0 us)
Async XLA Ops:
  0.6 16.3 %copy-start.17 = (f32[32]{0:T(128)S(1)}, f32[32]{0:T(128)}, u32[]{:S(2)}) copy-start(f32[32]{0:T(128)} %param.32) | copy-start | bytes 388
  3.4 13.6 %collective-permute-start = (bf16[3,32,128]{2,1,0:T(8,128)(2,1)}, bf16[3,32,128]{2,1,0:T(8,128)(2,1)S(1)}, u32[]{:S(2)}, u32[]{:S(2)}) collective-permute-start(bf16[3,32,128]{2,1,0:T(8,128)(2,1)} %get-tuple-element.18), channel_id=1, source_target_pairs={{0,12},{4,8},{8,4},{12,0},{1,13},{5,9},{9,5},{13,1},{2,14},{6,10},... | collective-permute-start | bytes 73736 | tf_op jit(solution)/shard_map/ppermute | solution.py:461
  8.6 20.6 %collective-permute-start.1 = (bf16[3,32,128]{2,1,0:T(8,128)(2,1)}, bf16[3,32,128]{2,1,0:T(8,128)(2,1)S(1)}, u32[]{:S(2)}, u32[]{:S(2)}) collective-permute-start(bf16[3,32,128]{2,1,0:T(8,128)(2,1)} %get-tuple-element.19), channel_id=1, source_target_pairs={{0,8},{4,12},{8,0},{12,4},{1,9},{5,13},{9,1},{13,5},{2,10},{6,14},... | collective-permute-start | bytes 73736 | tf_op jit(solution)/shard_map/ppermute | solution.py:461
  8.6 20.6 %collective-permute-start.2 = (bf16[3,32,128]{2,1,0:T(8,128)(2,1)}, bf16[3,32,128]{2,1,0:T(8,128)(2,1)S(1)}, u32[]{:S(2)}, u32[]{:S(2)}) collective-permute-start(bf16[3,32,128]{2,1,0:T(8,128)(2,1)} %get-tuple-element.20), channel_id=1, source_target_pairs={{0,4},{4,0},{8,12},{12,8},{1,5},{5,1},{9,13},{13,9},{2,6},{6,2},{1... | collective-permute-start | bytes 73736 | tf_op jit(solution)/shard_map/ppermute | solution.py:461
  9.3 26.9 %collective-permute-start.6 = (bf16[3,2,128,256]{3,2,1,0:T(8,128)(2,1)}, bf16[3,2,128,256]{3,2,1,0:T(8,128)(2,1)S(1)}, u32[]{:S(2)}, u32[]{:S(2)}) collective-permute-start(bf16[3,2,128,256]{3,2,1,0:T(8,128)(2,1)} %get-tuple-element.25), channel_id=1, source_target_pairs={{0,12},{4,8},{8,4},{12,0},{1,13},{5,9},{9,5},{13,1},{2,14},{6,10},... | collective-permute-start | bytes 1179656 | tf_op jit(solution)/shard_map/ppermute | solution.py:461
  16.8 47.6 %collective-permute-start.7 = (bf16[3,2,128,256]{3,2,1,0:T(8,128)(2,1)}, bf16[3,2,128,256]{3,2,1,0:T(8,128)(2,1)S(1)}, u32[]{:S(2)}, u32[]{:S(2)}) collective-permute-start(bf16[3,2,128,256]{3,2,1,0:T(8,128)(2,1)} %get-tuple-element.26), channel_id=1, source_target_pairs={{0,8},{4,12},{8,0},{12,4},{1,9},{5,13},{9,1},{13,5},{2,10},{6,14},... | collective-permute-start | bytes 1179656 | tf_op jit(solution)/shard_map/ppermute | solution.py:461
  17.1 12.7 %copy-start.18 = (bf16[3,32,128]{2,1,0:T(8,128)(2,1)}, bf16[3,32,128]{2,1,0:T(8,128)(2,1)S(1)}, u32[]{:S(2)}) copy-start(bf16[3,32,128]{2,1,0:T(8,128)(2,1)S(1)} %collective-permute-done.rest_0_) | copy-start | bytes 73732
  17.1 47.3 %collective-permute-start.8 = (bf16[3,2,128,256]{3,2,1,0:T(8,128)(2,1)}, bf16[3,2,128,256]{3,2,1,0:T(8,128)(2,1)S(1)}, u32[]{:S(2)}, u32[]{:S(2)}) collective-permute-start(bf16[3,2,128,256]{3,2,1,0:T(8,128)(2,1)} %get-tuple-element.27), channel_id=1, source_target_pairs={{0,4},{4,0},{8,12},{12,8},{1,5},{5,1},{9,13},{13,9},{2,6},{6,2},{1... | collective-permute-start | bytes 1179656 | tf_op jit(solution)/shard_map/ppermute | solution.py:461
  29.2 0.6 copy-start.19
  29.2 0.6 copy-start.20
  29.8 10.8 %copy-start.2 = (bf16[11,32,2048]{2,1,0:T(8,128)(2,1)S(1)}, bf16[11,32,2048]{2,1,0:T(8,128)(2,1)}, u32[]{:S(2)}) copy-start(bf16[11,32,2048]{2,1,0:T(8,128)(2,1)} %input_ref.1) | copy-start | bytes 4325380
  29.8 10.8 %copy-start.3 = (bf16[11,32,2048]{2,1,0:T(8,128)(2,1)S(1)}, bf16[11,32,2048]{2,1,0:T(8,128)(2,1)}, u32[]{:S(2)}) copy-start(bf16[11,32,2048]{2,1,0:T(8,128)(2,1)} %gate_ref.1) | copy-start | bytes 4325380
  29.8 10.8 %copy-start.15 = (f32[32]{0:T(128)S(1)}, f32[32]{0:T(128)}, u32[]{:S(2)}) copy-start(f32[32]{0:T(128)} %param.29) | copy-start | bytes 388
  36.0 39.4 %collective-permute-start.5 = (bf16[3,32,2048]{2,1,0:T(8,128)(2,1)}, bf16[3,32,2048]{2,1,0:T(8,128)(2,1)S(1)}, u32[]{:S(2)}, u32[]{:S(2)}) collective-permute-start(bf16[3,32,2048]{2,1,0:T(8,128)(2,1)} %get-tuple-element.24), channel_id=1, source_target_pairs={{0,4},{4,0},{8,12},{12,8},{1,5},{5,1},{9,13},{13,9},{2,6},{6,2},{1... | collective-permute-start | bytes 1179656 | tf_op jit(solution)/shard_map/ppermute | solution.py:461
  36.1 41.4 %collective-permute-start.3 = (bf16[3,32,2048]{2,1,0:T(8,128)(2,1)}, bf16[3,32,2048]{2,1,0:T(8,128)(2,1)S(1)}, u32[]{:S(2)}, u32[]{:S(2)}) collective-permute-start(bf16[3,32,2048]{2,1,0:T(8,128)(2,1)} %get-tuple-element.21), channel_id=1, source_target_pairs={{0,8},{4,12},{8,0},{12,4},{1,9},{5,13},{9,1},{13,5},{2,10},{6,14},... | collective-permute-start | bytes 1179656 | tf_op jit(solution)/shard_map/ppermute | solution.py:461
  36.2 41.3 %collective-permute-start.4 = (bf16[3,32,2048]{2,1,0:T(8,128)(2,1)}, bf16[3,32,2048]{2,1,0:T(8,128)(2,1)S(1)}, u32[]{:S(2)}, u32[]{:S(2)}) collective-permute-start(bf16[3,32,2048]{2,1,0:T(8,128)(2,1)} %get-tuple-element.22), channel_id=1, source_target_pairs={{0,12},{4,8},{8,4},{12,0},{1,13},{5,9},{9,5},{13,1},{2,14},{6,10},... | collective-permute-start | bytes 1179656 | tf_op jit(solution)/shard_map/ppermute | solution.py:461
  40.6 0.9 %copy-start.6 = (bf16[11,32,128]{2,1,0:T(8,128)(2,1)S(1)}, bf16[11,32,128]{2,1,0:T(8,128)(2,1)}, u32[]{:S(2)}) copy-start(bf16[11,32,128]{2,1,0:T(8,128)(2,1)} %rest_3_.2) | copy-start | bytes 270340
  41.5 0.9 %copy-start.7 = (f32[11,32,32]{2,1,0:T(8,128)S(1)}, f32[11,32,32]{2,1,0:T(8,128)}, u32[]{:S(2)}) copy-start(f32[11,32,32]{2,1,0:T(8,128)} %step_ref.1) | copy-start | bytes 135172
  42.4 0.9 %copy-start.10 = (bf16[11,32,128]{2,1,0:T(8,128)(2,1)S(1)}, bf16[11,32,128]{2,1,0:T(8,128)(2,1)}, u32[]{:S(2)}) copy-start(bf16[11,32,128]{2,1,0:T(8,128)(2,1)} %write_ref.1) | copy-start | bytes 270340
  43.3 21.1 %copy-start = (bf16[48,16,256]{2,1,0:T(8,128)(2,1)S(1)}, bf16[48,16,256]{2,1,0:T(8,128)(2,1)}, u32[]{:S(2)}) copy-start(bf16[48,16,256]{2,1,0:T(8,128)(2,1)} %rest_3_.3) | copy-start | bytes 1179652
  43.3 21.1 %copy-start.1 = (bf16[48,16,256]{2,1,0:T(8,128)(2,1)S(1)}, bf16[48,16,256]{2,1,0:T(8,128)(2,1)}, u32[]{:S(2)}) copy-start(bf16[48,16,256]{2,1,0:T(8,128)(2,1)} %rest_4_.1) | copy-start | bytes 1179652
  43.3 21.1 %copy-start.4 = (bf16[11,32,2048]{2,1,0:T(8,128)(2,1)S(1)}, bf16[11,32,2048]{2,1,0:T(8,128)(2,1)}, u32[]{:S(2)}) copy-start(bf16[11,32,2048]{2,1,0:T(8,128)(2,1)} %query_ref.1) | copy-start | bytes 4325380
  43.3 21.1 %copy-start.8 = (bf16[11,32,256]{2,1,0:T(8,128)(2,1)S(1)}, bf16[11,32,256]{2,1,0:T(8,128)(2,1)}, u32[]{:S(2)}) copy-start(bf16[11,32,256]{2,1,0:T(8,128)(2,1)} %key_ref.1) | copy-start | bytes 540676
  43.3 21.1 %copy-start.9 = (bf16[11,32,256]{2,1,0:T(8,128)(2,1)S(1)}, bf16[11,32,256]{2,1,0:T(8,128)(2,1)}, u32[]{:S(2)}) copy-start(bf16[11,32,256]{2,1,0:T(8,128)(2,1)} %value_ref.1) | copy-start | bytes 540676
  43.3 21.1 %copy-start.11 = (s32[44,8]{0,1:T(8,128)S(1)}, s32[44,8]{0,1:T(8,128)}, u32[]{:S(2)}) copy-start(s32[44,8]{0,1:T(8,128)} %param.22) | copy-start | bytes 4228
  43.3 21.1 %copy-start.13 = (s32[11]{0:T(128)S(1)}, s32[11]{0:T(128)}, u32[]{:S(2)}) copy-start(s32[11]{0:T(128)} %live_ref.5) | copy-start | bytes 136
  43.4 21.1 %copy-start.14 = (s32[50]{0:T(128)S(1)}, s32[50]{0:T(128)}, u32[]{:S(2)}) copy-start(s32[50]{0:T(128)} %get-tuple-element.15.plan_ref) | copy-start | bytes 604
  43.4 21.1 %copy-start.16 = (s32[11]{0:T(128)S(1)}, s32[11]{0:T(128)}, u32[]{:S(2)}) copy-start(s32[11]{0:T(128)} %count_ref.1) | copy-start | bytes 136
  50.9 24.5 %copy-start.5 = (bf16[3,32,2048]{2,1,0:T(8,128)(2,1)S(1)}, bf16[3,32,2048]{2,1,0:T(8,128)(2,1)}, u32[]{:S(2)}) copy-start(bf16[3,32,2048]{2,1,0:T(8,128)(2,1)} %get-tuple-element.23.rest_0_) | copy-start | bytes 1179652
  50.9 24.5 %copy-start.12 = (f32[2048]{0:T(1024)S(1)}, f32[2048]{0:T(1024)}, u32[]{:S(2)}) copy-start(f32[2048]{0:T(1024)} %param.34) | copy-start | bytes 24580
